TPU v7x, 32 devices: a whole 2x2x4 slice. The times are simulated.
32 devices in a mesh: lat: 4 (over y, x), lon: 8 (over z, core).
Axes of the slice: x: 2, y: 2, z: 4, core: 2. Of those that a mesh axis runs over, the one named last changes fastest.
Arguments:
- field: float32 [32, 1024, 1024], P(None, 'lat', 'lon'), may hold values from -300 to 300
- lon_rate: float32 [1024], replicated, may hold values from 0.06 to 0.15
- lat_rate: float32 [1024], replicated, may hold values from 0.06 to 0.15
Outputs:
- basis_field: bfloat16 [32, 1024, 1024], P(None, 'lat', 'lon')
- factor: float32 [32, 32], replicated
All inputs are finite; a program needn't handle non-finite values.
Results may differ from a plain program's by a relative error of at most 0.001.
Values sent between devices are 32-bit elements; how exact they have to be, the bound alone decides.
No kernel may reach another device: no remote copies, remote signals or barrier semaphores. Data moves between devices by JAX's collectives and lax.ppermute only.
A program may use at most 64 MiB of HBM per device.

v0:
```python
import math

import jax
import jax.numpy as jnp
from jax import lax
from jax.sharding import PartitionSpec as P

stencil_weights = (-205.0 / 72.0, 8.0 / 5.0, -1.0 / 5.0, 8.0 / 315.0, -1.0 / 560.0)


def with_halo(block, sides, width, periodic):
    for axis, dim in sides:
        count = lax.axis_size(axis)
        forward = [(i, i + 1) for i in range(count - 1)]
        if periodic:
            forward.append((count - 1, 0))
        backward = [(target, source) for source, target in forward]
        low = lax.ppermute(
            lax.slice_in_dim(block, block.shape[dim] - width, None, axis=dim), axis, forward
        )
        high = lax.ppermute(lax.slice_in_dim(block, 0, width, axis=dim), axis, backward)
        block = jnp.concatenate([low, block, high], axis=dim)
    return block


def area_weight(first_row, row_count, total_rows):
    row_index = (jnp.arange(row_count) + first_row).astype(jnp.float32)
    latitude = (-90.0 + (row_index + 0.5) * (180.0 / total_rows)) * (math.pi / 180.0)
    return jnp.sqrt(jnp.cos(latitude))


def diffuse(center, zonal_pad, merid_pad, zonal_rate, merid_rate):
    row_count = center.shape[1]
    col_count = center.shape[2]
    zonal_part = stencil_weights[0] * center
    merid_part = stencil_weights[0] * center
    for offset in range(1, 5):
        zonal_part = zonal_part + stencil_weights[offset] * (
            zonal_pad[:, :, 4 + offset : 4 + offset + col_count]
            + zonal_pad[:, :, 4 - offset : 4 - offset + col_count]
        )
        merid_part = merid_part + stencil_weights[offset] * (
            merid_pad[:, 4 + offset : 4 + offset + row_count, :]
            + merid_pad[:, 4 - offset : 4 - offset + row_count, :]
        )
    return center + zonal_rate[None, :, None] * zonal_part + merid_rate[None, :, None] * merid_part


def one_pass(grid_field, zonal_rate, merid_rate):
    zonal_pad = with_halo(grid_field, (("lon", 2),), 4, True)
    merid_pad = with_halo(grid_field, (("lat", 1),), 4, False)
    return diffuse(grid_field, zonal_pad, merid_pad, zonal_rate, merid_rate)


def shards(field, lon_rate, lat_rate):
    snapshots, row_count, col_count = field.shape
    row_start = lax.axis_index("lat") * row_count
    total_rows = row_count * lax.axis_size("lat")
    total_cells = total_rows * col_count * lax.axis_size("lon")
    zonal_rate = lax.dynamic_slice_in_dim(lon_rate, row_start, row_count)
    merid_rate = lax.dynamic_slice_in_dim(lat_rate, row_start, row_count)
    smoothed = field
    for repeat in range(2):
        smoothed = one_pass(smoothed, zonal_rate, merid_rate)
    weighted = smoothed * area_weight(row_start, row_count, total_rows)[None, :, None]
    flat_field = weighted.reshape(snapshots, row_count * col_count)
    partial_gram = jnp.dot(
        flat_field,
        flat_field.T,
        precision=lax.Precision.HIGHEST,
        preferred_element_type=jnp.float32,
    )
    gram_matrix = lax.psum(partial_gram, ("lat", "lon"))
    lower_factor = jnp.linalg.cholesky(gram_matrix)
    inverse = jax.scipy.linalg.solve_triangular(
        lower_factor, jnp.eye(snapshots, dtype=jnp.float32), lower=True
    )
    root_count = math.sqrt(total_cells)
    basis_field = (
        jnp.dot(
            inverse, flat_field, precision=lax.Precision.HIGHEST, preferred_element_type=jnp.float32
        )
        * root_count
    )
    basis_field = basis_field.astype(jnp.bfloat16).reshape(snapshots, row_count, col_count)
    return (basis_field, lower_factor.T / root_count)


def solution(mesh):
    return jax.shard_map(
        shards,
        mesh=mesh,
        in_specs=(P(None, "lat", "lon"), P(), P()),
        out_specs=(P(None, "lat", "lon"), P()),
        check_vma=False,
    )
```

profile of v0, /device:TPU:0, one launch (start us, length us, event | category | flops | bytes accessed | tf_op | source)
XLA Modules:
  0.0 192.0 jit_solution(18362169146937607562)
XLA Ops:
  0.6 5.5 %copy.44 = f32[32,256,128]{1,0,2:T(8,128)} copy(f32[32,256,128]{2,1,0:T(8,128)} %param.3) | data formatting | bytes 8388608 | tf_op args[0]
  7.1 4.5 %collective-permute-start = (f32[32,256,4]{1,0,2:T(8,128)S(1)}, f32[32,256,4]{1,0,2:T(8,128)S(1)}, u32[]{:S(2)}, u32[]{:S(2)}) collective-permute-start(f32[32,256,4]{1,0,2:T(8,128)S(1)} %get-tuple-element.16), channel_id=1, source_target_pairs={{1,0},{2,1},{3,2},{4,3},{5,4},{6,5},{7,6},{0,7},{9,8},{10,9},{11,1... | collective-permute-start | bytes 393224 | tf_op jit(solution)/shard_map/ppermute | solution.py:21
  12.7 1.3 collective-permute-start.2
  14.0 4.5 %collective-permute-start.3 = (f32[32,4,128]{2,0,1:T(8,128)S(1)}, f32[32,4,128]{2,0,1:T(8,128)S(1)}, u32[]{:S(2)}, u32[]{:S(2)}) collective-permute-start(f32[32,4,128]{2,0,1:T(8,128)S(1)} %copy.62), channel_id=1, source_target_pairs={{0,8},{8,16},{16,24},{1,9},{9,17},{17,25},{2,10},{10,18},{18,26},{... | collective-permute-start | bytes 196616 | tf_op jit(solution)/shard_map/ppermute | solution.py:18
  20.1 1.9 copy.47
  22.0 2.9 %copy.49 = f32[32,4,128]{1,0,2:T(8,128)} copy(f32[32,4,128]{2,0,1:T(8,128)S(1)} %collective-permute-done.3) | data formatting | bytes 131072 | tf_op jit(solution)/shard_map/ppermute | solution.py:18
  24.8 36.2 %fusion.26 = f32[32,256,128]{1,0,2:T(8,128)} fusion(f32[32,256,128]{1,0,2:T(8,128)} %copy.44, f32[32,256,4]{1,0,2:T(8,128)S(1)} %collective-permute-done.1, f32[32,256,4]{1,0,2:T(8,128)S(1)} %collective-permute-done, f32[32,4,128]{1,0,2:T(8,128)} %copy.49, f32[32,4,128]{1,0,2:T(8,128)S(1)} %copy.47, f32[256]{0:T(256)S(1)} %dynamic_slice.7, ...), kind=kLoop, calls=%fused_computation.63 | loop fusion | flops 47185920 | bytes 8783872 | tf_op jit(solution)/shard_map/add | solution.py:46
  62.0 3.0 %collective-permute-start.4 = (f32[32,256,4]{1,0,2:T(8,128)S(1)}, f32[32,256,4]{1,0,2:T(8,128)S(1)}, u32[]{:S(2)}, u32[]{:S(2)}) collective-permute-start(f32[32,256,4]{1,0,2:T(8,128)S(1)} %get-tuple-element.12), channel_id=1, source_target_pairs={{1,0},{2,1},{3,2},{4,3},{5,4},{6,5},{7,6},{0,7},{9,8},{10,9},{11,1... | collective-permute-start | bytes 393224 | tf_op jit(solution)/shard_map/ppermute | solution.py:21
  65.1 4.3 %fusion.90 = (f32[32,4,128]{1,0,2:T(8,128)}, f32[32,4,128]{1,0,2:T(8,128)S(1)}) fusion(f32[32,256,128]{1,0,2:T(8,128)} %fusion.26), kind=kLoop, calls=%fused_computation.147 | loop fusion | bytes 262144 | tf_op jit(solution)/shard_map/slice | solution.py:21
  69.3 2.7 %copy.51 = f32[32,4,128]{2,0,1:T(8,128)S(1)} copy(f32[32,4,128]{1,0,2:T(8,128)} %get-tuple-element.10) | data formatting | bytes 131072 | tf_op jit(solution)/shard_map/slice | solution.py:21
  72.0 1.3 copy.53
  73.3 4.3 %collective-permute-start.7 = (f32[32,4,128]{2,0,1:T(8,128)S(1)}, f32[32,4,128]{2,0,1:T(8,128)S(1)}, u32[]{:S(2)}, u32[]{:S(2)}) collective-permute-start(f32[32,4,128]{2,0,1:T(8,128)S(1)} %copy.53), channel_id=1, source_target_pairs={{0,8},{8,16},{16,24},{1,9},{9,17},{17,25},{2,10},{10,18},{18,26},{... | collective-permute-start | bytes 196616 | tf_op jit(solution)/shard_map/ppermute | solution.py:18
  77.6 1.5 collective-permute-start.6
  79.2 4.6 %collective-permute-done.6 = f32[32,4,128]{2,0,1:T(8,128)S(1)} collective-permute-done((f32[32,4,128]{2,0,1:T(8,128)S(1)}, f32[32,4,128]{2,0,1:T(8,128)S(1)}, u32[]{:S(2)}, u32[]{:S(2)}) %collective-permute-start.6) | collective-permute-done | bytes 65568 | tf_op jit(solution)/shard_map/ppermute | solution.py:21
  83.8 1.9 copy.52
  85.7 2.9 %copy.54 = f32[32,4,128]{1,0,2:T(8,128)} copy(f32[32,4,128]{2,0,1:T(8,128)S(1)} %collective-permute-done.7) | data formatting | bytes 131072 | tf_op jit(solution)/shard_map/ppermute | solution.py:18
  88.5 35.6 %fusion.8 = f32[32,256,128]{1,0,2:T(8,128)} fusion(f32[32,256,128]{1,0,2:T(8,128)} %fusion.26, f32[32,256,4]{1,0,2:T(8,128)S(1)} %collective-permute-done.5, f32[32,256,4]{1,0,2:T(8,128)S(1)} %collective-permute-done.4, f32[32,4,128]{1,0,2:T(8,128)} %copy.54, f32[32,4,128]{1,0,2:T(8,128)S(1)} %copy.52, f32[256]{0:T(256)S(1)} %cosine_sqrt_fusion, ...), kind=kLoop, calls=%fused_computation.45 | loop fusion | flops 48234496 | bytes 8784896 | tf_op jit(solution)/shard_map/mul | solution.py:65
  124.1 6.9 %convolution_bitcast_fusion = f32[32,32]{0,1:T(8,128)S(1)} fusion(f32[32,256,128]{1,0,2:T(8,128)} %fusion.8), kind=kOutput, calls=%fused_computation.134 | convolution fusion | flops 402653184 | bytes 4198400 | tf_op jit(solution)/shard_map/dot_general | solution.py:67
  131.1 5.3 %copy.57 = f32[32,256,128]{2,1,0:T(8,128)} copy(f32[32,256,128]{1,0,2:T(8,128)} %fusion.8) | data formatting | bytes 8388608 | tf_op jit(solution)/shard_map/mul | solution.py:65
  136.4 37.8 %psum.7 = f32[32,32]{0,1:T(8,128)S(1)} all-reduce(f32[32,32]{0,1:T(8,128)S(1)} %convolution_bitcast_fusion), channel_id=1, replica_groups=mesh['lat'=4,'lon'=8] {'lat','lon'}, use_global_device_ids=true, to_apply=%region_0.0 | all-reduce | flops 1024 | bytes 8192 | tf_op jit(solution)/shard_map/psum | solution.py:73
  174.3 2.9 %cholesky.17 = f32[32,32]{1,0:T(8,128)S(1)} custom-call(f32[32,32]{1,0:T(8,128)S(1)} %fusion.89), custom_call_target="Cholesky" | custom-call | tf_op jit(solution)/shard_map/jit(cholesky)/cholesky | solution.py:74
  179.2 2.4 %custom-call.7 = f32[1,32,32]{1,2,0:T(8,128)S(1)} custom-call(f32[1,32,32]{2,1,0:T(8,128)S(1)} %get-tuple-element.19), custom_call_target="InvertDiagBlocksLowerTriangular" | custom-call | tf_op jit(solution)/shard_map/jit(_solve_triangular)/triangular_solve | solution.py:75
  181.9 8.4 %fusion.84 = bf16[4,8,256,128]{3,1,2,0:T(8,128)(2,1)S(1)} fusion(f32[32,32]{1,0:T(8,128)S(1)} %fusion.87, f32[4,8,256,128]{3,2,1,0:T(8,128)} %bitcast.25), kind=kOutput, calls=%fused_computation.133 | convolution fusion | flops 404750336 | bytes 6295552 | tf_op jit(solution)/shard_map/dot_general | solution.py:80
  190.3 1.8 copy.64
  (24 shorter events, 6.9 us)
Async XLA Ops:
  7.1 17.7 %collective-permute-start = (f32[32,256,4]{1,0,2:T(8,128)S(1)}, f32[32,256,4]{1,0,2:T(8,128)S(1)}, u32[]{:S(2)}, u32[]{:S(2)}) collective-permute-start(f32[32,256,4]{1,0,2:T(8,128)S(1)} %get-tuple-element.16), channel_id=1, source_target_pairs={{1,0},{2,1},{3,2},{4,3},{5,4},{6,5},{7,6},{0,7},{9,8},{10,9},{11,1... | collective-permute-start | bytes 393224 | tf_op jit(solution)/shard_map/ppermute | solution.py:21
  11.7 13.2 %collective-permute-start.1 = (f32[32,256,4]{1,0,2:T(8,128)S(1)}, f32[32,256,4]{1,0,2:T(8,128)S(1)}, u32[]{:S(2)}, u32[]{:S(2)}) collective-permute-start(f32[32,256,4]{1,0,2:T(8,128)S(1)} %get-tuple-element.17), channel_id=1, source_target_pairs={{0,1},{1,2},{2,3},{3,4},{4,5},{5,6},{6,7},{7,0},{8,9},{9,10},{10,1... | collective-permute-start | bytes 393224 | tf_op jit(solution)/shard_map/ppermute | solution.py:18
  12.7 7.4 %collective-permute-start.2 = (f32[32,4,128]{2,0,1:T(8,128)S(1)}, f32[32,4,128]{2,0,1:T(8,128)S(1)}, u32[]{:S(2)}, u32[]{:S(2)}) collective-permute-start(f32[32,4,128]{2,0,1:T(8,128)S(1)} %copy.61), channel_id=1, source_target_pairs={{8,0},{16,8},{24,16},{9,1},{17,9},{25,17},{10,2},{18,10},{26,18},{... | collective-permute-start | bytes 196616 | tf_op jit(solution)/shard_map/ppermute | solution.py:21
  14.0 8.0 %collective-permute-start.3 = (f32[32,4,128]{2,0,1:T(8,128)S(1)}, f32[32,4,128]{2,0,1:T(8,128)S(1)}, u32[]{:S(2)}, u32[]{:S(2)}) collective-permute-start(f32[32,4,128]{2,0,1:T(8,128)S(1)} %copy.62), channel_id=1, source_target_pairs={{0,8},{8,16},{16,24},{1,9},{9,17},{17,25},{2,10},{10,18},{18,26},{... | collective-permute-start | bytes 196616 | tf_op jit(solution)/shard_map/ppermute | solution.py:18
  62.0 26.5 %collective-permute-start.4 = (f32[32,256,4]{1,0,2:T(8,128)S(1)}, f32[32,256,4]{1,0,2:T(8,128)S(1)}, u32[]{:S(2)}, u32[]{:S(2)}) collective-permute-start(f32[32,256,4]{1,0,2:T(8,128)S(1)} %get-tuple-element.12), channel_id=1, source_target_pairs={{1,0},{2,1},{3,2},{4,3},{5,4},{6,5},{7,6},{0,7},{9,8},{10,9},{11,1... | collective-permute-start | bytes 393224 | tf_op jit(solution)/shard_map/ppermute | solution.py:21
  65.1 23.5 %collective-permute-start.5 = (f32[32,256,4]{1,0,2:T(8,128)S(1)}, f32[32,256,4]{1,0,2:T(8,128)S(1)}, u32[]{:S(2)}, u32[]{:S(2)}) collective-permute-start(f32[32,256,4]{1,0,2:T(8,128)S(1)} %get-tuple-element.13), channel_id=1, source_target_pairs={{0,1},{1,2},{2,3},{3,4},{4,5},{5,6},{6,7},{7,0},{8,9},{9,10},{10,1... | collective-permute-start | bytes 393224 | tf_op jit(solution)/shard_map/ppermute | solution.py:18
  73.3 12.3 %collective-permute-start.7 = (f32[32,4,128]{2,0,1:T(8,128)S(1)}, f32[32,4,128]{2,0,1:T(8,128)S(1)}, u32[]{:S(2)}, u32[]{:S(2)}) collective-permute-start(f32[32,4,128]{2,0,1:T(8,128)S(1)} %copy.53), channel_id=1, source_target_pairs={{0,8},{8,16},{16,24},{1,9},{9,17},{17,25},{2,10},{10,18},{18,26},{... | collective-permute-start | bytes 196616 | tf_op jit(solution)/shard_map/ppermute | solution.py:18
  77.6 6.2 %collective-permute-start.6 = (f32[32,4,128]{2,0,1:T(8,128)S(1)}, f32[32,4,128]{2,0,1:T(8,128)S(1)}, u32[]{:S(2)}, u32[]{:S(2)}) collective-permute-start(f32[32,4,128]{2,0,1:T(8,128)S(1)} %copy.51), channel_id=1, source_target_pairs={{8,0},{16,8},{24,16},{9,1},{17,9},{25,17},{10,2},{18,10},{26,18},{... | collective-permute-start | bytes 196616 | tf_op jit(solution)/shard_map/ppermute | solution.py:21
where the time goes:
time: 193 us; the launch traced here: 192 us
  other arithmetic  78.5 us (41%)
  blocking collectives  37.8 us (20%)
  local copies, waits for them, and re-layouts  35.6 us (18%)
  starting transfers between devices  19.2 us (10%)
  matrix products  15.5 us (8%)
  waiting for transfers between devices  4.65 us (2%)
    psum x1, blocking collectives, shards(): gram_matrix = lax.psum(partial_gram, ('lat', 'lon'))  37.8 us
    add x1, other arithmetic, diffuse(): center + zonal_rate[None, :, None] * zonal_part  36.2 us
    mul x1, other arithmetic, shards(): smoothed * area_weight(row_start, row_count, total_rows)[None, :, None]  35.6 us
    ppermute x4, starting transfers between devices, with_halo(): lax.ppermute(lax.slice_in_dim(block, 0, width, axis=dim), axis, backward)  10.3 us
    slice x5, local copies, waits for them, and re-layouts, with_halo(): lax.slice_in_dim(block, 0, width, axis=dim)  9.91 us
    ppermute x4, starting transfers between devices, with_halo(): lax.ppermute(lax.slice_in_dim(block, block.shape[dim] - width, None, axis...  8.85 us
    dot_general x1, matrix products, shards(): jnp.dot(inverse, flat_field, precision=lax.Precision.HIGHEST, preferred_e...  8.37 us
    unnamed x5, local copies, waits for them, and re-layouts  7.98 us
  transfers between devices with their start and end apart: 8, of which 1 were waited for; matrix products, arithmetic and copies ran while one was open for 11% of the time, Pallas kernels for 0%

commit v1 on v0

v1 whole, which is shorter than its diff:
```python
import functools
import math

import jax
import jax.numpy as jnp
import numpy as np
from jax import lax
from jax.experimental import pallas as pl
from jax.experimental.pallas import tpu as pltpu
from jax.sharding import PartitionSpec as P

stencil_weights = (-205.0 / 72.0, 8.0 / 5.0, -1.0 / 5.0, 8.0 / 315.0, -1.0 / 560.0)

HALO = 8
STRIP = 2 * HALO
LANES = 128
GROUPS = LANES // STRIP
TILE = 16
VMEM_BYTES = 48 * 1024 * 1024


def area_weight(first_row, row_count, total_rows):
    row_index = (jnp.arange(row_count) + first_row).astype(jnp.float32)
    latitude = (-90.0 + (row_index + 0.5) * (180.0 / total_rows)) * (math.pi / 180.0)
    return jnp.sqrt(jnp.cos(latitude))


def hi_lo(values):
    hi = values.astype(jnp.bfloat16)
    lo = (values - hi.astype(jnp.float32)).astype(jnp.bfloat16)
    return hi, lo


def band(in_cols, out_cols):
    offset = np.abs(np.asarray(in_cols)[:, None] - np.asarray(out_cols)[None, :])
    table = np.asarray(stencil_weights, np.float32)
    return np.where(offset <= 4, table[np.minimum(offset, 4)], np.float32(0.0)).astype(np.float32)


def two_terms(matrix):
    hi = matrix.astype(jnp.bfloat16)
    lo = (matrix - hi.astype(np.float32)).astype(jnp.bfloat16)
    return np.concatenate([hi, lo], axis=1)


def zonal_matrices():
    own = np.arange(LANES)
    outer = np.concatenate([np.arange(-HALO, 0), LANES + np.arange(HALO)])
    inner = np.concatenate([np.arange(LANES - HALO, LANES), np.arange(HALO)])
    main = two_terms(band(own, own))
    side = two_terms(band(outer, own))
    near = band(outer, outer)
    far = band(inner, outer)
    near[:HALO, HALO:] = near[HALO:, :HALO] = 0.0
    far[:HALO, :HALO] = far[HALO:, HALO:] = 0.0
    strip_near = np.zeros((LANES, LANES), np.float32)
    strip_far = np.zeros((LANES, LANES), np.float32)
    for group in range(GROUPS):
        at = slice(group * STRIP, (group + 1) * STRIP)
        strip_near[at, at] = near
        strip_far[at, at] = far
    strip_near, strip_far = two_terms(strip_near), two_terms(strip_far)
    return (
        np.concatenate([main, main], axis=0),
        side,
        np.concatenate([strip_near, strip_near, strip_far, strip_far], axis=0),
    )


def strip_kernel(span, field_ref, turned_ref, strip_ref):
    rows = turned_ref.shape[0]
    group_of = lax.broadcasted_iota(jnp.int32, (TILE, LANES), 1) // STRIP

    def body(at, carry):
        packed = jnp.zeros((TILE, LANES), jnp.float32)
        for group in range(GROUPS):
            row = jnp.clip(group * span + at - HALO, 0, rows - 1)
            values = field_ref[pl.ds(row, TILE, stride=rows), :]
            turned_ref[row] = values
            moved = pltpu.roll(values, (HALO + STRIP * group) % LANES, 1)
            packed = jnp.where(group_of == group, moved, packed)
        strip_ref[at] = packed
        return carry

    lax.fori_loop(0, span, body, 0)


def message_kernel(span, strip_ref, low_ref, high_ref, full_ref, first_ref, second_ref):
    snaps = strip_ref.shape[1]
    half = span // 2
    lane = lax.broadcasted_iota(jnp.int32, (snaps, LANES), 1)
    lat_even = lax.axis_index("lat") % 2 == 0
    lon_even = lax.axis_index("lon") % 2 == 0
    full_ref[...] = strip_ref[...]
    for at in range(HALO):
        first = low_ref[pl.ds(at, snaps, stride=HALO), :]
        second = high_ref[pl.ds(at, snaps, stride=HALO), :]
        north = jnp.where(lat_even, second, first)
        south = jnp.where(lat_even, first, second)
        full_ref[at] = jnp.where(lane < STRIP, pltpu.roll(north, HALO, 1), full_ref[at])
        last = span - HALO + at
        full_ref[last] = jnp.where(
            lane >= LANES - STRIP, pltpu.roll(south, LANES - HALO, 1), full_ref[last]
        )
    left = lane % STRIP < HALO
    for at in range(half):
        upper, lower = full_ref[at], full_ref[at + half]
        eastward = jnp.where(left, upper, pltpu.roll(lower, HALO, 1))
        westward = jnp.where(left, pltpu.roll(lower, LANES - HALO, 1), upper)
        first_ref[at] = jnp.where(lon_even, eastward, westward)
        second_ref[at] = jnp.where(lon_even, westward, eastward)


def stencil_row(center, pairs, zonal, zonal_rate, merid_rate):
    merid = stencil_weights[1] * pairs[0]
    for offset in range(2, 5):
        merid = merid + stencil_weights[offset] * pairs[offset - 1]
    scale = 1.0 + stencil_weights[0] * merid_rate
    return scale * center + merid_rate * merid + zonal_rate * zonal


def smooth_kernel(
    span,
    rates_ref,
    turned_ref,
    strip_ref,
    first_ref,
    second_ref,
    low_ref,
    high_ref,
    main_ref,
    side_ref,
    edge_ref,
    split_ref,
    gram_ref,
    ext_ref,
    once_ref,
    both_ref,
    weights_ref,
    outer_ref,
    near_ref,
    inner_ref,
    zonal_ref,
    strip_rates_ref,
    in_sem,
    out_sem,
):
    rows, snaps, _ = turned_ref.shape
    half = span // 2
    total = span * GROUPS
    tiles = snaps // TILE
    lat_even = lax.axis_index("lat") % 2 == 0
    lon_even = lax.axis_index("lon") % 2 == 0
    lane = lax.broadcasted_iota(jnp.int32, (TILE, LANES), 1)
    left = lane % STRIP < HALO

    def load(tile):
        return pltpu.make_async_copy(
            turned_ref.at[:, tile * TILE : (tile + 1) * TILE, :],
            ext_ref.at[tile, 4 + HALO : 4 + HALO + rows],
            in_sem.at[tile],
        )

    for tile in range(tiles):
        load(tile).start()
    for group in range(GROUPS):
        weights_ref[group, : 2 * LANES] = main_ref[...]
        weights_ref[group, 2 * LANES :] = jnp.zeros((2 * LANES, 2 * LANES), jnp.bfloat16)
        for part in (2, 3):
            begin = part * LANES + group * STRIP
            weights_ref[group, begin : begin + STRIP] = side_ref[...]
    group_of = lax.broadcasted_iota(jnp.int32, (8, LANES), 1) // STRIP
    for at in range(span):
        for kind in range(2):
            value = jnp.zeros((8, LANES), jnp.float32)
            for group in range(GROUPS):
                value = jnp.where(group_of == group, rates_ref[kind, group * span + at], value)
            strip_rates_ref[kind, at] = value

    def zonal(values, packed, weights):
        hi, lo = hi_lo(values)
        product = jnp.dot(
            jnp.concatenate([hi, lo, packed], axis=1), weights, preferred_element_type=jnp.float32
        )
        return product[:, :LANES] + product[:, LANES:]

    for tile in range(tiles):
        snap = slice(tile * TILE, (tile + 1) * TILE)
        for at in range(HALO):
            first = low_ref[pl.ds(tile * TILE * HALO + at, TILE, stride=HALO), :]
            second = high_ref[pl.ds(tile * TILE * HALO + at, TILE, stride=HALO), :]
            ext_ref[tile, 4 + at] = jnp.where(lat_even, second, first)
            ext_ref[tile, 4 + HALO + rows + at] = jnp.where(lat_even, first, second)
        for at in range(4):
            ext_ref[tile, at] = jnp.zeros((TILE, LANES), jnp.float32)
            ext_ref[tile, total + 4 + at] = jnp.zeros((TILE, LANES), jnp.float32)
        for at in range(half):
            first, second = first_ref[at, snap], second_ref[at, snap]
            west = jnp.where(lon_even, second, first)
            east = jnp.where(lon_even, first, second)
            outer_ref[4 + at] = jnp.where(left, west, east)
            outer_ref[4 + half + at] = jnp.where(
                left, pltpu.roll(west, LANES - HALO, 1), pltpu.roll(east, HALO, 1)
            )
        for at in range(4):
            outer_ref[at] = pltpu.roll(outer_ref[span + at], STRIP, 1)
            outer_ref[span + 4 + at] = pltpu.roll(outer_ref[4 + at], LANES - STRIP, 1)
        outer = outer_ref[4 : 4 + span].reshape(span * TILE, LANES)
        hi, lo = hi_lo(outer)
        near_ref[...] = jnp.concatenate([hi, lo], axis=1)
        own_hi, own_lo = hi_lo(strip_ref[:, snap].reshape(span * TILE, LANES))
        product = jnp.dot(
            jnp.concatenate([hi, lo, own_hi, own_lo], axis=1),
            edge_ref[...],
            preferred_element_type=jnp.float32,
        )
        zonal_ref[...] = (product[:, :LANES] + product[:, LANES:]).reshape(span, TILE, LANES)

        def strip_row(at, carry):
            pairs = [
                outer_ref[4 + at + offset] + outer_ref[4 + at - offset] for offset in range(1, 5)
            ]
            rates = [
                jnp.concatenate([strip_rates_ref[kind, at]] * (TILE // 8), axis=0)
                for kind in range(2)
            ]
            value = stencil_row(outer_ref[4 + at], pairs, zonal_ref[at], rates[0], rates[1])
            hi, lo = hi_lo(value)
            begin = pl.multiple_of(at * TILE, TILE)
            inner_ref[pl.ds(begin, TILE), :LANES] = hi
            inner_ref[pl.ds(begin, TILE), LANES:] = lo
            return carry

        lax.fori_loop(0, span, strip_row, 0)
        load(tile).wait()

        def first_pass(group, carry):
            begin = group * span
            center = ext_ref[tile, pl.ds(4 + begin, span)].reshape(span * TILE, LANES)
            part = zonal(center, near_ref[...], weights_ref[group]).reshape(span, TILE, LANES)
            for at in range(span):
                here = 4 + begin + at
                pairs = [
                    ext_ref[tile, here + offset] + ext_ref[tile, here - offset]
                    for offset in range(1, 5)
                ]
                once_ref[here] = stencil_row(
                    ext_ref[tile, here],
                    pairs,
                    part[at],
                    rates_ref[0, begin + at],
                    rates_ref[1, begin + at],
                )
            return carry

        lax.fori_loop(0, GROUPS, first_pass, 0)
        for at in range(4):
            once_ref[at] = jnp.zeros((TILE, LANES), jnp.float32)
            once_ref[total + 4 + at] = jnp.zeros((TILE, LANES), jnp.float32)

        def second_pass(group, carry):
            begin = group * span
            center = once_ref[pl.ds(4 + begin, span)].reshape(span * TILE, LANES)
            part = zonal(center, inner_ref[...], weights_ref[group]).reshape(span, TILE, LANES)
            for at in range(span):
                here = 4 + begin + at
                pairs = [
                    once_ref[here + offset] + once_ref[here - offset] for offset in range(1, 5)
                ]
                value = rates_ref[2, begin + at] * stencil_row(
                    once_ref[here],
                    pairs,
                    part[at],
                    rates_ref[0, begin + at],
                    rates_ref[1, begin + at],
                )
                hi, lo = hi_lo(value)
                both_ref[begin + at, tile * TILE : (tile + 1) * TILE] = hi
                both_ref[begin + at, snaps + tile * TILE : snaps + (tile + 1) * TILE] = lo
            return carry

        lax.fori_loop(0, GROUPS, second_pass, 0)

    store = pltpu.make_async_copy(both_ref.at[HALO : HALO + rows], split_ref, out_sem)
    store.start()

    def product(at, total):
        two = jnp.concatenate([both_ref[HALO + 2 * at], both_ref[HALO + 2 * at + 1]], axis=1)
        return total + lax.dot_general(
            two, two, (((1,), (1,)), ((), ())), preferred_element_type=jnp.float32
        )

    grams = lax.fori_loop(
        0, rows // 2, product, jnp.zeros((2 * snaps, 2 * snaps), jnp.float32), unroll=8
    )
    gram_ref[...] = (
        grams[:snaps, :snaps]
        + grams[snaps:, snaps:]
        + (grams[:snaps, snaps:] + grams[snaps:, :snaps])
    )
    store.wait()


def basis_kernel(root_count, gram_ref, split_ref, basis_ref, factor_ref, left_ref, wide_ref):
    snaps = gram_ref.shape[0]
    rows = split_ref.shape[0]

    @pl.when(pl.program_id(0) == 0)
    def _():
        row = lax.broadcasted_iota(jnp.int32, (snaps, 2 * snaps), 0)
        col = lax.broadcasted_iota(jnp.int32, (snaps, 2 * snaps), 1)
        work = jnp.concatenate([gram_ref[...], jnp.zeros((snaps, snaps), jnp.float32)], axis=1)
        work = jnp.where(col == row + snaps, 1.0, work)
        for step in range(snaps):
            pivot_row = work[step : step + 1, :]
            ratio = work[:, step : step + 1] / work[step : step + 1, step : step + 1]
            work = work - jnp.where(row > step, ratio, 0.0) * pivot_row
        diagonal = jnp.sum(jnp.where(row == col, work, 0.0), axis=1, keepdims=True)
        work = work * lax.rsqrt(diagonal)
        upper = jnp.where(col >= row, work, 0.0)
        factor_ref[...] = upper[:, :snaps] / root_count
        hi, lo = hi_lo(work[:, snaps:] * root_count)
        left_ref[:snaps] = jnp.concatenate([hi, hi], axis=1)
        left_ref[snaps:] = jnp.concatenate([lo, jnp.zeros_like(lo)], axis=1)

    left = left_ref[...]

    def body(at, carry):
        two = jnp.concatenate([split_ref[2 * at], split_ref[2 * at + 1]], axis=1)
        product = jnp.dot(left, two, preferred_element_type=jnp.float32)
        value = product[:snaps] + product[snaps:]
        wide_ref[pl.ds(2 * at, snaps, stride=rows), :] = value[:, :LANES]
        wide_ref[pl.ds(2 * at + 1, snaps, stride=rows), :] = value[:, LANES:]
        return carry

    lax.fori_loop(0, rows // 2, body, 0, unroll=4)
    for snap in range(snaps):
        basis_ref[snap] = wide_ref[snap * rows : (snap + 1) * rows].astype(jnp.bfloat16)


def pair_permutes(values, axis, periodic):
    count = lax.axis_size(axis)
    inner = [(i, i ^ 1) for i in range(count)]
    outer = []
    for i in range(1, count, 2):
        if periodic or i + 1 < count:
            outer += [(i, (i + 1) % count), ((i + 1) % count, i)]
    return lax.ppermute(values[0], axis, inner), lax.ppermute(values[1], axis, outer)


def sum_all(values):
    for axis in ("lon", "lat"):
        count = lax.axis_size(axis)
        step = 1
        while step < count:
            values = values + lax.ppermute(values, axis, [(i, i ^ step) for i in range(count)])
            step *= 2
    return values


def whole(memory_space=pltpu.VMEM):
    return pl.BlockSpec(memory_space=memory_space)


def shards(field, lon_rate, lat_rate):
    snaps, rows, cols = field.shape
    lat, lon = lax.axis_index("lat"), lax.axis_index("lon")
    row_start = lat * rows
    total_rows = rows * lax.axis_size("lat")
    total_cells = total_rows * cols * lax.axis_size("lon")
    span = (rows + 2 * HALO) // GROUPS
    tiles = snaps // TILE
    f32 = jnp.float32
    limits = pltpu.CompilerParams(vmem_limit_bytes=VMEM_BYTES)

    lat_even = lat % 2 == 0
    start = jnp.where(lat_even, rows - HALO, 0)
    other = rows - HALO - start
    edges = [
        lax.dynamic_slice_in_dim(field, begin, HALO, axis=1).reshape(snaps * HALO, cols)
        for begin in (start, other)
    ]
    low, high = pair_permutes(edges, "lat", False)

    turned, strip = pl.pallas_call(
        functools.partial(strip_kernel, span),
        grid=(tiles,),
        in_specs=[pl.BlockSpec((TILE * rows, cols), lambda i: (i, 0))],
        out_specs=[
            pl.BlockSpec((rows, TILE, cols), lambda i: (0, i, 0)),
            pl.BlockSpec((span, TILE, cols), lambda i: (0, i, 0)),
        ],
        out_shape=[
            jax.ShapeDtypeStruct((rows, snaps, cols), f32),
            jax.ShapeDtypeStruct((span, snaps, cols), f32),
        ],
        compiler_params=limits,
        name="turn_and_pack",
    )(field.reshape(snaps * rows, cols))

    half = jax.ShapeDtypeStruct((span // 2, snaps, cols), f32)
    strip, first, second = pl.pallas_call(
        functools.partial(message_kernel, span),
        in_specs=[whole()] * 3,
        out_specs=[whole()] * 3,
        out_shape=[jax.ShapeDtypeStruct(strip.shape, f32), half, half],
        compiler_params=limits,
        name="lon_messages",
    )(strip, low, high)
    first, second = pair_permutes([first, second], "lon", True)

    pad = jnp.zeros((HALO,), f32)
    rates = [
        lax.dynamic_slice_in_dim(jnp.concatenate([pad, rate, pad]), row_start, rows + 2 * HALO)
        for rate in (lon_rate, lat_rate)
    ]
    weight = jnp.concatenate([pad, area_weight(row_start, rows, total_rows), pad])
    rates = jnp.stack([rates[0], rates[1], weight])

    main, side, edge = zonal_matrices()
    total = span * GROUPS
    bf16 = jnp.bfloat16
    split, gram = pl.pallas_call(
        functools.partial(smooth_kernel, span),
        in_specs=[whole(pltpu.SMEM), whole(pl.ANY)] + [whole()] * 8,
        out_specs=[whole(pl.ANY), whole()],
        out_shape=[
            jax.ShapeDtypeStruct((rows, 2 * snaps, cols), bf16),
            jax.ShapeDtypeStruct((snaps, snaps), f32),
        ],
        scratch_shapes=[
            pltpu.VMEM((tiles, total + 8, TILE, cols), f32),
            pltpu.VMEM((total + 8, TILE, cols), f32),
            pltpu.VMEM((total, 2 * snaps, cols), bf16),
            pltpu.VMEM((GROUPS, 4 * LANES, 2 * LANES), bf16),
            pltpu.VMEM((span + 8, TILE, cols), f32),
            pltpu.VMEM((span * TILE, 2 * LANES), bf16),
            pltpu.VMEM((span * TILE, 2 * LANES), bf16),
            pltpu.VMEM((span, TILE, cols), f32),
            pltpu.VMEM((2, span, 8, cols), f32),
            pltpu.SemaphoreType.DMA((tiles,)),
            pltpu.SemaphoreType.DMA,
        ],
        compiler_params=limits,
        name="smooth_and_gram",
    )(rates, turned, strip, first, second, low, high, main, side, edge)

    gram = sum_all(gram)
    block = 64
    basis, factor = pl.pallas_call(
        functools.partial(basis_kernel, math.sqrt(total_cells)),
        grid=(rows // block,),
        in_specs=[
            pl.BlockSpec((snaps, snaps), lambda i: (0, 0)),
            pl.BlockSpec((block, 2 * snaps, cols), lambda i: (i, 0, 0)),
        ],
        out_specs=[
            pl.BlockSpec((snaps, block, cols), lambda i: (0, i, 0)),
            pl.BlockSpec((snaps, snaps), lambda i: (0, 0)),
        ],
        out_shape=[
            jax.ShapeDtypeStruct((snaps, rows, cols), bf16),
            jax.ShapeDtypeStruct((snaps, snaps), f32),
        ],
        scratch_shapes=[
            pltpu.VMEM((2 * snaps, 2 * snaps), bf16),
            pltpu.VMEM((snaps * block, cols), f32),
        ],
        compiler_params=limits,
        name="factor_and_basis",
    )(gram, split)
    return (basis, factor)


def solution(mesh):
    return jax.shard_map(
        shards,
        mesh=mesh,
        in_specs=(P(None, "lat", "lon"), P(), P()),
        out_specs=(P(None, "lat", "lon"), P()),
        check_vma=False,
    )
```

time: 193 us -> 78.5 us (0.41)
  other arithmetic: 78.5 us -> 0.16 us
  Pallas kernels: 0 us -> 40.6 us
  blocking collectives: 37.8 us -> 0 us
  local copies, waits for them, and re-layouts: 35.6 us -> 3.4 us
  waiting for transfers between devices: 4.65 us -> 21.2 us
  matrix products: 15.5 us -> 0 us
  starting transfers between devices: 19.2 us -> 12.1 us
    pallas_call x0 -> x4, Pallas kernels: none -> 40.6 us  [the longest x1 18.3 us: shards(): pl.pallas_call(functools.partial(smooth_kernel, span), in_specs=[whole(pl...]
    psum x1 -> x0, blocking collectives: 37.8 us -> none  [shards(): gram_matrix = lax.psum(partial_gram, ('lat', 'lon'))]
    add x1 -> x5, other arithmetic: 36.2 us -> 0.02 us  [sum_all(): values + lax.ppermute(values, axis, [(i, i ^ step) for i in range(count)])]
    mul x1 -> x0, other arithmetic: 35.6 us -> none  [shards(): smoothed * area_weight(row_start, row_count, total_rows)[None, :, None]]
    ppermute x8 -> x9, waiting for transfers between devices: 4.65 us -> 21.2 us  [the longest x5 15.2 us: sum_all(): lax.ppermute(values, axis, [(i, i ^ step) for i in range(count)])]
    dot_general x2 -> x0, matrix products: 15.3 us -> none  [the longest x1 8.37 us: shards(): jnp.dot(inverse, flat_field, precision=lax.Precision.HIGHEST, preferred_e...]
    slice x6 -> x0, local copies, waits for them, and re-layouts: 11.2 us -> none  [the longest x5 9.91 us: with_halo(): lax.slice_in_dim(block, 0, width, axis=dim)]
    ppermute x4 -> x0, local copies, waits for them, and re-layouts: 9.47 us -> none  [the longest x2 5.73 us: with_halo(): lax.ppermute(lax.slice_in_dim(block, block.shape[dim] - width, None, axis...]
  transfers between devices with their start and end apart: 8 -> 9, of which waited for: 1 -> 6; matrix products, arithmetic and copies ran while one was open for 11% -> 1% of each run, Pallas kernels for 0% -> 15%
where the time goes in v1:
time: 78.5 us; the launch traced here: 78.3 us
  Pallas kernels  40.6 us (52%)
  waiting for transfers between devices  21.2 us (27%)
  starting transfers between devices  12.1 us (15%)
  local copies, waits for them, and re-layouts  3.4 us (4%)
  between operations  0.79 us (1%)
    pallas_call x1, Pallas kernels, shards(): pl.pallas_call(functools.partial(smooth_kernel, span), in_specs=[whole(pl...  18.3 us
    ppermute x5, waiting for transfers between devices, sum_all(): lax.ppermute(values, axis, [(i, i ^ step) for i in range(count)])  15.2 us
    pallas_call x1, Pallas kernels, shards(): pl.pallas_call(functools.partial(strip_kernel, span), grid=(tiles,), in_s...  11.5 us
    pallas_call x1, Pallas kernels, shards(): pl.pallas_call(functools.partial(basis_kernel, math.sqrt(total_cells)), g...  10.5 us
    ppermute x2, waiting for transfers between devices, pair_permutes(): lax.ppermute(values[1], axis, outer)  6.01 us
    ppermute x2, starting transfers between devices, pair_permutes(): lax.ppermute(values[0], axis, inner)  5.81 us
    ppermute x2, starting transfers between devices, pair_permutes(): lax.ppermute(values[1], axis, outer)  4.37 us
    unnamed x12, local copies, waits for them, and re-layouts  1.98 us
  transfers between devices with their start and end apart: 9, of which 6 were waited for; matrix products, arithmetic and copies ran while one was open for 1% of the time, Pallas kernels for 15%

profile of v1, /device:TPU:0, one launch (start us, length us, event | category | flops | bytes accessed | tf_op | source)
XLA Modules:
  0.0 78.3 jit_solution(16180428195443232501)
XLA Ops:
  0.7 1.1 %dynamic-slice_bitcast_fusion = (f32[256,128]{1,0:T(8,128)S(1)}, f32[256,128]{1,0:T(8,128)S(1)}) fusion(f32[32,256,128]{2,1,0:T(8,128)} %param.6, s32[]{:T(128)S(6)} %select_n.22, s32[]{:T(128)S(6)} %select_n.21), kind=kLoop, calls=%fused_computation | loop fusion | bytes 524296 | tf_op jit(solution)/shard_map/reshape | solution.py:380
  1.8 0.7 collective-permute-start.1
  2.5 5.7 %collective-permute-start = (f32[256,128]{1,0:T(8,128)S(1)}, f32[256,128]{1,0:T(8,128)S(1)}, u32[]{:S(2)}, u32[]{:S(2)}) collective-permute-start(f32[256,128]{1,0:T(8,128)S(1)} %get-tuple-element.17), channel_id=1, source_target_pairs={{0,8},{8,0},{16,24},{24,16},{1,9},{9,1},{17,25},{25,17},{2,10},{10... | collective-permute-start | bytes 393224 | tf_op jit(solution)/shard_map/ppermute | solution.py:348
  8.2 11.5 %turn_and_pack.1 = (f32[256,32,128]{2,1,0:T(8,128)S(1)}, f32[34,32,128]{2,1,0:T(8,128)S(1)}) custom-call(f32[8192,128]{1,0:T(8,128)} %bitcast.5), custom_call_target="tpu_custom_call" | custom-call | tf_op jit(solution)/shard_map/turn_and_pack/pallas_call | solution.py:385
  19.7 1.9 %copy-done = f32[256,32,128]{2,1,0:T(8,128)} copy-done((f32[256,32,128]{2,1,0:T(8,128)}, f32[256,32,128]{2,1,0:T(8,128)S(1)}, u32[]{:S(2)}) %copy-start) | copy-done | bytes 4194328
  21.7 0.3 lon_messages.1
  22.0 0.1 collective-permute-start.2
  22.1 3.7 %collective-permute-start.3 = (f32[17,32,128]{2,1,0:T(8,128)S(1)}, f32[17,32,128]{2,1,0:T(8,128)S(1)}, u32[]{:S(2)}, u32[]{:S(2)}) collective-permute-start(f32[17,32,128]{2,1,0:T(8,128)S(1)} %get-tuple-element.13), channel_id=1, source_target_pairs={{1,2},{2,1},{3,4},{4,3},{5,6},{6,5},{7,0},{0,7},{9,10},{10,9},{11,... | collective-permute-start | bytes 835592 | tf_op jit(solution)/shard_map/ppermute | solution.py:348
  25.8 0.1 pad_maximum_fusion.1
  25.9 0.1 concatenate.10
  26.0 0.1 dynamic_slice.13
  26.1 0.1 concatenate.9
  26.1 0.1 dynamic_slice.12
  26.3 6.0 %collective-permute-done.3.second_ref = f32[17,32,128]{2,1,0:T(8,128)S(1)} collective-permute-done((f32[17,32,128]{2,1,0:T(8,128)S(1)}, f32[17,32,128]{2,1,0:T(8,128)S(1)}, u32[]{:S(2)}, u32[]{:S(2)}) %collective-permute-start.3) | collective-permute-done | bytes 278560 | tf_op jit(solution)/shard_map/ppermute | solution.py:348
  32.3 18.3 %smooth_and_gram.1 = (bf16[256,64,128]{2,1,0:T(8,128)(2,1)S(1)}, f32[32,32]{1,0:T(8,128)S(1)}) custom-call(f32[3,272]{1,0:T(4,128)S(1)} %pad_maximum_fusion.rates_ref, f32[256,32,128]{2,1,0:T(8,128)} %copy-done, f32[34,32,128]{2,1,0:T(8,128)S(1)} %get-tuple-element.11.strip_ref, f32[17,32,128]{2,1,0:T(8,128)S(1)} %collective-permute-done.2.first_ref, ...), custom_call_target="tpu_custom_call" | custom-call | tf_op jit(solution)/shard_map/smooth_and_gram/pallas_call | solution.py:423
  50.6 0.1 collective-permute-start.4
  50.7 1.2 %collective-permute-done.4 = f32[32,32]{1,0:T(8,128)S(1)} collective-permute-done((f32[32,32]{1,0:T(8,128)S(1)}, f32[32,32]{1,0:T(8,128)S(1)}, u32[]{:S(2)}, u32[]{:S(2)}) %collective-permute-start.4) | collective-permute-done | bytes 4128 | tf_op jit(solution)/shard_map/ppermute | solution.py:356
  51.9 0.5 collective-permute-start.5
  52.3 3.3 %collective-permute-done.5 = f32[32,32]{1,0:T(8,128)S(1)} collective-permute-done((f32[32,32]{1,0:T(8,128)S(1)}, f32[32,32]{1,0:T(8,128)S(1)}, u32[]{:S(2)}, u32[]{:S(2)}) %collective-permute-start.5) | collective-permute-done | bytes 4128 | tf_op jit(solution)/shard_map/ppermute | solution.py:356
  55.6 1.4 %collective-permute-start.6 = (f32[32,32]{1,0:T(8,128)S(1)}, f32[32,32]{1,0:T(8,128)S(1)}, u32[]{:S(2)}, u32[]{:S(2)}) collective-permute-start(f32[32,32]{1,0:T(8,128)S(1)} %add.56), channel_id=1, source_target_pairs={{0,4},{1,5},{2,6},{3,7},{4,0},{5,1},{6,2},{7,3},{8,12},{9,13},{10,... | collective-permute-start | bytes 12296 | tf_op jit(solution)/shard_map/ppermute | solution.py:356
  57.0 3.3 %collective-permute-done.6 = f32[32,32]{1,0:T(8,128)S(1)} collective-permute-done((f32[32,32]{1,0:T(8,128)S(1)}, f32[32,32]{1,0:T(8,128)S(1)}, u32[]{:S(2)}, u32[]{:S(2)}) %collective-permute-start.6) | collective-permute-done | bytes 4128 | tf_op jit(solution)/shard_map/ppermute | solution.py:356
  60.3 3.7 %collective-permute-done.7 = f32[32,32]{1,0:T(8,128)S(1)} collective-permute-done((f32[32,32]{1,0:T(8,128)S(1)}, f32[32,32]{1,0:T(8,128)S(1)}, u32[]{:S(2)}, u32[]{:S(2)}) %collective-permute-start.7) | collective-permute-done | bytes 4128 | tf_op jit(solution)/shard_map/ppermute | solution.py:356
  64.1 3.7 %collective-permute-done.8 = f32[32,32]{1,0:T(8,128)S(1)} collective-permute-done((f32[32,32]{1,0:T(8,128)S(1)}, f32[32,32]{1,0:T(8,128)S(1)}, u32[]{:S(2)}, u32[]{:S(2)}) %collective-permute-start.8) | collective-permute-done | bytes 4128 | tf_op jit(solution)/shard_map/ppermute | solution.py:356
  67.8 10.5 %factor_and_basis.1 = (bf16[32,256,128]{2,1,0:T(8,128)(2,1)}, f32[32,32]{1,0:T(8,128)}) custom-call(f32[32,32]{1,0:T(8,128)S(1)} %add.59.gram_ref, bf16[256,64,128]{2,1,0:T(8,128)(2,1)S(1)} %get-tuple-element.15.split_ref), custom_call_target="tpu_custom_call" | custom-call | tf_op jit(solution)/shard_map/factor_and_basis/pallas_call | solution.py:450
  (27 shorter events, 0.2 us)
Async XLA Ops:
  0.6 31.6 %copy-start.1 = (bf16[512,256]{1,0:T(8,128)(2,1)S(1)}, bf16[512,256]{1,0:T(8,128)(2,1)}, u32[]{:S(2)}) copy-start(bf16[512,256]{1,0:T(8,128)(2,1)} %constant.46.clone.edge_ref) | copy-start | bytes 786436
  0.6 31.6 %copy-start.3 = (bf16[16,256]{1,0:T(8,128)(2,1)S(1)}, bf16[16,256]{1,0:T(8,128)(2,1)}, u32[]{:S(2)}) copy-start(bf16[16,256]{1,0:T(8,128)(2,1)} %constant.45.clone.side_ref) | copy-start | bytes 24580
  0.7 31.6 %copy-start.2 = (bf16[256,256]{1,0:T(8,128)(2,1)S(1)}, bf16[256,256]{1,0:T(8,128)(2,1)}, u32[]{:S(2)}) copy-start(bf16[256,256]{1,0:T(8,128)(2,1)} %constant.44.clone.main_ref) | copy-start | bytes 393220
  0.7 25.2 %copy-start.4 = (f32[1024]{0:T(1024)S(1)}, f32[1024]{0:T(1024)}, u32[]{:S(2)}) copy-start(f32[1024]{0:T(1024)} %param.8) | copy-start | bytes 12292
  0.7 25.4 %copy-start.5 = (f32[1024]{0:T(1024)S(1)}, f32[1024]{0:T(1024)}, u32[]{:S(2)}) copy-start(f32[1024]{0:T(1024)} %param.7) | copy-start | bytes 12292
  1.8 19.9 %collective-permute-start.1 = (f32[256,128]{1,0:T(8,128)S(1)}, f32[256,128]{1,0:T(8,128)S(1)}, u32[]{:S(2)}, u32[]{:S(2)}) collective-permute-start(f32[256,128]{1,0:T(8,128)S(1)} %get-tuple-element.16), channel_id=1, source_target_pairs={{8,16},{16,8},{9,17},{17,9},{10,18},{18,10},{11,19},{19,11},{12,20... | collective-permute-start | bytes 393224 | tf_op jit(solution)/shard_map/ppermute | solution.py:348
  2.5 19.2 %collective-permute-start = (f32[256,128]{1,0:T(8,128)S(1)}, f32[256,128]{1,0:T(8,128)S(1)}, u32[]{:S(2)}, u32[]{:S(2)}) collective-permute-start(f32[256,128]{1,0:T(8,128)S(1)} %get-tuple-element.17), channel_id=1, source_target_pairs={{0,8},{8,0},{16,24},{24,16},{1,9},{9,1},{17,25},{25,17},{2,10},{10... | collective-permute-start | bytes 393224 | tf_op jit(solution)/shard_map/ppermute | solution.py:348
  19.7 2.0 %copy-start = (f32[256,32,128]{2,1,0:T(8,128)}, f32[256,32,128]{2,1,0:T(8,128)S(1)}, u32[]{:S(2)}) copy-start(f32[256,32,128]{2,1,0:T(8,128)S(1)} %get-tuple-element.9.turned_ref) | copy-start | bytes 12582916
  22.0 4.3 %collective-permute-start.2 = (f32[17,32,128]{2,1,0:T(8,128)S(1)}, f32[17,32,128]{2,1,0:T(8,128)S(1)}, u32[]{:S(2)}, u32[]{:S(2)}) collective-permute-start(f32[17,32,128]{2,1,0:T(8,128)S(1)} %get-tuple-element.12), channel_id=1, source_target_pairs={{0,1},{1,0},{2,3},{3,2},{4,5},{5,4},{6,7},{7,6},{8,9},{9,8},{10,11... | collective-permute-start | bytes 835592 | tf_op jit(solution)/shard_map/ppermute | solution.py:348
  22.1 10.2 %collective-permute-start.3 = (f32[17,32,128]{2,1,0:T(8,128)S(1)}, f32[17,32,128]{2,1,0:T(8,128)S(1)}, u32[]{:S(2)}, u32[]{:S(2)}) collective-permute-start(f32[17,32,128]{2,1,0:T(8,128)S(1)} %get-tuple-element.13), channel_id=1, source_target_pairs={{1,2},{2,1},{3,4},{4,3},{5,6},{6,5},{7,0},{0,7},{9,10},{10,9},{11,... | collective-permute-start | bytes 835592 | tf_op jit(solution)/shard_map/ppermute | solution.py:348
  50.6 1.2 %collective-permute-start.4 = (f32[32,32]{1,0:T(8,128)S(1)}, f32[32,32]{1,0:T(8,128)S(1)}, u32[]{:S(2)}, u32[]{:S(2)}) collective-permute-start(f32[32,32]{1,0:T(8,128)S(1)} %get-tuple-element.14), channel_id=1, source_target_pairs={{0,1},{1,0},{2,3},{3,2},{4,5},{5,4},{6,7},{7,6},{8,9},{9,8},{10,11... | collective-permute-start | bytes 12296 | tf_op jit(solution)/shard_map/ppermute | solution.py:356
  51.9 3.7 %collective-permute-start.5 = (f32[32,32]{1,0:T(8,128)S(1)}, f32[32,32]{1,0:T(8,128)S(1)}, u32[]{:S(2)}, u32[]{:S(2)}) collective-permute-start(f32[32,32]{1,0:T(8,128)S(1)} %add.55), channel_id=1, source_target_pairs={{0,2},{1,3},{2,0},{3,1},{4,6},{5,7},{6,4},{7,5},{8,10},{9,11},{10,... | collective-permute-start | bytes 12296 | tf_op jit(solution)/shard_map/ppermute | solution.py:356
  55.6 4.7 %collective-permute-start.6 = (f32[32,32]{1,0:T(8,128)S(1)}, f32[32,32]{1,0:T(8,128)S(1)}, u32[]{:S(2)}, u32[]{:S(2)}) collective-permute-start(f32[32,32]{1,0:T(8,128)S(1)} %add.56), channel_id=1, source_target_pairs={{0,4},{1,5},{2,6},{3,7},{4,0},{5,1},{6,2},{7,3},{8,12},{9,13},{10,... | collective-permute-start | bytes 12296 | tf_op jit(solution)/shard_map/ppermute | solution.py:356
  60.3 3.7 %collective-permute-start.7 = (f32[32,32]{1,0:T(8,128)S(1)}, f32[32,32]{1,0:T(8,128)S(1)}, u32[]{:S(2)}, u32[]{:S(2)}) collective-permute-start(f32[32,32]{1,0:T(8,128)S(1)} %add.57), channel_id=1, source_target_pairs={{0,8},{8,0},{16,24},{24,16},{1,9},{9,1},{17,25},{25,17},{2,10},{10... | collective-permute-start | bytes 12296 | tf_op jit(solution)/shard_map/ppermute | solution.py:356
  64.1 3.7 %collective-permute-start.8 = (f32[32,32]{1,0:T(8,128)S(1)}, f32[32,32]{1,0:T(8,128)S(1)}, u32[]{:S(2)}, u32[]{:S(2)}) collective-permute-start(f32[32,32]{1,0:T(8,128)S(1)} %add.58), channel_id=1, source_target_pairs={{0,16},{8,24},{16,0},{24,8},{1,17},{9,25},{17,1},{25,9},{2,18},{10... | collective-permute-start | bytes 12296 | tf_op jit(solution)/shard_map/ppermute | solution.py:356

commit v2 on v1

v2 whole, which is shorter than its diff:
```python
import functools
import math

import jax
import jax.numpy as jnp
import numpy as np
from jax import lax
from jax.experimental import pallas as pl
from jax.experimental.pallas import tpu as pltpu
from jax.sharding import PartitionSpec as P

stencil_weights = (-205.0 / 72.0, 8.0 / 5.0, -1.0 / 5.0, 8.0 / 315.0, -1.0 / 560.0)

HALO = 8
STRIP = 2 * HALO
LANES = 128
GROUPS = LANES // STRIP
TILE = 16
VMEM_BYTES = 40 * 1024 * 1024


def area_weight(first_row, row_count, total_rows):
    row_index = (jnp.arange(row_count) + first_row).astype(jnp.float32)
    latitude = (-90.0 + (row_index + 0.5) * (180.0 / total_rows)) * (math.pi / 180.0)
    return jnp.sqrt(jnp.cos(latitude))


def hi_lo(values):
    hi = values.astype(jnp.bfloat16)
    lo = (values - hi.astype(jnp.float32)).astype(jnp.bfloat16)
    return hi, lo


def band(in_cols, out_cols):
    offset = np.abs(np.asarray(in_cols)[:, None] - np.asarray(out_cols)[None, :])
    table = np.asarray(stencil_weights, np.float32)
    return np.where(offset <= 4, table[np.minimum(offset, 4)], np.float32(0.0)).astype(np.float32)


def two_terms(matrix):
    hi = matrix.astype(jnp.bfloat16)
    lo = (matrix - hi.astype(np.float32)).astype(jnp.bfloat16)
    return np.concatenate([hi, lo], axis=1)


def zonal_matrices():
    own = np.arange(LANES)
    outer = np.concatenate([np.arange(-HALO, 0), LANES + np.arange(HALO)])
    inner = np.concatenate([np.arange(LANES - HALO, LANES), np.arange(HALO)])
    main = two_terms(band(own, own))
    side = two_terms(band(outer, own))
    near = band(outer, outer)
    far = band(inner, outer)
    near[:HALO, HALO:] = near[HALO:, :HALO] = 0.0
    far[:HALO, :HALO] = far[HALO:, HALO:] = 0.0
    strip_near = np.zeros((LANES, LANES), np.float32)
    strip_far = np.zeros((LANES, LANES), np.float32)
    for group in range(GROUPS):
        at = slice(group * STRIP, (group + 1) * STRIP)
        strip_near[at, at] = near
        strip_far[at, at] = far
    strip_near, strip_far = two_terms(strip_near), two_terms(strip_far)
    return (
        np.concatenate([main, main], axis=0),
        side,
        np.concatenate([strip_near, strip_near, strip_far, strip_far], axis=0),
    )


def turn_rows(field_ref, rows, store):
    def body(at, carry):
        begin = pl.multiple_of(at * 8, 8)
        store(begin, jnp.swapaxes(field_ref[:, pl.ds(begin, 8), :], 0, 1))
        return carry

    lax.fori_loop(0, rows // 8, body, 0, unroll=4)


def strip_kernel(span, field_ref, strip_ref, first_ref, second_ref, turned_ref):
    tile, rows, _ = field_ref.shape
    lat_even = lax.axis_index("lat") % 2 == 0
    north = field_ref[:, :HALO].reshape(tile * HALO, LANES)
    south = field_ref[:, rows - HALO :].reshape(tile * HALO, LANES)
    first_ref[...] = jnp.where(lat_even, south, north)
    second_ref[...] = jnp.where(lat_even, north, south)
    group_of = lax.broadcasted_iota(jnp.int32, (tile, LANES), 1) // STRIP

    def store(begin, values):
        turned_ref[pl.ds(HALO + begin, 8)] = values

    turn_rows(field_ref, rows, store)
    for at in range(HALO):
        turned_ref[at] = jnp.zeros((tile, LANES), jnp.float32)
        turned_ref[HALO + rows + at] = jnp.zeros((tile, LANES), jnp.float32)

    def body(at, carry):
        packed = jnp.zeros((tile, LANES), jnp.float32)
        for group in range(GROUPS):
            values = turned_ref[group * span + at]
            moved = pltpu.roll(values, (HALO + STRIP * group) % LANES, 1)
            packed = jnp.where(group_of == group, moved, packed)
        strip_ref[at] = packed
        return carry

    lax.fori_loop(0, span, body, 0, unroll=2)


def message_kernel(span, strip_ref, low_ref, high_ref, full_ref, first_ref, second_ref):
    snaps = strip_ref.shape[1]
    half = span // 2
    lane = lax.broadcasted_iota(jnp.int32, (snaps, LANES), 1)
    lat_even = lax.axis_index("lat") % 2 == 0
    lon_even = lax.axis_index("lon") % 2 == 0
    full_ref[...] = strip_ref[...]
    for at in range(HALO):
        first = low_ref[pl.ds(at, snaps, stride=HALO), :]
        second = high_ref[pl.ds(at, snaps, stride=HALO), :]
        north = jnp.where(lat_even, second, first)
        south = jnp.where(lat_even, first, second)
        full_ref[at] = jnp.where(lane < STRIP, pltpu.roll(north, HALO, 1), full_ref[at])
        last = span - HALO + at
        full_ref[last] = jnp.where(
            lane >= LANES - STRIP, pltpu.roll(south, LANES - HALO, 1), full_ref[last]
        )
    left = lane % STRIP < HALO
    for at in range(half):
        upper, lower = full_ref[at], full_ref[at + half]
        eastward = jnp.where(left, upper, pltpu.roll(lower, HALO, 1))
        westward = jnp.where(left, pltpu.roll(lower, LANES - HALO, 1), upper)
        first_ref[at] = jnp.where(lon_even, eastward, westward)
        second_ref[at] = jnp.where(lon_even, westward, eastward)


def stencil_row(center, pairs, zonal, zonal_rate, merid_rate):
    merid = stencil_weights[1] * pairs[0]
    for offset in range(2, 5):
        merid = merid + stencil_weights[offset] * pairs[offset - 1]
    scale = 1.0 + stencil_weights[0] * merid_rate
    return scale * center + merid_rate * merid + zonal_rate * zonal


def zonal_terms(parts, weights):
    product = jnp.dot(
        jnp.concatenate(parts, axis=1), weights, preferred_element_type=jnp.float32
    )
    return product[:, :LANES] + product[:, LANES:]


def stencil_rows(source_ref, begin, span, part, rates_ref, store):
    loaded = {}

    def row(at):
        if at not in loaded:
            loaded[at] = source_ref[begin + at]
        return loaded[at]

    for at in range(span):
        here = at + 4
        pairs = [row(here + offset) + row(here - offset) for offset in range(1, 5)]
        store(
            at,
            stencil_row(
                row(here), pairs, part[at], rates_ref[0, begin + at], rates_ref[1, begin + at]
            ),
        )


def first_kernel(span, rates_ref, field_ref, low_ref, high_ref, main_ref, once_ref, ext_ref):
    rows = field_ref.shape[1]
    total = span * GROUPS
    lat_even = lax.axis_index("lat") % 2 == 0
    for at in range(HALO):
        first = low_ref[pl.ds(at, TILE, stride=HALO), :]
        second = high_ref[pl.ds(at, TILE, stride=HALO), :]
        ext_ref[4 + at] = jnp.where(lat_even, second, first)
        ext_ref[4 + HALO + rows + at] = jnp.where(lat_even, first, second)
    for at in range(4):
        ext_ref[at] = jnp.zeros((TILE, LANES), jnp.float32)
        ext_ref[total + 4 + at] = jnp.zeros((TILE, LANES), jnp.float32)
        once_ref[at] = jnp.zeros((TILE, LANES), jnp.float32)
        once_ref[total + 4 + at] = jnp.zeros((TILE, LANES), jnp.float32)

    def turn(begin, values):
        ext_ref[pl.ds(4 + HALO + begin, 8)] = values

    turn_rows(field_ref, rows, turn)

    def body(group, carry):
        begin = group * span
        center = ext_ref[pl.ds(4 + begin, span)].reshape(span * TILE, LANES)
        part = zonal_terms(hi_lo(center), main_ref[...]).reshape(span, TILE, LANES)

        def store(at, value):
            once_ref[4 + begin + at] = value

        stencil_rows(ext_ref, begin, span, part, rates_ref, store)
        return carry

    lax.fori_loop(0, GROUPS, body, 0)


def second_kernel(
    span,
    rates_ref,
    once_ref,
    strip_ref,
    first_ref,
    second_ref,
    main_ref,
    side_ref,
    edge_ref,
    split_ref,
    gram_ref,
    full_ref,
    weights_ref,
    outer_ref,
    near_ref,
    inner_ref,
    zonal_ref,
    strip_rates_ref,
):
    both = split_ref.shape[1]
    rows = split_ref.shape[0] - HALO
    snaps = both // 2
    half = span // 2
    tile = pl.program_id(0)
    lon_even = lax.axis_index("lon") % 2 == 0
    lane = lax.broadcasted_iota(jnp.int32, (TILE, LANES), 1)
    left = lane % STRIP < HALO

    @pl.when(tile == 0)
    def _():
        for group in range(GROUPS):
            weights_ref[group, : 2 * LANES] = main_ref[...]
            weights_ref[group, 2 * LANES :] = jnp.zeros((2 * LANES, 2 * LANES), jnp.bfloat16)
            for part in (2, 3):
                begin = part * LANES + group * STRIP
                weights_ref[group, begin : begin + STRIP] = side_ref[...]
        group_of = lax.broadcasted_iota(jnp.int32, (8, LANES), 1) // STRIP
        for at in range(span):
            for kind in range(2):
                value = jnp.zeros((8, LANES), jnp.float32)
                for group in range(GROUPS):
                    value = jnp.where(group_of == group, rates_ref[kind, group * span + at], value)
                strip_rates_ref[kind, at] = value

    for at in range(half):
        first, second = first_ref[at], second_ref[at]
        west = jnp.where(lon_even, second, first)
        east = jnp.where(lon_even, first, second)
        outer_ref[4 + at] = jnp.where(left, west, east)
        outer_ref[4 + half + at] = jnp.where(
            left, pltpu.roll(west, LANES - HALO, 1), pltpu.roll(east, HALO, 1)
        )
    for at in range(4):
        outer_ref[at] = pltpu.roll(outer_ref[span + at], STRIP, 1)
        outer_ref[span + 4 + at] = pltpu.roll(outer_ref[4 + at], LANES - STRIP, 1)
    hi, lo = hi_lo(outer_ref[4 : 4 + span].reshape(span * TILE, LANES))
    near_ref[...] = jnp.concatenate([hi, lo], axis=1)
    own_hi, own_lo = hi_lo(strip_ref[...].reshape(span * TILE, LANES))
    zonal_ref[...] = zonal_terms([hi, lo, own_hi, own_lo], edge_ref[...]).reshape(
        span, TILE, LANES
    )

    def strip_row(at, carry):
        pairs = [outer_ref[4 + at + offset] + outer_ref[4 + at - offset] for offset in range(1, 5)]
        rates = [
            jnp.concatenate([strip_rates_ref[kind, at]] * (TILE // 8), axis=0) for kind in range(2)
        ]
        value = stencil_row(outer_ref[4 + at], pairs, zonal_ref[at], rates[0], rates[1])
        hi, lo = hi_lo(value)
        begin = pl.multiple_of(at * TILE, TILE)
        inner_ref[pl.ds(begin, TILE), :LANES] = hi
        inner_ref[pl.ds(begin, TILE), LANES:] = lo
        return carry

    lax.fori_loop(0, span, strip_row, 0, unroll=2)

    def complete(group, carry):
        begin = group * span
        part = zonal_terms([near_ref[...]], weights_ref[group, 2 * LANES :]).reshape(
            span, TILE, LANES
        )
        for at in range(span):
            here = 4 + begin + at
            full_ref[here] = once_ref[here] + rates_ref[0, begin + at] * part[at]
        return carry

    lax.fori_loop(0, GROUPS, complete, 0)
    for at in range(4):
        full_ref[at] = once_ref[at]
        full_ref[span * GROUPS + 4 + at] = once_ref[span * GROUPS + 4 + at]

    def second_pass(group, carry):
        begin = group * span
        center = full_ref[pl.ds(4 + begin, span)].reshape(span * TILE, LANES)
        hi, lo = hi_lo(center)
        part = zonal_terms([hi, lo, inner_ref[...]], weights_ref[group]).reshape(
            span, TILE, LANES
        )

        def store(at, value):
            hi, lo = hi_lo(rates_ref[2, begin + at] * value)
            row = jnp.maximum(begin + at - HALO, 0)
            split_ref[row, pl.ds(pl.multiple_of(tile * TILE, TILE), TILE)] = hi
            split_ref[row, pl.ds(pl.multiple_of(snaps + tile * TILE, TILE), TILE)] = lo

        stencil_rows(full_ref, begin, span, part, rates_ref, store)
        return carry

    lax.fori_loop(0, GROUPS, second_pass, 0)

    @pl.when(tile == snaps // TILE - 1)
    def _():
        def product(at, total):
            two = jnp.concatenate([split_ref[2 * at], split_ref[2 * at + 1]], axis=1)
            return total + lax.dot_general(
                two, two, (((1,), (1,)), ((), ())), preferred_element_type=jnp.float32
            )

        grams = lax.fori_loop(
            0, rows // 2, product, jnp.zeros((both, both), jnp.float32), unroll=8
        )
        gram_ref[...] = (
            grams[:snaps, :snaps]
            + grams[snaps:, snaps:]
            + (grams[:snaps, snaps:] + grams[snaps:, :snaps])
        )


def basis_kernel(root_count, gram_ref, split_ref, basis_ref, factor_ref, left_ref):
    snaps = gram_ref.shape[0]

    @pl.when(pl.program_id(0) == 0)
    def _():
        row = lax.broadcasted_iota(jnp.int32, (snaps, 2 * snaps), 0)
        col = lax.broadcasted_iota(jnp.int32, (snaps, 2 * snaps), 1)
        work = jnp.concatenate([gram_ref[...], jnp.zeros((snaps, snaps), jnp.float32)], axis=1)
        work = jnp.where(col == row + snaps, 1.0, work)
        for step in range(snaps):
            pivot_row = work[step : step + 1, :]
            ratio = work[:, step : step + 1] / work[step : step + 1, step : step + 1]
            work = work - jnp.where(row > step, ratio, 0.0) * pivot_row
        diagonal = jnp.sum(jnp.where(row == col, work, 0.0), axis=1, keepdims=True)
        work = work * lax.rsqrt(diagonal)
        upper = jnp.where(col >= row, work, 0.0)
        factor_ref[...] = upper[:, :snaps] / root_count
        hi, lo = hi_lo(work[:, snaps:] * root_count)
        left_ref[:snaps] = jnp.concatenate([hi, hi], axis=1)
        left_ref[snaps:] = jnp.concatenate([lo, jnp.zeros_like(lo)], axis=1)

    left = left_ref[...]
    start = pl.program_id(0) * basis_ref.shape[1]

    def body(at, carry):
        begin = pl.multiple_of(at * 16, 16)
        values = []
        for pair in range(8):
            row = start + begin + 2 * pair
            two = jnp.concatenate([split_ref[row], split_ref[row + 1]], axis=1)
            product = jnp.dot(left, two, preferred_element_type=jnp.float32)
            value = product[:snaps] + product[snaps:]
            values += [value[:, :LANES], value[:, LANES:]]
        turned = jnp.swapaxes(jnp.stack(values, axis=0), 0, 1)
        basis_ref[:, pl.ds(begin, 16), :] = turned.astype(jnp.bfloat16)
        return carry

    lax.fori_loop(0, basis_ref.shape[1] // 16, body, 0)


def pair_permutes(values, axis, periodic):
    count = lax.axis_size(axis)
    inner = [(i, i ^ 1) for i in range(count)]
    outer = []
    for i in range(1, count, 2):
        if periodic or i + 1 < count:
            outer += [(i, (i + 1) % count), ((i + 1) % count, i)]
    return lax.ppermute(values[0], axis, inner), lax.ppermute(values[1], axis, outer)


def sum_all(values):
    for axis in ("lon", "lat"):
        count = lax.axis_size(axis)
        step = 1
        while step < count:
            values = values + lax.ppermute(values, axis, [(i, i ^ step) for i in range(count)])
            step *= 2
    return values


def whole(memory_space=pltpu.VMEM):
    return pl.BlockSpec(memory_space=memory_space)


def shards(field, lon_rate, lat_rate):
    snaps, rows, cols = field.shape
    row_start = lax.axis_index("lat") * rows
    total_rows = rows * lax.axis_size("lat")
    total_cells = total_rows * cols * lax.axis_size("lon")
    span = (rows + 2 * HALO) // GROUPS
    tiles = snaps // TILE
    f32 = jnp.float32
    limits = pltpu.CompilerParams(vmem_limit_bytes=VMEM_BYTES)

    edge_rows = pl.BlockSpec((8 * HALO, cols), lambda i: (i, 0))
    edges = jax.ShapeDtypeStruct((snaps * HALO, cols), f32)
    strip, first, second = pl.pallas_call(
        functools.partial(strip_kernel, span),
        grid=(snaps // 8,),
        in_specs=[pl.BlockSpec((8, rows, cols), lambda i: (i, 0, 0))],
        out_specs=[
            pl.BlockSpec((span, 8, cols), lambda i: (0, i, 0)),
            edge_rows,
            edge_rows,
        ],
        out_shape=[jax.ShapeDtypeStruct((span, snaps, cols), f32), edges, edges],
        scratch_shapes=[pltpu.VMEM((rows + 2 * HALO, 8, cols), f32)],
        compiler_params=pltpu.CompilerParams(vmem_limit_bytes=60 * 1024 * 1024),
        name="pack_edges",
    )(field)
    low, high = pair_permutes([first, second], "lat", False)

    half = jax.ShapeDtypeStruct((span // 2, snaps, cols), f32)
    strip, first, second = pl.pallas_call(
        functools.partial(message_kernel, span),
        in_specs=[whole()] * 3,
        out_specs=[whole()] * 3,
        out_shape=[jax.ShapeDtypeStruct(strip.shape, f32), half, half],
        compiler_params=limits,
        name="lon_messages",
    )(strip, low, high)
    first, second = pair_permutes([first, second], "lon", True)

    pad = jnp.zeros((HALO,), f32)
    rates = [
        lax.dynamic_slice_in_dim(jnp.concatenate([pad, rate, pad]), row_start, rows + 2 * HALO)
        for rate in (lon_rate, lat_rate)
    ]
    weight = jnp.concatenate([pad, area_weight(row_start, rows, total_rows), pad])
    rates = jnp.stack([rates[0], rates[1], weight])

    main, side, edge = zonal_matrices()
    total = span * GROUPS
    bf16 = jnp.bfloat16

    def tile_of(shape):
        return pl.BlockSpec((shape, TILE, cols), lambda i: (0, i, 0))

    once = pl.pallas_call(
        functools.partial(first_kernel, span),
        grid=(tiles,),
        in_specs=[
            whole(pltpu.SMEM),
            pl.BlockSpec((TILE, rows, cols), lambda i: (i, 0, 0)),
            pl.BlockSpec((TILE * HALO, cols), lambda i: (i, 0)),
            pl.BlockSpec((TILE * HALO, cols), lambda i: (i, 0)),
            whole(),
        ],
        out_specs=tile_of(total + 8),
        out_shape=jax.ShapeDtypeStruct((total + 8, snaps, cols), f32),
        scratch_shapes=[pltpu.VMEM((total + 8, TILE, cols), f32)],
        compiler_params=limits,
        cost_estimate=pl.CostEstimate(
            flops=100 * snaps * rows * cols, bytes_accessed=8 * snaps * rows * cols, transcendentals=0
        ),
        name="first_pass",
    )(rates, field, low, high, main)
    split, gram = pl.pallas_call(
        functools.partial(second_kernel, span),
        grid=(tiles,),
        in_specs=[
            whole(pltpu.SMEM),
            tile_of(total + 8),
            tile_of(span),
            tile_of(span // 2),
            tile_of(span // 2),
            whole(),
            whole(),
            whole(),
        ],
        out_specs=[whole(), whole()],
        out_shape=[
            jax.ShapeDtypeStruct((rows + HALO, 2 * snaps, cols), bf16),
            jax.ShapeDtypeStruct((snaps, snaps), f32),
        ],
        scratch_shapes=[
            pltpu.VMEM((total + 8, TILE, cols), f32),
            pltpu.VMEM((GROUPS, 4 * LANES, 2 * LANES), bf16),
            pltpu.VMEM((span + 8, TILE, cols), f32),
            pltpu.VMEM((span * TILE, 2 * LANES), bf16),
            pltpu.VMEM((span * TILE, 2 * LANES), bf16),
            pltpu.VMEM((span, TILE, cols), f32),
            pltpu.VMEM((2, span, 8, cols), f32),
        ],
        compiler_params=limits,
        name="second_pass_and_gram",
    )(rates, once, strip, first, second, main, side, edge)

    gram = sum_all(gram)
    block = 64
    basis, factor = pl.pallas_call(
        functools.partial(basis_kernel, math.sqrt(total_cells)),
        grid=(rows // block,),
        in_specs=[
            pl.BlockSpec((snaps, snaps), lambda i: (0, 0)),
            whole(),
        ],
        out_specs=[
            pl.BlockSpec((snaps, block, cols), lambda i: (0, i, 0)),
            pl.BlockSpec((snaps, snaps), lambda i: (0, 0)),
        ],
        out_shape=[
            jax.ShapeDtypeStruct((snaps, rows, cols), bf16),
            jax.ShapeDtypeStruct((snaps, snaps), f32),
        ],
        scratch_shapes=[
            pltpu.VMEM((2 * snaps, 2 * snaps), bf16),
        ],
        compiler_params=limits,
        name="factor_and_basis",
    )(gram, split)
    return (basis, factor)


def solution(mesh):
    return jax.shard_map(
        shards,
        mesh=mesh,
        in_specs=(P(None, "lat", "lon"), P(), P()),
        out_specs=(P(None, "lat", "lon"), P()),
        check_vma=False,
    )
```

time: 78.5 us -> 74.4 us (0.948)
  waiting for transfers between devices: 21.2 us -> 15.7 us
  starting transfers between devices: 12.1 us -> 15.5 us
  Pallas kernels: 40.6 us -> 38.4 us
    ppermute x2, waiting for transfers between devices: 6.01 us -> 0.01 us  [pair_permutes(): lax.ppermute(values[1], axis, outer)]
    ppermute x5, starting transfers between devices: 1.96 us -> 7.89 us  [sum_all(): lax.ppermute(values, axis, [(i, i ^ step) for i in range(count)])]
    pallas_call x1, Pallas kernels: 10.5 us -> 7.29 us  [shards(): pl.pallas_call(functools.partial(basis_kernel, math.sqrt(total_cells)), g...]
    ppermute x2, waiting for transfers between devices: 0.01 us -> 3.04 us  [pair_permutes(): lax.ppermute(values[0], axis, inner)]
    ppermute x2, starting transfers between devices: 5.81 us -> 3.01 us  [pair_permutes(): lax.ppermute(values[0], axis, inner)]
    ppermute x5, waiting for transfers between devices: 15.2 us -> 12.7 us  [sum_all(): lax.ppermute(values, axis, [(i, i ^ step) for i in range(count)])]
    unnamed x12 -> x14, local copies, waits for them, and re-layouts: 1.98 us -> 3.26 us
    reshape x1 -> x0, local copies, waits for them, and re-layouts: 1.09 us -> none  [shards(): lax.dynamic_slice_in_dim(field, begin, HALO, axis=1)]
  transfers between devices with their start and end apart: 9 -> 9, of which waited for: 6 -> 6; matrix products, arithmetic and copies ran while one was open for 1% -> 1% of each run, Pallas kernels for 15% -> 9%
where the time goes in v2:
time: 74.4 us; the launch traced here: 74.1 us
  Pallas kernels  38.4 us (52%)
  waiting for transfers between devices  15.7 us (21%)
  starting transfers between devices  15.5 us (21%)
  local copies, waits for them, and re-layouts  3.58 us (5%)
  between operations  0.78 us (1%)
    pallas_call x1, Pallas kernels, shards(): pl.pallas_call(functools.partial(second_kernel, span), grid=(tiles,), in_...  15.6 us
    ppermute x5, waiting for transfers between devices, sum_all(): lax.ppermute(values, axis, [(i, i ^ step) for i in range(count)])  12.7 us
    pallas_call x1, Pallas kernels, shards(): pl.pallas_call(functools.partial(strip_kernel, span), grid=(snaps // 8,),...  8.76 us
    ppermute x5, starting transfers between devices, sum_all(): lax.ppermute(values, axis, [(i, i ^ step) for i in range(count)])  7.89 us
    pallas_call x1, Pallas kernels, shards(): pl.pallas_call(functools.partial(basis_kernel, math.sqrt(total_cells)), g...  7.29 us
    pallas_call x1, Pallas kernels, shards(): pl.pallas_call(functools.partial(first_kernel, span), grid=(tiles,), in_s...  6.43 us
    ppermute x2, starting transfers between devices, pair_permutes(): lax.ppermute(values[1], axis, outer)  4.61 us
    unnamed x14, local copies, waits for them, and re-layouts  3.26 us
  transfers between devices with their start and end apart: 9, of which 6 were waited for; matrix products, arithmetic and copies ran while one was open for 1% of the time, Pallas kernels for 9%

profile of v2, /device:TPU:0, one launch (start us, length us, event | category | flops | bytes accessed | tf_op | source)
XLA Modules:
  0.0 74.1 jit_solution(12419011123942672353)
XLA Ops:
  0.7 8.8 %pack_edges.1 = (f32[34,32,128]{2,1,0:T(8,128)}, f32[256,128]{1,0:T(8,128)}, f32[256,128]{1,0:T(8,128)}) custom-call(f32[32,256,128]{2,1,0:T(8,128)} %field_ref.3), custom_call_target="tpu_custom_call" | custom-call | tf_op jit(solution)/shard_map/pack_edges/pallas_call | solution.py:407
  9.4 2.9 %collective-permute-start = (f32[256,128]{1,0:T(8,128)}, f32[256,128]{1,0:T(8,128)S(1)}, u32[]{:S(2)}, u32[]{:S(2)}) collective-permute-start(f32[256,128]{1,0:T(8,128)} %get-tuple-element.10), channel_id=1, source_target_pairs={{0,8},{8,0},{16,24},{24,16},{1,9},{9,1},{17,25},{25,17},{2,10},{10... | collective-permute-start | bytes 393224 | tf_op jit(solution)/shard_map/ppermute | solution.py:378
  12.4 0.7 collective-permute-start.1
  13.0 3.0 %collective-permute-done.low_ref = f32[256,128]{1,0:T(8,128)S(1)} collective-permute-done((f32[256,128]{1,0:T(8,128)}, f32[256,128]{1,0:T(8,128)S(1)}, u32[]{:S(2)}, u32[]{:S(2)}) %collective-permute-start) | collective-permute-done | bytes 131104 | tf_op jit(solution)/shard_map/ppermute | solution.py:378
  16.1 1.1 %copy-done.1 = f32[34,32,128]{2,1,0:T(8,128)S(1)} copy-done((f32[34,32,128]{2,1,0:T(8,128)S(1)}, f32[34,32,128]{2,1,0:T(8,128)}, u32[]{:S(2)}) %copy-start.1) | copy-done | bytes 557080
  17.1 0.3 lon_messages.1
  17.5 4.0 %collective-permute-start.3 = (f32[17,32,128]{2,1,0:T(8,128)S(1)}, f32[17,32,128]{2,1,0:T(8,128)S(1)}, u32[]{:S(2)}, u32[]{:S(2)}) collective-permute-start(f32[17,32,128]{2,1,0:T(8,128)S(1)} %get-tuple-element.15), channel_id=1, source_target_pairs={{1,2},{2,1},{3,4},{4,3},{5,6},{6,5},{7,0},{0,7},{9,10},{10,9},{11,... | collective-permute-start | bytes 835592 | tf_op jit(solution)/shard_map/ppermute | solution.py:378
  21.5 0.1 pad_maximum_fusion.1
  21.6 0.1 concatenate.10
  21.7 0.1 dynamic_slice.7
  21.8 0.1 concatenate.9
  21.8 0.1 dynamic_slice.6
  22.0 2.2 %copy-done = f32[32,256,128]{2,1,0:T(8,128)S(1)} copy-done((f32[32,256,128]{2,1,0:T(8,128)S(1)}, f32[32,256,128]{2,1,0:T(8,128)}, u32[]{:S(2)}) %copy-start) | copy-done | bytes 4194328
  24.1 6.4 %first_pass.1.once_ref = f32[280,32,128]{2,1,0:T(8,128)S(1)} custom-call(f32[3,272]{1,0:T(4,128)S(1)} %pad_maximum_fusion.rates_ref, f32[32,256,128]{2,1,0:T(8,128)S(1)} %copy-done, f32[256,128]{1,0:T(8,128)S(1)} %collective-permute-done.low_ref, f32[256,128]{1,0:T(8,128)S(1)} %collective-permute-done.1.high_ref, bf16[256,256]{1,0:T(8,128)(2,1)S(1)} %copy-done.2), custom_call_target="tpu_custom_call" | custom-call | flops 104857600 | bytes 8388608 | tf_op jit(solution)/shard_map/first_pass/pallas_call | solution.py:449
  30.6 15.6 %second_pass_and_gram.1 = (bf16[264,64,128]{2,1,0:T(8,128)(2,1)S(1)}, f32[32,32]{1,0:T(8,128)S(1)}) custom-call(f32[3,272]{1,0:T(4,128)S(1)} %pad_maximum_fusion.rates_ref, f32[280,32,128]{2,1,0:T(8,128)S(1)} %first_pass.1.once_ref, f32[34,32,128]{2,1,0:T(8,128)S(1)} %get-tuple-element.13.strip_ref, f32[17,32,128]{2,1,0:T(8,128)S(1)} %collective-permute-done.2.first_ref, ...), custom_call_target="tpu_custom_call" | custom-call | tf_op jit(solution)/shard_map/second_pass_and_gram/pallas_call | solution.py:468
  46.3 1.2 %collective-permute-done.4 = f32[32,32]{1,0:T(8,128)S(1)} collective-permute-done((f32[32,32]{1,0:T(8,128)S(1)}, f32[32,32]{1,0:T(8,128)S(1)}, u32[]{:S(2)}, u32[]{:S(2)}) %collective-permute-start.4) | collective-permute-done | bytes 4128 | tf_op jit(solution)/shard_map/ppermute | solution.py:386
  47.5 3.7 %collective-permute-done.5 = f32[32,32]{1,0:T(8,128)S(1)} collective-permute-done((f32[32,32]{1,0:T(8,128)S(1)}, f32[32,32]{1,0:T(8,128)S(1)}, u32[]{:S(2)}, u32[]{:S(2)}) %collective-permute-start.5) | collective-permute-done | bytes 4128 | tf_op jit(solution)/shard_map/ppermute | solution.py:386
  51.2 0.3 collective-permute-start.6
  51.5 4.3 %collective-permute-done.6 = f32[32,32]{1,0:T(8,128)S(1)} collective-permute-done((f32[32,32]{1,0:T(8,128)S(1)}, f32[32,32]{1,0:T(8,128)S(1)}, u32[]{:S(2)}, u32[]{:S(2)}) %collective-permute-start.6) | collective-permute-done | bytes 4128 | tf_op jit(solution)/shard_map/ppermute | solution.py:386
  55.9 5.3 %collective-permute-start.7 = (f32[32,32]{1,0:T(8,128)S(1)}, f32[32,32]{1,0:T(8,128)S(1)}, u32[]{:S(2)}, u32[]{:S(2)}) collective-permute-start(f32[32,32]{1,0:T(8,128)S(1)} %add.46), channel_id=1, source_target_pairs={{0,8},{8,0},{16,24},{24,16},{1,9},{9,1},{17,25},{25,17},{2,10},{10... | collective-permute-start | bytes 12296 | tf_op jit(solution)/shard_map/ppermute | solution.py:386
  61.1 1.7 %collective-permute-done.7 = f32[32,32]{1,0:T(8,128)S(1)} collective-permute-done((f32[32,32]{1,0:T(8,128)S(1)}, f32[32,32]{1,0:T(8,128)S(1)}, u32[]{:S(2)}, u32[]{:S(2)}) %collective-permute-start.7) | collective-permute-done | bytes 4128 | tf_op jit(solution)/shard_map/ppermute | solution.py:386
  62.8 2.3 %collective-permute-start.8 = (f32[32,32]{1,0:T(8,128)S(1)}, f32[32,32]{1,0:T(8,128)S(1)}, u32[]{:S(2)}, u32[]{:S(2)}) collective-permute-start(f32[32,32]{1,0:T(8,128)S(1)} %add.47), channel_id=1, source_target_pairs={{0,16},{8,24},{16,0},{24,8},{1,17},{9,25},{17,1},{25,9},{2,18},{10... | collective-permute-start | bytes 12296 | tf_op jit(solution)/shard_map/ppermute | solution.py:386
  65.1 1.7 %collective-permute-done.8 = f32[32,32]{1,0:T(8,128)S(1)} collective-permute-done((f32[32,32]{1,0:T(8,128)S(1)}, f32[32,32]{1,0:T(8,128)S(1)}, u32[]{:S(2)}, u32[]{:S(2)}) %collective-permute-start.8) | collective-permute-done | bytes 4128 | tf_op jit(solution)/shard_map/ppermute | solution.py:386
  66.8 7.3 %factor_and_basis.1 = (bf16[32,256,128]{2,1,0:T(8,128)(2,1)}, f32[32,32]{1,0:T(8,128)}) custom-call(f32[32,32]{1,0:T(8,128)S(1)} %add.48.gram_ref, bf16[264,64,128]{2,1,0:T(8,128)(2,1)S(1)} %get-tuple-element.17.split_ref), custom_call_target="tpu_custom_call" | custom-call | tf_op jit(solution)/shard_map/factor_and_basis/pallas_call | solution.py:501
  (29 shorter events, 0.3 us)
Async XLA Ops:
  0.6 21.3 %copy-start.2 = (bf16[256,256]{1,0:T(8,128)(2,1)S(1)}, bf16[256,256]{1,0:T(8,128)(2,1)}, u32[]{:S(2)}) copy-start(bf16[256,256]{1,0:T(8,128)(2,1)} %constant.27.clone.main_ref) | copy-start | bytes 393220
  0.6 21.0 %copy-start.5 = (f32[1024]{0:T(1024)S(1)}, f32[1024]{0:T(1024)}, u32[]{:S(2)}) copy-start(f32[1024]{0:T(1024)} %param.8) | copy-start | bytes 12292
  0.7 21.1 %copy-start.6 = (f32[1024]{0:T(1024)S(1)}, f32[1024]{0:T(1024)}, u32[]{:S(2)}) copy-start(f32[1024]{0:T(1024)} %param.7) | copy-start | bytes 12292
  9.4 6.6 %collective-permute-start = (f32[256,128]{1,0:T(8,128)}, f32[256,128]{1,0:T(8,128)S(1)}, u32[]{:S(2)}, u32[]{:S(2)}) collective-permute-start(f32[256,128]{1,0:T(8,128)} %get-tuple-element.10), channel_id=1, source_target_pairs={{0,8},{8,0},{16,24},{24,16},{1,9},{9,1},{17,25},{25,17},{2,10},{10... | collective-permute-start | bytes 393224 | tf_op jit(solution)/shard_map/ppermute | solution.py:378
  12.4 3.7 %collective-permute-start.1 = (f32[256,128]{1,0:T(8,128)}, f32[256,128]{1,0:T(8,128)S(1)}, u32[]{:S(2)}, u32[]{:S(2)}) collective-permute-start(f32[256,128]{1,0:T(8,128)} %get-tuple-element.11), channel_id=1, source_target_pairs={{8,16},{16,8},{9,17},{17,9},{10,18},{18,10},{11,19},{19,11},{12,20... | collective-permute-start | bytes 393224 | tf_op jit(solution)/shard_map/ppermute | solution.py:378
  16.1 1.1 %copy-start.1 = (f32[34,32,128]{2,1,0:T(8,128)S(1)}, f32[34,32,128]{2,1,0:T(8,128)}, u32[]{:S(2)}) copy-start(f32[34,32,128]{2,1,0:T(8,128)} %get-tuple-element.12.strip_ref) | copy-start | bytes 1671172
  17.4 13.2 %collective-permute-start.2 = (f32[17,32,128]{2,1,0:T(8,128)S(1)}, f32[17,32,128]{2,1,0:T(8,128)S(1)}, u32[]{:S(2)}, u32[]{:S(2)}) collective-permute-start(f32[17,32,128]{2,1,0:T(8,128)S(1)} %get-tuple-element.14), channel_id=1, source_target_pairs={{0,1},{1,0},{2,3},{3,2},{4,5},{5,4},{6,7},{7,6},{8,9},{9,8},{10,11... | collective-permute-start | bytes 835592 | tf_op jit(solution)/shard_map/ppermute | solution.py:378
  17.5 13.1 %collective-permute-start.3 = (f32[17,32,128]{2,1,0:T(8,128)S(1)}, f32[17,32,128]{2,1,0:T(8,128)S(1)}, u32[]{:S(2)}, u32[]{:S(2)}) collective-permute-start(f32[17,32,128]{2,1,0:T(8,128)S(1)} %get-tuple-element.15), channel_id=1, source_target_pairs={{1,2},{2,1},{3,4},{4,3},{5,6},{6,5},{7,0},{0,7},{9,10},{10,9},{11,... | collective-permute-start | bytes 835592 | tf_op jit(solution)/shard_map/ppermute | solution.py:378
  22.0 2.2 %copy-start = (f32[32,256,128]{2,1,0:T(8,128)S(1)}, f32[32,256,128]{2,1,0:T(8,128)}, u32[]{:S(2)}) copy-start(f32[32,256,128]{2,1,0:T(8,128)} %field_ref.3) | copy-start | bytes 12582916
  24.1 6.5 %copy-start.3 = (bf16[512,256]{1,0:T(8,128)(2,1)S(1)}, bf16[512,256]{1,0:T(8,128)(2,1)}, u32[]{:S(2)}) copy-start(bf16[512,256]{1,0:T(8,128)(2,1)} %constant.29.clone.edge_ref) | copy-start | bytes 786436
  24.1 6.5 %copy-start.4 = (bf16[16,256]{1,0:T(8,128)(2,1)S(1)}, bf16[16,256]{1,0:T(8,128)(2,1)}, u32[]{:S(2)}) copy-start(bf16[16,256]{1,0:T(8,128)(2,1)} %constant.28.clone.side_ref) | copy-start | bytes 24580
  46.2 1.2 %collective-permute-start.4 = (f32[32,32]{1,0:T(8,128)S(1)}, f32[32,32]{1,0:T(8,128)S(1)}, u32[]{:S(2)}, u32[]{:S(2)}) collective-permute-start(f32[32,32]{1,0:T(8,128)S(1)} %get-tuple-element.16), channel_id=1, source_target_pairs={{0,1},{1,0},{2,3},{3,2},{4,5},{5,4},{6,7},{7,6},{8,9},{9,8},{10,11... | collective-permute-start | bytes 12296 | tf_op jit(solution)/shard_map/ppermute | solution.py:386
  47.5 3.7 %collective-permute-start.5 = (f32[32,32]{1,0:T(8,128)S(1)}, f32[32,32]{1,0:T(8,128)S(1)}, u32[]{:S(2)}, u32[]{:S(2)}) collective-permute-start(f32[32,32]{1,0:T(8,128)S(1)} %add.44), channel_id=1, source_target_pairs={{0,2},{1,3},{2,0},{3,1},{4,6},{5,7},{6,4},{7,5},{8,10},{9,11},{10,... | collective-permute-start | bytes 12296 | tf_op jit(solution)/shard_map/ppermute | solution.py:386
  51.2 4.6 %collective-permute-start.6 = (f32[32,32]{1,0:T(8,128)S(1)}, f32[32,32]{1,0:T(8,128)S(1)}, u32[]{:S(2)}, u32[]{:S(2)}) collective-permute-start(f32[32,32]{1,0:T(8,128)S(1)} %add.45), channel_id=1, source_target_pairs={{0,4},{1,5},{2,6},{3,7},{4,0},{5,1},{6,2},{7,3},{8,12},{9,13},{10,... | collective-permute-start | bytes 12296 | tf_op jit(solution)/shard_map/ppermute | solution.py:386
  55.9 7.0 %collective-permute-start.7 = (f32[32,32]{1,0:T(8,128)S(1)}, f32[32,32]{1,0:T(8,128)S(1)}, u32[]{:S(2)}, u32[]{:S(2)}) collective-permute-start(f32[32,32]{1,0:T(8,128)S(1)} %add.46), channel_id=1, source_target_pairs={{0,8},{8,0},{16,24},{24,16},{1,9},{9,1},{17,25},{25,17},{2,10},{10... | collective-permute-start | bytes 12296 | tf_op jit(solution)/shard_map/ppermute | solution.py:386
  62.8 4.0 %collective-permute-start.8 = (f32[32,32]{1,0:T(8,128)S(1)}, f32[32,32]{1,0:T(8,128)S(1)}, u32[]{:S(2)}, u32[]{:S(2)}) collective-permute-start(f32[32,32]{1,0:T(8,128)S(1)} %add.47), channel_id=1, source_target_pairs={{0,16},{8,24},{16,0},{24,8},{1,17},{9,25},{17,1},{25,9},{2,18},{10... | collective-permute-start | bytes 12296 | tf_op jit(solution)/shard_map/ppermute | solution.py:386

commit v3 on v2

v3 whole, which is shorter than its diff:
```python
import functools
import math

import jax
import jax.numpy as jnp
import numpy as np
from jax import lax
from jax.experimental import pallas as pl
from jax.experimental.pallas import tpu as pltpu
from jax.sharding import PartitionSpec as P

stencil_weights = (-205.0 / 72.0, 8.0 / 5.0, -1.0 / 5.0, 8.0 / 315.0, -1.0 / 560.0)

HALO = 8
STRIP = 2 * HALO
LANES = 128
GROUPS = LANES // STRIP
TILE = 16
VMEM_BYTES = 24 * 1024 * 1024


def area_weight(first_row, row_count, total_rows):
    row_index = (jnp.arange(row_count) + first_row).astype(jnp.float32)
    latitude = (-90.0 + (row_index + 0.5) * (180.0 / total_rows)) * (math.pi / 180.0)
    return jnp.sqrt(jnp.cos(latitude))


def hi_lo(values):
    hi = values.astype(jnp.bfloat16)
    lo = (values - hi.astype(jnp.float32)).astype(jnp.bfloat16)
    return hi, lo


def band(in_cols, out_cols):
    offset = np.abs(np.asarray(in_cols)[:, None] - np.asarray(out_cols)[None, :])
    table = np.asarray(stencil_weights, np.float32)
    return np.where(offset <= 4, table[np.minimum(offset, 4)], np.float32(0.0)).astype(np.float32)


def two_terms(matrix):
    hi = matrix.astype(jnp.bfloat16)
    lo = (matrix - hi.astype(np.float32)).astype(jnp.bfloat16)
    return np.concatenate([hi, lo], axis=1)


def block_diagonal(matrix):
    return np.kron(np.eye(GROUPS, dtype=np.float32), matrix)


def zonal_matrices():
    own = np.arange(LANES)
    outer = np.concatenate([np.arange(-HALO, 0), LANES + np.arange(HALO)])
    inner = np.concatenate([np.arange(LANES - HALO, LANES), np.arange(HALO)])
    main = two_terms(band(own, own))
    near = band(outer, outer)
    far = band(inner, outer)
    inward = band(outer, inner)
    near[:HALO, HALO:] = near[HALO:, :HALO] = 0.0
    near, far, inward = [two_terms(block_diagonal(part)) for part in (near, far, inward)]
    edge = np.concatenate([near, near, far, far], axis=0)
    inward = np.concatenate([inward, inward], axis=0)
    inward_only = np.concatenate([inward, np.zeros_like(inward)], axis=0)
    return np.concatenate([main, main], axis=0), np.concatenate([edge, inward_only], axis=1), inward


def strip_kernel(span, field_ref, ext_ref, strip_ref, first_ref, second_ref):
    snaps, rows, _ = field_ref.shape
    lat_even = lax.axis_index("lat") % 2 == 0
    north = field_ref[:, :HALO].reshape(snaps * HALO, LANES)
    south = field_ref[:, rows - HALO :].reshape(snaps * HALO, LANES)
    first_ref[...] = jnp.where(lat_even, south, north)
    second_ref[...] = jnp.where(lat_even, north, south)

    def turn(at, carry):
        begin = pl.multiple_of(at * 8, 8)
        for tile in range(0, snaps, 8):
            ext_ref[pl.ds(4 + HALO + begin, 8), tile : tile + 8] = jnp.swapaxes(
                field_ref[tile : tile + 8, pl.ds(begin, 8), :], 0, 1
            )
        return carry

    lax.fori_loop(0, rows // 8, turn, 0, unroll=2)
    ends = jnp.zeros((4 + HALO, snaps, LANES), jnp.float32)
    ext_ref[: 4 + HALO] = ends
    ext_ref[4 + HALO + rows :] = ends
    group_of = lax.broadcasted_iota(jnp.int32, (snaps, LANES), 1) // STRIP

    def pack(at, carry):
        packed = jnp.zeros((snaps, LANES), jnp.float32)
        for group in range(GROUPS):
            values = ext_ref[4 + group * span + at]
            moved = pltpu.roll(values, (HALO + STRIP * group) % LANES, 1)
            packed = jnp.where(group_of == group, moved, packed)
        strip_ref[at] = packed
        return carry

    lax.fori_loop(0, span, pack, 0, unroll=2)


def message_kernel(
    span, ext_in_ref, strip_ref, low_ref, high_ref, ext_ref, full_ref, first_ref, second_ref
):
    snaps = strip_ref.shape[1]
    half = span // 2
    end = ext_ref.shape[0] - 4 - HALO
    lane = lax.broadcasted_iota(jnp.int32, (snaps, LANES), 1)
    lat_even = lax.axis_index("lat") % 2 == 0
    lon_even = lax.axis_index("lon") % 2 == 0
    full_ref[...] = strip_ref[...]
    for tile in range(0, snaps, 8):
        part = slice(tile * HALO, (tile + 8) * HALO)
        first = jnp.swapaxes(low_ref[part].reshape(8, HALO, LANES), 0, 1)
        second = jnp.swapaxes(high_ref[part].reshape(8, HALO, LANES), 0, 1)
        ext_ref[4 : 4 + HALO, tile : tile + 8] = jnp.where(lat_even, second, first)
        ext_ref[end : end + HALO, tile : tile + 8] = jnp.where(lat_even, first, second)
    for at in range(HALO):
        north, south = ext_ref[4 + at], ext_ref[end + at]
        full_ref[at] = jnp.where(lane < STRIP, pltpu.roll(north, HALO, 1), full_ref[at])
        last = span - HALO + at
        full_ref[last] = jnp.where(
            lane >= LANES - STRIP, pltpu.roll(south, LANES - HALO, 1), full_ref[last]
        )
    left = lane % STRIP < HALO
    for at in range(half):
        upper, lower = full_ref[at], full_ref[at + half]
        eastward = jnp.where(left, upper, pltpu.roll(lower, HALO, 1))
        westward = jnp.where(left, pltpu.roll(lower, LANES - HALO, 1), upper)
        first_ref[at] = jnp.where(lon_even, eastward, westward)
        second_ref[at] = jnp.where(lon_even, westward, eastward)


def stencil_row(center, pairs, zonal, zonal_rate, merid_rate):
    merid = stencil_weights[1] * pairs[0]
    for offset in range(2, 5):
        merid = merid + stencil_weights[offset] * pairs[offset - 1]
    scale = 1.0 + stencil_weights[0] * merid_rate
    return scale * center + merid_rate * merid + zonal_rate * zonal


def zonal_terms(parts, weights):
    product = jnp.dot(
        jnp.concatenate(parts, axis=1), weights, preferred_element_type=jnp.float32
    )
    return product[:, :LANES] + product[:, LANES:]


def stencil_rows(load, begin, span, part, rates_ref, store):
    loaded = {}

    def row(at):
        if at not in loaded:
            loaded[at] = load(begin + at)
        return loaded[at]

    for at in range(span):
        here = at + 4
        pairs = [row(here + offset) + row(here - offset) for offset in range(1, 5)]
        store(
            at,
            stencil_row(
                row(here), pairs, part[at], rates_ref[0, begin + at], rates_ref[1, begin + at]
            ),
        )


def first_kernel(span, rates_ref, ext_ref, main_ref, once_ref):
    snaps = ext_ref.shape[1]
    total = span * GROUPS
    ends = jnp.zeros((4, snaps, LANES), jnp.float32)
    once_ref[:4] = ends
    once_ref[total + 4 :] = ends
    for tile in range(0, snaps, TILE):
        snap = slice(tile, tile + TILE)

        def body(group, carry):
            begin = group * span
            center = ext_ref[pl.ds(4 + begin, span), snap].reshape(span * TILE, LANES)
            part = zonal_terms(hi_lo(center), main_ref[...]).reshape(span, TILE, LANES)

            def load(at):
                return ext_ref[at, snap]

            def store(at, value):
                once_ref[4 + begin + at, snap] = value

            stencil_rows(load, begin, span, part, rates_ref, store)
            return carry

        lax.fori_loop(0, GROUPS, body, 0)


def second_kernel(
    span,
    rates_ref,
    once_ref,
    strip_ref,
    first_ref,
    second_ref,
    main_ref,
    edge_ref,
    inward_ref,
    split_ref,
    gram_ref,
    full_ref,
    outer_ref,
    zonal_ref,
    add_ref,
    strip_rates_ref,
):
    both = split_ref.shape[1]
    rows = split_ref.shape[0] - HALO
    snaps = both // 2
    half = span // 2
    total = span * GROUPS
    lon_even = lax.axis_index("lon") % 2 == 0
    lane = lax.broadcasted_iota(jnp.int32, (TILE, LANES), 1)
    left = lane % STRIP < HALO
    rim = (lane < HALO) | (lane >= LANES - HALO)
    group_of = lax.broadcasted_iota(jnp.int32, (8, LANES), 1) // STRIP
    for at in range(span):
        for kind in range(3):
            value = jnp.zeros((8, LANES), jnp.float32)
            for group in range(GROUPS):
                value = jnp.where(group_of == group, rates_ref[kind, group * span + at], value)
            strip_rates_ref[kind, at] = value

    def strip_rate(kind, at):
        return jnp.concatenate([strip_rates_ref[kind, at]] * (TILE // 8), axis=0)

    for tile in range(0, snaps, TILE):
        snap = slice(tile, tile + TILE)
        for at in range(half):
            first, second = first_ref[at, snap], second_ref[at, snap]
            west = jnp.where(lon_even, second, first)
            east = jnp.where(lon_even, first, second)
            outer_ref[4 + at] = jnp.where(left, west, east)
            outer_ref[4 + half + at] = jnp.where(
                left, pltpu.roll(west, LANES - HALO, 1), pltpu.roll(east, HALO, 1)
            )
        for at in range(4):
            outer_ref[at] = pltpu.roll(outer_ref[span + at], STRIP, 1)
            outer_ref[span + 4 + at] = pltpu.roll(outer_ref[4 + at], LANES - STRIP, 1)
        hi, lo = hi_lo(outer_ref[4 : 4 + span].reshape(span * TILE, LANES))
        own_hi, own_lo = hi_lo(strip_ref[:, snap].reshape(span * TILE, LANES))
        product = jnp.dot(
            jnp.concatenate([hi, lo, own_hi, own_lo], axis=1),
            edge_ref[...],
            preferred_element_type=jnp.float32,
        ).reshape(span, TILE, 4 * LANES)
        for at in range(span):
            zonal = product[at, :, :LANES] + product[at, :, LANES : 2 * LANES]
            pairs = [
                outer_ref[4 + at + offset] + outer_ref[4 + at - offset] for offset in range(1, 5)
            ]
            zonal_rate = strip_rate(0, at)
            zonal_ref[at] = stencil_row(
                outer_ref[4 + at], pairs, zonal, zonal_rate, strip_rate(1, at)
            )
            add_ref[0, at] = zonal_rate * (
                product[at, :, 2 * LANES : 3 * LANES] + product[at, :, 3 * LANES :]
            )
        inner = zonal_ref[...].reshape(span * TILE, LANES)
        product = zonal_terms(hi_lo(inner), inward_ref[...]).reshape(span, TILE, LANES)
        for at in range(span):
            add_ref[1, at] = (strip_rate(2, at) * strip_rate(0, at)) * product[at]

        def added(kind, at, group):
            moved = pltpu.roll(add_ref[kind, at], LANES - HALO - STRIP * group, 1)
            return jnp.where(rim, moved, 0.0)

        def complete(group, carry):
            begin = group * span
            for at in range(span):
                here = 4 + begin + at
                full_ref[here] = once_ref[here, snap] + added(0, at, group)
            return carry

        lax.fori_loop(0, GROUPS, complete, 0)
        for at in range(4):
            full_ref[at] = once_ref[at, snap]
            full_ref[total + 4 + at] = once_ref[total + 4 + at, snap]

        def second_pass(group, carry):
            begin = group * span
            center = full_ref[pl.ds(4 + begin, span)].reshape(span * TILE, LANES)
            part = zonal_terms(hi_lo(center), main_ref[...]).reshape(span, TILE, LANES)

            def load(at):
                return full_ref[at]

            def store(at, value):
                hi, lo = hi_lo(rates_ref[2, begin + at] * value + added(1, at, group))
                row = jnp.maximum(begin + at - HALO, 0)
                split_ref[row, snap] = hi
                split_ref[row, snaps + tile : snaps + tile + TILE] = lo

            stencil_rows(load, begin, span, part, rates_ref, store)
            return carry

        lax.fori_loop(0, GROUPS, second_pass, 0)

    def square(at, total):
        two = jnp.concatenate([split_ref[2 * at], split_ref[2 * at + 1]], axis=1)
        return total + lax.dot_general(
            two, two, (((1,), (1,)), ((), ())), preferred_element_type=jnp.float32
        )

    grams = lax.fori_loop(0, rows // 2, square, jnp.zeros((both, both), jnp.float32), unroll=8)
    gram = (
        grams[:snaps, :snaps]
        + grams[snaps:, snaps:]
        + (grams[:snaps, snaps:] + grams[snaps:, :snaps])
    )
    gram_ref[...] = jnp.concatenate(
        [gram[at : at + 8] for at in range(0, snaps, 8)], axis=1
    )


def basis_kernel(root_count, gram_ref, split_ref, basis_ref, factor_ref, left_ref):
    snaps = basis_ref.shape[0]

    @pl.when(pl.program_id(0) == 0)
    def _():
        row = lax.broadcasted_iota(jnp.int32, (snaps, 2 * snaps), 0)
        col = lax.broadcasted_iota(jnp.int32, (snaps, 2 * snaps), 1)
        packed = jnp.sum(gram_ref[...], axis=0)
        gram = jnp.concatenate(
            [packed[:, at : at + snaps] for at in range(0, packed.shape[1], snaps)], axis=0
        )
        work = jnp.concatenate([gram, jnp.zeros((snaps, snaps), jnp.float32)], axis=1)
        work = jnp.where(col == row + snaps, 1.0, work)
        for step in range(snaps):
            pivot_row = work[step : step + 1, :]
            ratio = work[:, step : step + 1] / work[step : step + 1, step : step + 1]
            work = work - jnp.where(row > step, ratio, 0.0) * pivot_row
        diagonal = jnp.sum(jnp.where(row == col, work, 0.0), axis=1, keepdims=True)
        work = work * lax.rsqrt(diagonal)
        upper = jnp.where(col >= row, work, 0.0)
        factor_ref[...] = upper[:, :snaps] / root_count
        hi, lo = hi_lo(work[:, snaps:] * root_count)
        left_ref[:snaps] = jnp.concatenate([hi, hi], axis=1)
        left_ref[snaps:] = jnp.concatenate([lo, jnp.zeros_like(lo)], axis=1)

    left = left_ref[...]
    start = pl.program_id(0) * basis_ref.shape[1]

    def body(at, carry):
        begin = pl.multiple_of(at * 16, 16)
        values = []
        for pair in range(8):
            row = start + begin + 2 * pair
            two = jnp.concatenate([split_ref[row], split_ref[row + 1]], axis=1)
            product = jnp.dot(left, two, preferred_element_type=jnp.float32)
            value = product[:snaps] + product[snaps:]
            values += [value[:, :LANES], value[:, LANES:]]
        turned = jnp.swapaxes(jnp.stack(values, axis=0), 0, 1)
        basis_ref[:, pl.ds(begin, 16), :] = turned.astype(jnp.bfloat16)
        return carry

    lax.fori_loop(0, basis_ref.shape[1] // 16, body, 0)


def pair_permutes(values, axis, periodic):
    count = lax.axis_size(axis)
    inner = [(i, i ^ 1) for i in range(count)]
    outer = []
    for i in range(1, count, 2):
        if periodic or i + 1 < count:
            outer += [(i, (i + 1) % count), ((i + 1) % count, i)]
    return lax.ppermute(values[0], axis, inner), lax.ppermute(values[1], axis, outer)


def gather_all(values):
    axes = ("lat", "lon")
    count = lax.axis_size(axes)
    return lax.all_to_all(jnp.broadcast_to(values, (count,) + values.shape), axes, 0, 0)


def whole(memory_space=pltpu.VMEM):
    return pl.BlockSpec(memory_space=memory_space)


def shards(field, lon_rate, lat_rate):
    snaps, rows, cols = field.shape
    row_start = lax.axis_index("lat") * rows
    total_rows = rows * lax.axis_size("lat")
    total_cells = total_rows * cols * lax.axis_size("lon")
    span = (rows + 2 * HALO) // GROUPS
    f32 = jnp.float32
    limits = pltpu.CompilerParams(vmem_limit_bytes=VMEM_BYTES)

    total = span * GROUPS
    ext = jax.ShapeDtypeStruct((total + 8, snaps, cols), f32)
    strip = jax.ShapeDtypeStruct((span, snaps, cols), f32)
    half = jax.ShapeDtypeStruct((span // 2, snaps, cols), f32)
    edge_rows = jax.ShapeDtypeStruct((snaps * HALO, cols), f32)
    turned, packed, first, second = pl.pallas_call(
        functools.partial(strip_kernel, span),
        in_specs=[whole()],
        out_specs=[whole()] * 4,
        out_shape=[ext, strip, edge_rows, edge_rows],
        compiler_params=limits,
        name="turn_and_pack",
    )(field)
    low, high = pair_permutes([first, second], "lat", False)
    turned, packed, first, second = pl.pallas_call(
        functools.partial(message_kernel, span),
        in_specs=[whole()] * 4,
        out_specs=[whole()] * 4,
        out_shape=[ext, strip, half, half],
        input_output_aliases={0: 0},
        compiler_params=limits,
        name="lon_messages",
    )(turned, packed, low, high)
    first, second = pair_permutes([first, second], "lon", True)

    pad = jnp.zeros((HALO,), f32)
    rates = [
        lax.dynamic_slice_in_dim(jnp.concatenate([pad, rate, pad]), row_start, rows + 2 * HALO)
        for rate in (lon_rate, lat_rate)
    ]
    weight = jnp.concatenate([pad, area_weight(row_start, rows, total_rows), pad])
    rates = jnp.stack([rates[0], rates[1], weight])

    main, edge, inward = zonal_matrices()
    bf16 = jnp.bfloat16
    once = pl.pallas_call(
        functools.partial(first_kernel, span),
        in_specs=[whole(pltpu.SMEM), whole(), whole()],
        out_specs=whole(),
        out_shape=ext,
        compiler_params=limits,
        cost_estimate=pl.CostEstimate(
            flops=100 * snaps * rows * cols, bytes_accessed=8 * snaps * rows * cols, transcendentals=0
        ),
        name="first_pass",
    )(rates, turned, main)
    split, gram = pl.pallas_call(
        functools.partial(second_kernel, span),
        in_specs=[whole(pltpu.SMEM)] + [whole()] * 7,
        out_specs=[whole(), whole()],
        out_shape=[
            jax.ShapeDtypeStruct((rows + HALO, 2 * snaps, cols), bf16),
            jax.ShapeDtypeStruct((8, snaps // 8 * snaps), f32),
        ],
        scratch_shapes=[
            pltpu.VMEM((total + 8, TILE, cols), f32),
            pltpu.VMEM((span + 8, TILE, cols), f32),
            pltpu.VMEM((span, TILE, cols), f32),
            pltpu.VMEM((2, span, TILE, cols), f32),
            pltpu.VMEM((3, span, 8, cols), f32),
        ],
        compiler_params=limits,
        name="second_pass_and_gram",
    )(rates, once, packed, first, second, main, edge, inward)

    grams = gather_all(gram)
    block = 64
    basis, factor = pl.pallas_call(
        functools.partial(basis_kernel, math.sqrt(total_cells)),
        grid=(rows // block,),
        in_specs=[
            whole(),
            whole(),
        ],
        out_specs=[
            pl.BlockSpec((snaps, block, cols), lambda i: (0, i, 0)),
            pl.BlockSpec((snaps, snaps), lambda i: (0, 0)),
        ],
        out_shape=[
            jax.ShapeDtypeStruct((snaps, rows, cols), bf16),
            jax.ShapeDtypeStruct((snaps, snaps), f32),
        ],
        scratch_shapes=[
            pltpu.VMEM((2 * snaps, 2 * snaps), bf16),
        ],
        compiler_params=limits,
        name="factor_and_basis",
    )(grams, split)
    return (basis, factor)


def solution(mesh):
    return jax.shard_map(
        shards,
        mesh=mesh,
        in_specs=(P(None, "lat", "lon"), P(), P()),
        out_specs=(P(None, "lat", "lon"), P()),
        check_vma=False,
    )
```

time: 74.4 us -> 66.4 us (0.89)
  blocking collectives: 0 us -> 14.2 us
  waiting for transfers between devices: 15.7 us -> 2.83 us
  Pallas kernels: 38.4 us -> 29.3 us
  starting transfers between devices: 15.5 us -> 7.56 us
  local copies, waits for them, and re-layouts: 3.58 us -> 11.3 us
    all_to_all x0 -> x1, blocking collectives: none -> 14.2 us  [gather_all(): lax.all_to_all(jnp.broadcast_to(values, (count,) + values.shape), axes, 0...]
    ppermute x5 -> x0, waiting for transfers between devices: 12.7 us -> none  [sum_all(): lax.ppermute(values, axis, [(i, i ^ step) for i in range(count)])]
    pallas_call x3, Pallas kernels: 30.8 us -> 21.7 us  [the longest x1 13.3 us: shards(): pl.pallas_call(functools.partial(second_kernel, span), in_specs=[whole(pl...]
    ppermute x5 -> x0, starting transfers between devices: 7.89 us -> none  [sum_all(): lax.ppermute(values, axis, [(i, i ^ step) for i in range(count)])]
    unnamed x14 -> x20, local copies, waits for them, and re-layouts: 3.26 us -> 11 us
  transfers between devices with their start and end apart: 9 -> 4, of which waited for: 6 -> 1; matrix products, arithmetic and copies ran while one was open for 1% -> 1% of each run, Pallas kernels for 9% -> 8%
where the time goes in v3:
time: 66.4 us; the launch traced here: 66.1 us
  Pallas kernels  29.3 us (44%)
  blocking collectives  14.2 us (21%)
  local copies, waits for them, and re-layouts  11.3 us (17%)
  starting transfers between devices  7.56 us (11%)
  waiting for transfers between devices  2.83 us (4%)
  between operations  0.78 us (1%)
    all_to_all x1, blocking collectives, gather_all(): lax.all_to_all(jnp.broadcast_to(values, (count,) + values.shape), axes, 0...  14.2 us
    pallas_call x1, Pallas kernels, shards(): pl.pallas_call(functools.partial(second_kernel, span), in_specs=[whole(pl...  13.3 us
    unnamed x20, local copies, waits for them, and re-layouts  11 us
    pallas_call x1, Pallas kernels, shards(): pl.pallas_call(functools.partial(basis_kernel, math.sqrt(total_cells)), g...  7.37 us
    pallas_call x1, Pallas kernels, shards(): pl.pallas_call(functools.partial(first_kernel, span), in_specs=[whole(plt...  5.12 us
    ppermute x2, starting transfers between devices, pair_permutes(): lax.ppermute(values[1], axis, outer)  4.62 us
    pallas_call x1, Pallas kernels, shards(): pl.pallas_call(functools.partial(strip_kernel, span), in_specs=[whole()],...  3.2 us
    ppermute x2, starting transfers between devices, pair_permutes(): lax.ppermute(values[0], axis, inner)  2.94 us
  transfers between devices with their start and end apart: 4, of which 1 were waited for; matrix products, arithmetic and copies ran while one was open for 1% of the time, Pallas kernels for 8%

profile of v3, /device:TPU:0, one launch (start us, length us, event | category | flops | bytes accessed | tf_op | source)
XLA Modules:
  0.0 66.1 jit_solution(8800456725801439083)
XLA Ops:
  0.6 2.2 %copy-done.4 = f32[32,256,128]{2,1,0:T(8,128)S(1)} copy-done((f32[32,256,128]{2,1,0:T(8,128)S(1)}, f32[32,256,128]{2,1,0:T(8,128)}, u32[]{:S(2)}) %copy-start.4) | copy-done | bytes 4194328
  2.8 3.2 %turn_and_pack.1 = (f32[280,32,128]{2,1,0:T(8,128)S(1)}, f32[34,32,128]{2,1,0:T(8,128)S(1)}, f32[256,128]{1,0:T(8,128)S(1)}, f32[256,128]{1,0:T(8,128)S(1)}) custom-call(f32[32,256,128]{2,1,0:T(8,128)S(1)} %copy-done.4), custom_call_target="tpu_custom_call" | custom-call | tf_op jit(solution)/shard_map/turn_and_pack/pallas_call | solution.py:397
  6.0 2.1 %copy-done = f32[280,32,128]{2,1,0:T(8,128)} copy-done((f32[280,32,128]{2,1,0:T(8,128)}, f32[280,32,128]{2,1,0:T(8,128)S(1)}, u32[]{:S(2)}) %copy-start) | copy-done | bytes 4587544
  8.1 2.9 %collective-permute-start = (f32[256,128]{1,0:T(8,128)S(1)}, f32[256,128]{1,0:T(8,128)S(1)}, u32[]{:S(2)}, u32[]{:S(2)}) collective-permute-start(f32[256,128]{1,0:T(8,128)S(1)} %get-tuple-element.14), channel_id=1, source_target_pairs={{0,8},{8,0},{16,24},{24,16},{1,9},{9,1},{17,25},{25,17},{2,10},{10... | collective-permute-start | bytes 393224 | tf_op jit(solution)/shard_map/ppermute | solution.py:370
  11.1 0.7 collective-permute-start.1
  11.7 2.8 %collective-permute-done.low_ref = f32[256,128]{1,0:T(8,128)S(1)} collective-permute-done((f32[256,128]{1,0:T(8,128)S(1)}, f32[256,128]{1,0:T(8,128)S(1)}, u32[]{:S(2)}, u32[]{:S(2)}) %collective-permute-start) | collective-permute-done | bytes 131104 | tf_op jit(solution)/shard_map/ppermute | solution.py:370
  14.6 0.0 collective-permute-done.1.high_ref
  14.6 2.3 %copy-done.1 = f32[280,32,128]{2,1,0:T(8,128)S(1)} copy-done((f32[280,32,128]{2,1,0:T(8,128)S(1)}, f32[280,32,128]{2,1,0:T(8,128)}, u32[]{:S(2)}) %copy-start.1) | copy-done | bytes 4587544
  16.9 0.3 lon_messages.1
  17.2 2.1 %copy-done.2 = f32[280,32,128]{2,1,0:T(8,128)} copy-done((f32[280,32,128]{2,1,0:T(8,128)}, f32[280,32,128]{2,1,0:T(8,128)S(1)}, u32[]{:S(2)}) %copy-start.2) | copy-done | bytes 4587544
  19.3 0.0 collective-permute-start.2
  19.3 4.0 %collective-permute-start.3 = (f32[17,32,128]{2,1,0:T(8,128)S(1)}, f32[17,32,128]{2,1,0:T(8,128)S(1)}, u32[]{:S(2)}, u32[]{:S(2)}) collective-permute-start(f32[17,32,128]{2,1,0:T(8,128)S(1)} %get-tuple-element.19), channel_id=1, source_target_pairs={{1,2},{2,1},{3,4},{4,3},{5,6},{6,5},{7,0},{0,7},{9,10},{10,9},{11,... | collective-permute-start | bytes 835592 | tf_op jit(solution)/shard_map/ppermute | solution.py:370
  23.3 0.1 pad_maximum_fusion.1
  23.4 0.1 concatenate.10
  23.5 0.1 dynamic_slice.7
  23.6 0.1 concatenate.9
  23.6 0.1 dynamic_slice.6
  23.8 2.3 %copy-done.3 = f32[280,32,128]{2,1,0:T(8,128)S(1)} copy-done((f32[280,32,128]{2,1,0:T(8,128)S(1)}, f32[280,32,128]{2,1,0:T(8,128)}, u32[]{:S(2)}) %copy-start.3) | copy-done | bytes 4587544
  26.0 5.1 %first_pass.1.once_ref = f32[280,32,128]{2,1,0:T(8,128)S(1)} custom-call(f32[3,272]{1,0:T(4,128)S(1)} %pad_maximum_fusion.rates_ref, f32[280,32,128]{2,1,0:T(8,128)S(1)} %copy-done.3, bf16[256,256]{1,0:T(8,128)(2,1)S(1)} %copy-done.5), custom_call_target="tpu_custom_call" | custom-call | flops 104857600 | bytes 8388608 | tf_op jit(solution)/shard_map/first_pass/pallas_call | solution.py:427
  31.2 0.0 collective-permute-done.2.first_ref
  31.2 0.0 collective-permute-done.3.second_ref
  31.2 13.3 %second_pass_and_gram.1 = (bf16[264,64,128]{2,1,0:T(8,128)(2,1)S(1)}, f32[8,128]{1,0:T(8,128)S(1)}) custom-call(f32[3,272]{1,0:T(4,128)S(1)} %pad_maximum_fusion.rates_ref, f32[280,32,128]{2,1,0:T(8,128)S(1)} %first_pass.1.once_ref, f32[34,32,128]{2,1,0:T(8,128)S(1)} %get-tuple-element.17.strip_ref, f32[17,32,128]{2,1,0:T(8,128)S(1)} %collective-permute-done.2.first_ref, ...), custom_call_target="tpu_custom_call" | custom-call | tf_op jit(solution)/shard_map/second_pass_and_gram/pallas_call | solution.py:438
  44.6 14.2 %all_to_all.5.gram_ref = f32[32,8,128]{2,1,0:T(8,128)S(1)} all-to-all(f32[32,8,128]{2,1,0:T(8,128)S(1)} %broadcast_in_dim.3), channel_id=1, replica_groups=mesh['lat'=4,'lon'=8] {'lat','lon'}, dimensions={0} | all-to-all | bytes 262144 | tf_op jit(solution)/shard_map/all_to_all | solution.py:376
  58.7 7.4 %factor_and_basis.1 = (bf16[32,256,128]{2,1,0:T(8,128)(2,1)}, f32[32,32]{1,0:T(8,128)}) custom-call(f32[32,8,128]{2,1,0:T(8,128)S(1)} %all_to_all.5.gram_ref, bf16[264,64,128]{2,1,0:T(8,128)(2,1)S(1)} %get-tuple-element.21.split_ref), custom_call_target="tpu_custom_call" | custom-call | tf_op jit(solution)/shard_map/factor_and_basis/pallas_call | solution.py:459
  (22 shorter events, 0.1 us)
Async XLA Ops:
  0.6 2.2 %copy-start.4 = (f32[32,256,128]{2,1,0:T(8,128)S(1)}, f32[32,256,128]{2,1,0:T(8,128)}, u32[]{:S(2)}) copy-start(f32[32,256,128]{2,1,0:T(8,128)} %field_ref.1) | copy-start | bytes 12582916
  2.8 20.6 %copy-start.8 = (f32[1024]{0:T(1024)S(1)}, f32[1024]{0:T(1024)}, u32[]{:S(2)}) copy-start(f32[1024]{0:T(1024)} %param.8) | copy-start | bytes 12292
  2.8 20.7 %copy-start.9 = (f32[1024]{0:T(1024)S(1)}, f32[1024]{0:T(1024)}, u32[]{:S(2)}) copy-start(f32[1024]{0:T(1024)} %param.7) | copy-start | bytes 12292
  2.8 20.9 %copy-start.5 = (bf16[256,256]{1,0:T(8,128)(2,1)S(1)}, bf16[256,256]{1,0:T(8,128)(2,1)}, u32[]{:S(2)}) copy-start(bf16[256,256]{1,0:T(8,128)(2,1)} %constant.27.clone.main_ref) | copy-start | bytes 393220
  6.0 2.1 %copy-start = (f32[280,32,128]{2,1,0:T(8,128)}, f32[280,32,128]{2,1,0:T(8,128)S(1)}, u32[]{:S(2)}) copy-start(f32[280,32,128]{2,1,0:T(8,128)S(1)} %get-tuple-element.12.ext_in_ref) | copy-start | bytes 13762564
  8.1 6.4 %collective-permute-start = (f32[256,128]{1,0:T(8,128)S(1)}, f32[256,128]{1,0:T(8,128)S(1)}, u32[]{:S(2)}, u32[]{:S(2)}) collective-permute-start(f32[256,128]{1,0:T(8,128)S(1)} %get-tuple-element.14), channel_id=1, source_target_pairs={{0,8},{8,0},{16,24},{24,16},{1,9},{9,1},{17,25},{25,17},{2,10},{10... | collective-permute-start | bytes 393224 | tf_op jit(solution)/shard_map/ppermute | solution.py:370
  11.1 3.5 %collective-permute-start.1 = (f32[256,128]{1,0:T(8,128)S(1)}, f32[256,128]{1,0:T(8,128)S(1)}, u32[]{:S(2)}, u32[]{:S(2)}) collective-permute-start(f32[256,128]{1,0:T(8,128)S(1)} %get-tuple-element.15), channel_id=1, source_target_pairs={{8,16},{16,8},{9,17},{17,9},{10,18},{18,10},{11,19},{19,11},{12,20... | collective-permute-start | bytes 393224 | tf_op jit(solution)/shard_map/ppermute | solution.py:370
  14.6 2.3 %copy-start.1 = (f32[280,32,128]{2,1,0:T(8,128)S(1)}, f32[280,32,128]{2,1,0:T(8,128)}, u32[]{:S(2)}) copy-start(f32[280,32,128]{2,1,0:T(8,128)} %copy-done) | copy-start | bytes 13762564
  17.2 2.1 %copy-start.2 = (f32[280,32,128]{2,1,0:T(8,128)}, f32[280,32,128]{2,1,0:T(8,128)S(1)}, u32[]{:S(2)}) copy-start(f32[280,32,128]{2,1,0:T(8,128)S(1)} %get-tuple-element.16.ext_ref) | copy-start | bytes 13762564
  19.3 11.9 %collective-permute-start.2 = (f32[17,32,128]{2,1,0:T(8,128)S(1)}, f32[17,32,128]{2,1,0:T(8,128)S(1)}, u32[]{:S(2)}, u32[]{:S(2)}) collective-permute-start(f32[17,32,128]{2,1,0:T(8,128)S(1)} %get-tuple-element.18), channel_id=1, source_target_pairs={{0,1},{1,0},{2,3},{3,2},{4,5},{5,4},{6,7},{7,6},{8,9},{9,8},{10,11... | collective-permute-start | bytes 835592 | tf_op jit(solution)/shard_map/ppermute | solution.py:370
  19.3 11.9 %collective-permute-start.3 = (f32[17,32,128]{2,1,0:T(8,128)S(1)}, f32[17,32,128]{2,1,0:T(8,128)S(1)}, u32[]{:S(2)}, u32[]{:S(2)}) collective-permute-start(f32[17,32,128]{2,1,0:T(8,128)S(1)} %get-tuple-element.19), channel_id=1, source_target_pairs={{1,2},{2,1},{3,4},{4,3},{5,6},{6,5},{7,0},{0,7},{9,10},{10,9},{11,... | collective-permute-start | bytes 835592 | tf_op jit(solution)/shard_map/ppermute | solution.py:370
  23.7 2.3 %copy-start.3 = (f32[280,32,128]{2,1,0:T(8,128)S(1)}, f32[280,32,128]{2,1,0:T(8,128)}, u32[]{:S(2)}) copy-start(f32[280,32,128]{2,1,0:T(8,128)} %copy-done.2) | copy-start | bytes 13762564
  26.0 5.2 %copy-start.6 = (bf16[512,512]{1,0:T(8,128)(2,1)S(1)}, bf16[512,512]{1,0:T(8,128)(2,1)}, u32[]{:S(2)}) copy-start(bf16[512,512]{1,0:T(8,128)(2,1)} %constant.28.clone.edge_ref) | copy-start | bytes 1572868
  26.0 5.2 %copy-start.7 = (bf16[256,256]{1,0:T(8,128)(2,1)S(1)}, bf16[256,256]{1,0:T(8,128)(2,1)}, u32[]{:S(2)}) copy-start(bf16[256,256]{1,0:T(8,128)(2,1)} %constant.29.clone.inward_ref) | copy-start | bytes 393220

commit v4 on v3

--- a/solution.py
+++ b/solution.py
@@ -63,13 +63,25 @@
     return np.concatenate([main, main], axis=0), np.concatenate([edge, inward_only], axis=1), inward
 
 
-def strip_kernel(span, field_ref, ext_ref, strip_ref, first_ref, second_ref):
+def edge_kernel(field_ref, first_ref, second_ref, sems):
+    rows = field_ref.shape[1]
+    begin = (1 - lax.axis_index("lat") % 2) * (rows - HALO)
+    copies = []
+    for at, (start, target) in enumerate(
+        [(begin, first_ref), (rows - HALO - begin, second_ref)]
+    ):
+        start = pl.multiple_of(start, HALO)
+        copies.append(
+            pltpu.make_async_copy(field_ref.at[:, pl.ds(start, HALO), :], target, sems.at[at])
+        )
+    for copy in copies:
+        copy.start()
+    for copy in copies:
+        copy.wait()
+
+
+def strip_kernel(span, field_ref, ext_ref, strip_ref):
     snaps, rows, _ = field_ref.shape
-    lat_even = lax.axis_index("lat") % 2 == 0
-    north = field_ref[:, :HALO].reshape(snaps * HALO, LANES)
-    south = field_ref[:, rows - HALO :].reshape(snaps * HALO, LANES)
-    first_ref[...] = jnp.where(lat_even, south, north)
-    second_ref[...] = jnp.where(lat_even, north, south)
 
     def turn(at, carry):
         begin = pl.multiple_of(at * 8, 8)
@@ -108,9 +120,8 @@
     lon_even = lax.axis_index("lon") % 2 == 0
     full_ref[...] = strip_ref[...]
     for tile in range(0, snaps, 8):
-        part = slice(tile * HALO, (tile + 8) * HALO)
-        first = jnp.swapaxes(low_ref[part].reshape(8, HALO, LANES), 0, 1)
-        second = jnp.swapaxes(high_ref[part].reshape(8, HALO, LANES), 0, 1)
+        first = jnp.swapaxes(low_ref[tile : tile + 8], 0, 1)
+        second = jnp.swapaxes(high_ref[tile : tile + 8], 0, 1)
         ext_ref[4 : 4 + HALO, tile : tile + 8] = jnp.where(lat_even, second, first)
         ext_ref[end : end + HALO, tile : tile + 8] = jnp.where(lat_even, first, second)
     for at in range(HALO):
@@ -144,7 +155,18 @@
     return product[:, :LANES] + product[:, LANES:]
 
 
-def stencil_rows(load, begin, span, part, rates_ref, store):
+def rate_reader(rows, rates_refs):
+    last = rows * lax.axis_size("lat") - 1
+    origin = lax.axis_index("lat") * rows - HALO
+
+    def read(at):
+        row = jnp.clip(origin + at, 0, last)
+        return [ref[row] for ref in rates_refs]
+
+    return read
+
+
+def stencil_rows(load, begin, span, part, rates, store):
     loaded = {}
 
     def row(at):
@@ -155,20 +177,15 @@
     for at in range(span):
         here = at + 4
         pairs = [row(here + offset) + row(here - offset) for offset in range(1, 5)]
-        store(
-            at,
-            stencil_row(
-                row(here), pairs, part[at], rates_ref[0, begin + at], rates_ref[1, begin + at]
-            ),
-        )
-
-
-def first_kernel(span, rates_ref, ext_ref, main_ref, once_ref):
+        values = rates(begin + at)
+        store(at, stencil_row(row(here), pairs, part[at], values[0], values[1]), values)
+
+
+def first_kernel(span, lon_ref, lat_ref, ext_ref, main_ref, once_ref):
     snaps = ext_ref.shape[1]
     total = span * GROUPS
-    ends = jnp.zeros((4, snaps, LANES), jnp.float32)
-    once_ref[:4] = ends
-    once_ref[total + 4 :] = ends
+    rows = total - 2 * HALO
+    rates = rate_reader(rows, (lon_ref, lat_ref))
     for tile in range(0, snaps, TILE):
         snap = slice(tile, tile + TILE)
 
@@ -180,18 +197,23 @@
             def load(at):
                 return ext_ref[at, snap]
 
-            def store(at, value):
+            def store(at, value, _):
                 once_ref[4 + begin + at, snap] = value
 
-            stencil_rows(load, begin, span, part, rates_ref, store)
+            stencil_rows(load, begin, span, part, rates, store)
             return carry
 
         lax.fori_loop(0, GROUPS, body, 0)
+    ends = jnp.zeros((4, snaps, LANES), jnp.float32)
+    once_ref[:4] = ends
+    once_ref[total + 4 :] = ends
 
 
 def second_kernel(
     span,
-    rates_ref,
+    lon_ref,
+    lat_ref,
+    weight_ref,
     once_ref,
     strip_ref,
     first_ref,
@@ -217,12 +239,17 @@
     left = lane % STRIP < HALO
     rim = (lane < HALO) | (lane >= LANES - HALO)
     group_of = lax.broadcasted_iota(jnp.int32, (8, LANES), 1) // STRIP
+    rates = rate_reader(rows, (lon_ref, lat_ref, weight_ref))
     for at in range(span):
+        packed = [jnp.zeros((8, LANES), jnp.float32)] * 3
+        for group in range(GROUPS):
+            here = group_of == group
+            packed = [
+                jnp.where(here, value, old)
+                for value, old in zip(rates(group * span + at), packed)
+            ]
         for kind in range(3):
-            value = jnp.zeros((8, LANES), jnp.float32)
-            for group in range(GROUPS):
-                value = jnp.where(group_of == group, rates_ref[kind, group * span + at], value)
-            strip_rates_ref[kind, at] = value
+            strip_rates_ref[kind, at] = packed[kind]
 
     def strip_rate(kind, at):
         return jnp.concatenate([strip_rates_ref[kind, at]] * (TILE // 8), axis=0)
@@ -276,6 +303,16 @@
             return carry
 
         lax.fori_loop(0, GROUPS, complete, 0)
+        outside = jnp.zeros((HALO, TILE, LANES), jnp.float32)
+
+        @pl.when(lax.axis_index("lat") == 0)
+        def _():
+            full_ref[4 : 4 + HALO] = outside
+
+        @pl.when(lax.axis_index("lat") == lax.axis_size("lat") - 1)
+        def _():
+            full_ref[4 + HALO + rows : 4 + total] = outside
+
         for at in range(4):
             full_ref[at] = once_ref[at, snap]
             full_ref[total + 4 + at] = once_ref[total + 4 + at, snap]
@@ -288,13 +325,13 @@
             def load(at):
                 return full_ref[at]
 
-            def store(at, value):
-                hi, lo = hi_lo(rates_ref[2, begin + at] * value + added(1, at, group))
+            def store(at, value, values):
+                hi, lo = hi_lo(values[2] * value + added(1, at, group))
                 row = jnp.maximum(begin + at - HALO, 0)
                 split_ref[row, snap] = hi
                 split_ref[row, snaps + tile : snaps + tile + TILE] = lo
 
-            stencil_rows(load, begin, span, part, rates_ref, store)
+            stencil_rows(load, begin, span, part, rates, store)
             return carry
 
         lax.fori_loop(0, GROUPS, second_pass, 0)
@@ -382,7 +419,6 @@
 
 def shards(field, lon_rate, lat_rate):
     snaps, rows, cols = field.shape
-    row_start = lax.axis_index("lat") * rows
     total_rows = rows * lax.axis_size("lat")
     total_cells = total_rows * cols * lax.axis_size("lon")
     span = (rows + 2 * HALO) // GROUPS
@@ -393,16 +429,25 @@
     ext = jax.ShapeDtypeStruct((total + 8, snaps, cols), f32)
     strip = jax.ShapeDtypeStruct((span, snaps, cols), f32)
     half = jax.ShapeDtypeStruct((span // 2, snaps, cols), f32)
-    edge_rows = jax.ShapeDtypeStruct((snaps * HALO, cols), f32)
-    turned, packed, first, second = pl.pallas_call(
+    edge_rows = jax.ShapeDtypeStruct((snaps, HALO, cols), f32)
+    first, second = pl.pallas_call(
+        edge_kernel,
+        in_specs=[whole(pl.ANY)],
+        out_specs=[whole()] * 2,
+        out_shape=[edge_rows, edge_rows],
+        scratch_shapes=[pltpu.SemaphoreType.DMA((2,))],
+        compiler_params=pltpu.CompilerParams(vmem_limit_bytes=60 * 1024 * 1024),
+        name="lat_messages",
+    )(field)
+    low, high = pair_permutes([first, second], "lat", False)
+    turned, packed = pl.pallas_call(
         functools.partial(strip_kernel, span),
         in_specs=[whole()],
-        out_specs=[whole()] * 4,
-        out_shape=[ext, strip, edge_rows, edge_rows],
+        out_specs=[whole()] * 2,
+        out_shape=[ext, strip],
         compiler_params=limits,
         name="turn_and_pack",
     )(field)
-    low, high = pair_permutes([first, second], "lat", False)
     turned, packed, first, second = pl.pallas_call(
         functools.partial(message_kernel, span),
         in_specs=[whole()] * 4,
@@ -414,19 +459,13 @@
     )(turned, packed, low, high)
     first, second = pair_permutes([first, second], "lon", True)
 
-    pad = jnp.zeros((HALO,), f32)
-    rates = [
-        lax.dynamic_slice_in_dim(jnp.concatenate([pad, rate, pad]), row_start, rows + 2 * HALO)
-        for rate in (lon_rate, lat_rate)
-    ]
-    weight = jnp.concatenate([pad, area_weight(row_start, rows, total_rows), pad])
-    rates = jnp.stack([rates[0], rates[1], weight])
+    weight = area_weight(0, total_rows, total_rows)
 
     main, edge, inward = zonal_matrices()
     bf16 = jnp.bfloat16
     once = pl.pallas_call(
         functools.partial(first_kernel, span),
-        in_specs=[whole(pltpu.SMEM), whole(), whole()],
+        in_specs=[whole(pltpu.SMEM)] * 2 + [whole()] * 2,
         out_specs=whole(),
         out_shape=ext,
         compiler_params=limits,
@@ -434,10 +473,10 @@
             flops=100 * snaps * rows * cols, bytes_accessed=8 * snaps * rows * cols, transcendentals=0
         ),
         name="first_pass",
-    )(rates, turned, main)
+    )(lon_rate, lat_rate, turned, main)
     split, gram = pl.pallas_call(
         functools.partial(second_kernel, span),
-        in_specs=[whole(pltpu.SMEM)] + [whole()] * 7,
+        in_specs=[whole(pltpu.SMEM)] * 3 + [whole()] * 7,
         out_specs=[whole(), whole()],
         out_shape=[
             jax.ShapeDtypeStruct((rows + HALO, 2 * snaps, cols), bf16),
@@ -452,7 +491,7 @@
         ],
         compiler_params=limits,
         name="second_pass_and_gram",
-    )(rates, once, packed, first, second, main, edge, inward)
+    )(lon_rate, lat_rate, weight, once, packed, first, second, main, edge, inward)
 
     grams = gather_all(gram)
     block = 64

time: 66.4 us -> 57.7 us (0.87)
  local copies, waits for them, and re-layouts: 11.3 us -> 2.22 us
  Pallas kernels: 29.3 us -> 31.3 us
  waiting for transfers between devices: 2.83 us -> 1.26 us
    unnamed x20 -> x12, local copies, waits for them, and re-layouts: 11 us -> 2.21 us
    ppermute x2, waiting for transfers between devices: 2.83 us -> 0.01 us  [pair_permutes(): lax.ppermute(values[0], axis, inner)]
    pallas_call x0 -> x1, Pallas kernels: none -> 1.69 us  [shards(): pl.pallas_call(edge_kernel, in_specs=[whole(pl.ANY)], out_specs=[whole()]...]
    ppermute x2, waiting for transfers between devices: 0.01 us -> 1.26 us  [pair_permutes(): lax.ppermute(values[1], axis, outer)]
  transfers between devices with their start and end apart: 4 -> 4, of which waited for: 1 -> 1; matrix products, arithmetic and copies ran while one was open for 1% -> 0% of each run, Pallas kernels for 8% -> 14%
where the time goes in v4:
time: 57.7 us; the launch traced here: 57.5 us
  Pallas kernels  31.3 us (54%)
  blocking collectives  14.4 us (25%)
  starting transfers between devices  7.43 us (13%)
  local copies, waits for them, and re-layouts  2.22 us (4%)
  waiting for transfers between devices  1.26 us (2%)
  between operations  0.76 us (1%)
    all_to_all x1, blocking collectives, gather_all(): lax.all_to_all(jnp.broadcast_to(values, (count,) + values.shape), axes, 0...  14.4 us
    pallas_call x1, Pallas kernels, shards(): pl.pallas_call(functools.partial(second_kernel, span), in_specs=[whole(pl...  13.7 us
    pallas_call x1, Pallas kernels, shards(): pl.pallas_call(functools.partial(basis_kernel, math.sqrt(total_cells)), g...  7.35 us
    pallas_call x1, Pallas kernels, shards(): pl.pallas_call(functools.partial(first_kernel, span), in_specs=[whole(plt...  5.13 us
    ppermute x2, starting transfers between devices, pair_permutes(): lax.ppermute(values[1], axis, outer)  4.36 us
    pallas_call x1, Pallas kernels, shards(): pl.pallas_call(functools.partial(strip_kernel, span), in_specs=[whole()],...  3.17 us
    ppermute x2, starting transfers between devices, pair_permutes(): lax.ppermute(values[0], axis, inner)  3.07 us
    unnamed x12, local copies, waits for them, and re-layouts  2.21 us
  transfers between devices with their start and end apart: 4, of which 1 were waited for; matrix products, arithmetic and copies ran while one was open for 0% of the time, Pallas kernels for 14%

profile of v4, /device:TPU:0, one launch (start us, length us, event | category | flops | bytes accessed | tf_op | source)
XLA Modules:
  0.0 57.5 jit_solution(690303265595834366)
XLA Ops:
  0.6 1.7 %lat_messages.1 = (f32[32,8,128]{2,1,0:T(8,128)}, f32[32,8,128]{2,1,0:T(8,128)}) custom-call(f32[32,256,128]{2,1,0:T(8,128)} %field_ref.3), custom_call_target="tpu_custom_call" | custom-call | tf_op jit(solution)/shard_map/lat_messages/pallas_call | solution.py:433
  2.3 3.0 %collective-permute-start = (f32[32,8,128]{2,1,0:T(8,128)}, f32[32,8,128]{2,1,0:T(8,128)S(1)}, u32[]{:S(2)}, u32[]{:S(2)}) collective-permute-start(f32[32,8,128]{2,1,0:T(8,128)} %get-tuple-element.14), channel_id=1, source_target_pairs={{0,8},{8,0},{16,24},{24,16},{1,9},{9,1},{17,25},{25,17},{2,10},{10... | collective-permute-start | bytes 393224 | tf_op jit(solution)/shard_map/ppermute | solution.py:407
  5.3 0.7 %collective-permute-start.1 = (f32[32,8,128]{2,1,0:T(8,128)}, f32[32,8,128]{2,1,0:T(8,128)S(1)}, u32[]{:S(2)}, u32[]{:S(2)}) collective-permute-start(f32[32,8,128]{2,1,0:T(8,128)} %get-tuple-element.15), channel_id=1, source_target_pairs={{8,16},{16,8},{9,17},{17,9},{10,18},{18,10},{11,19},{19,11},{12,20... | collective-permute-start | bytes 393224 | tf_op jit(solution)/shard_map/ppermute | solution.py:407
  6.0 0.0 copy-start
  6.0 2.2 %copy-done = f32[32,256,128]{2,1,0:T(8,128)S(1)} copy-done((f32[32,256,128]{2,1,0:T(8,128)S(1)}, f32[32,256,128]{2,1,0:T(8,128)}, u32[]{:S(2)}) %copy-start) | copy-done | bytes 4194328
  8.2 3.2 %turn_and_pack.1 = (f32[280,32,128]{2,1,0:T(8,128)S(1)}, f32[34,32,128]{2,1,0:T(8,128)S(1)}) custom-call(f32[32,256,128]{2,1,0:T(8,128)S(1)} %copy-done), custom_call_target="tpu_custom_call" | custom-call | tf_op jit(solution)/shard_map/turn_and_pack/pallas_call | solution.py:443
  11.4 0.0 collective-permute-done.low_ref
  11.4 0.0 collective-permute-done.1.high_ref
  11.4 0.3 lon_messages.1
  11.7 0.1 collective-permute-start.2
  11.8 3.7 %collective-permute-start.3 = (f32[17,32,128]{2,1,0:T(8,128)S(1)}, f32[17,32,128]{2,1,0:T(8,128)S(1)}, u32[]{:S(2)}, u32[]{:S(2)}) collective-permute-start(f32[17,32,128]{2,1,0:T(8,128)S(1)} %get-tuple-element.19), channel_id=1, source_target_pairs={{1,2},{2,1},{3,4},{4,3},{5,6},{6,5},{7,0},{0,7},{9,10},{10,9},{11,... | collective-permute-start | bytes 835592 | tf_op jit(solution)/shard_map/ppermute | solution.py:407
  15.5 0.0 copy-done.1
  15.5 0.0 copy-done.4
  15.6 0.0 copy-done.5
  15.6 0.0 copy-start.2
  15.6 0.0 copy-start.3
  15.6 5.1 %first_pass.1.once_ref = f32[280,32,128]{2,1,0:T(8,128)S(1)} custom-call(f32[1024]{0:T(1024)S(1)} %copy-done.4, f32[1024]{0:T(1024)S(1)} %copy-done.5, f32[280,32,128]{2,1,0:T(8,128)S(1)} %get-tuple-element.16.ext_ref, bf16[256,256]{1,0:T(8,128)(2,1)S(1)} %copy-done.1), custom_call_target="tpu_custom_call" | custom-call | flops 104857600 | bytes 8388608 | tf_op jit(solution)/shard_map/first_pass/pallas_call | solution.py:466
  20.7 0.0 collective-permute-done.2.first_ref
  20.7 1.3 %collective-permute-done.3.second_ref = f32[17,32,128]{2,1,0:T(8,128)S(1)} collective-permute-done((f32[17,32,128]{2,1,0:T(8,128)S(1)}, f32[17,32,128]{2,1,0:T(8,128)S(1)}, u32[]{:S(2)}, u32[]{:S(2)}) %collective-permute-start.3) | collective-permute-done | bytes 278560 | tf_op jit(solution)/shard_map/ppermute | solution.py:407
  22.0 0.0 copy-done.2
  22.0 0.0 copy-done.3
  22.0 13.7 %second_pass_and_gram.1 = (bf16[264,64,128]{2,1,0:T(8,128)(2,1)S(1)}, f32[8,128]{1,0:T(8,128)S(1)}) custom-call(f32[1024]{0:T(1024)S(1)} %copy-done.4, f32[1024]{0:T(1024)S(1)} %copy-done.5, f32[1024]{0:T(1024)S(1)} %cosine_sqrt_fusion.weight_ref, f32[280,32,128]{2,1,0:T(8,128)S(1)} %first_pass.1.once_ref, f32[34,32,128]{2,1,0:T(8,128)S(1)} %get-tuple-element.17.strip_ref, ...), custom_call_target="tpu_custom_call" | custom-call | tf_op jit(solution)/shard_map/second_pass_and_gram/pallas_call | solution.py:477
  35.7 14.4 %all_to_all.5.gram_ref = f32[32,8,128]{2,1,0:T(8,128)S(1)} all-to-all(f32[32,8,128]{2,1,0:T(8,128)S(1)} %broadcast_in_dim.3), channel_id=1, replica_groups=mesh['lat'=4,'lon'=8] {'lat','lon'}, dimensions={0} | all-to-all | bytes 262144 | tf_op jit(solution)/shard_map/all_to_all | solution.py:413
  50.1 7.3 %factor_and_basis.1 = (bf16[32,256,128]{2,1,0:T(8,128)(2,1)}, f32[32,32]{1,0:T(8,128)}) custom-call(f32[32,8,128]{2,1,0:T(8,128)S(1)} %all_to_all.5.gram_ref, bf16[264,64,128]{2,1,0:T(8,128)(2,1)S(1)} %get-tuple-element.21.split_ref), custom_call_target="tpu_custom_call" | custom-call | tf_op jit(solution)/shard_map/factor_and_basis/pallas_call | solution.py:498
  (5 shorter events, 0.1 us)
Async XLA Ops:
  2.3 9.0 %collective-permute-start = (f32[32,8,128]{2,1,0:T(8,128)}, f32[32,8,128]{2,1,0:T(8,128)S(1)}, u32[]{:S(2)}, u32[]{:S(2)}) collective-permute-start(f32[32,8,128]{2,1,0:T(8,128)} %get-tuple-element.14), channel_id=1, source_target_pairs={{0,8},{8,0},{16,24},{24,16},{1,9},{9,1},{17,25},{25,17},{2,10},{10... | collective-permute-start | bytes 393224 | tf_op jit(solution)/shard_map/ppermute | solution.py:407
  5.3 6.1 %collective-permute-start.1 = (f32[32,8,128]{2,1,0:T(8,128)}, f32[32,8,128]{2,1,0:T(8,128)S(1)}, u32[]{:S(2)}, u32[]{:S(2)}) collective-permute-start(f32[32,8,128]{2,1,0:T(8,128)} %get-tuple-element.15), channel_id=1, source_target_pairs={{8,16},{16,8},{9,17},{17,9},{10,18},{18,10},{11,19},{19,11},{12,20... | collective-permute-start | bytes 393224 | tf_op jit(solution)/shard_map/ppermute | solution.py:407
  6.0 2.2 %copy-start = (f32[32,256,128]{2,1,0:T(8,128)S(1)}, f32[32,256,128]{2,1,0:T(8,128)}, u32[]{:S(2)}) copy-start(f32[32,256,128]{2,1,0:T(8,128)} %field_ref.3) | copy-start | bytes 12582916
  8.2 7.3 %copy-start.1 = (bf16[256,256]{1,0:T(8,128)(2,1)S(1)}, bf16[256,256]{1,0:T(8,128)(2,1)}, u32[]{:S(2)}) copy-start(bf16[256,256]{1,0:T(8,128)(2,1)} %constant.14.clone.main_ref) | copy-start | bytes 393220
  8.2 7.4 %copy-start.4 = (f32[1024]{0:T(1024)S(1)}, f32[1024]{0:T(1024)}, u32[]{:S(2)}) copy-start(f32[1024]{0:T(1024)} %lon_ref.3) | copy-start | bytes 12292
  8.2 7.4 %copy-start.5 = (f32[1024]{0:T(1024)S(1)}, f32[1024]{0:T(1024)}, u32[]{:S(2)}) copy-start(f32[1024]{0:T(1024)} %lat_ref.3) | copy-start | bytes 12292
  11.7 9.0 %collective-permute-start.2 = (f32[17,32,128]{2,1,0:T(8,128)S(1)}, f32[17,32,128]{2,1,0:T(8,128)S(1)}, u32[]{:S(2)}, u32[]{:S(2)}) collective-permute-start(f32[17,32,128]{2,1,0:T(8,128)S(1)} %get-tuple-element.18), channel_id=1, source_target_pairs={{0,1},{1,0},{2,3},{3,2},{4,5},{5,4},{6,7},{7,6},{8,9},{9,8},{10,11... | collective-permute-start | bytes 835592 | tf_op jit(solution)/shard_map/ppermute | solution.py:407
  11.8 10.2 %collective-permute-start.3 = (f32[17,32,128]{2,1,0:T(8,128)S(1)}, f32[17,32,128]{2,1,0:T(8,128)S(1)}, u32[]{:S(2)}, u32[]{:S(2)}) collective-permute-start(f32[17,32,128]{2,1,0:T(8,128)S(1)} %get-tuple-element.19), channel_id=1, source_target_pairs={{1,2},{2,1},{3,4},{4,3},{5,6},{6,5},{7,0},{0,7},{9,10},{10,9},{11,... | collective-permute-start | bytes 835592 | tf_op jit(solution)/shard_map/ppermute | solution.py:407
  15.6 6.4 %copy-start.2 = (bf16[512,512]{1,0:T(8,128)(2,1)S(1)}, bf16[512,512]{1,0:T(8,128)(2,1)}, u32[]{:S(2)}) copy-start(bf16[512,512]{1,0:T(8,128)(2,1)} %constant.15.clone.edge_ref) | copy-start | bytes 1572868
  15.6 6.4 %copy-start.3 = (bf16[256,256]{1,0:T(8,128)(2,1)S(1)}, bf16[256,256]{1,0:T(8,128)(2,1)}, u32[]{:S(2)}) copy-start(bf16[256,256]{1,0:T(8,128)(2,1)} %constant.16.clone.inward_ref) | copy-start | bytes 393220

commit v5 on v4

--- a/solution.py
+++ b/solution.py
@@ -56,11 +56,16 @@
     far = band(inner, outer)
     inward = band(outer, inner)
     near[:HALO, HALO:] = near[HALO:, :HALO] = 0.0
-    near, far, inward = [two_terms(block_diagonal(part)) for part in (near, far, inward)]
+    within = band(inner, inner)
+    within[:HALO, HALO:] = within[HALO:, :HALO] = 0.0
+    near, far, inward, within = [
+        two_terms(block_diagonal(part)) for part in (near, far, inward, within)
+    ]
     edge = np.concatenate([near, near, far, far], axis=0)
+    again = np.concatenate([inward, inward, within, within], axis=0)
     inward = np.concatenate([inward, inward], axis=0)
     inward_only = np.concatenate([inward, np.zeros_like(inward)], axis=0)
-    return np.concatenate([main, main], axis=0), np.concatenate([edge, inward_only], axis=1), inward
+    return np.concatenate([main, main], axis=0), np.concatenate([edge, inward_only], axis=1), again
 
 
 def edge_kernel(field_ref, first_ref, second_ref, sems):
@@ -181,15 +186,15 @@
         store(at, stencil_row(row(here), pairs, part[at], values[0], values[1]), values)
 
 
-def first_kernel(span, lon_ref, lat_ref, ext_ref, main_ref, once_ref):
+def tile_kernel(span, lon_ref, lat_ref, weight_ref, ext_ref, main_ref, twice_ref, once_ref):
     snaps = ext_ref.shape[1]
     total = span * GROUPS
     rows = total - 2 * HALO
-    rates = rate_reader(rows, (lon_ref, lat_ref))
+    rates = rate_reader(rows, (lon_ref, lat_ref, weight_ref))
     for tile in range(0, snaps, TILE):
         snap = slice(tile, tile + TILE)
 
-        def body(group, carry):
+        def first_pass(group, carry):
             begin = group * span
             center = ext_ref[pl.ds(4 + begin, span), snap].reshape(span * TILE, LANES)
             part = zonal_terms(hi_lo(center), main_ref[...]).reshape(span, TILE, LANES)
@@ -198,42 +203,74 @@
                 return ext_ref[at, snap]
 
             def store(at, value, _):
-                once_ref[4 + begin + at, snap] = value
+                once_ref[4 + begin + at] = value
 
             stencil_rows(load, begin, span, part, rates, store)
             return carry
 
-        lax.fori_loop(0, GROUPS, body, 0)
-    ends = jnp.zeros((4, snaps, LANES), jnp.float32)
-    once_ref[:4] = ends
-    once_ref[total + 4 :] = ends
-
-
-def second_kernel(
+        def second_pass(group, carry):
+            begin = group * span
+            center = once_ref[pl.ds(4 + begin, span)].reshape(span * TILE, LANES)
+            part = zonal_terms(hi_lo(center), main_ref[...]).reshape(span, TILE, LANES)
+
+            def load(at):
+                return once_ref[at]
+
+            def store(at, value, values):
+                twice_ref[begin + at, snap] = values[2] * value
+
+            stencil_rows(load, begin, span, part, rates, store)
+            return carry
+
+        lax.fori_loop(0, GROUPS, first_pass, 0)
+        ends = jnp.zeros((4, TILE, LANES), jnp.float32)
+        once_ref[:4] = ends
+        once_ref[total + 4 :] = ends
+        outside = jnp.zeros((HALO, TILE, LANES), jnp.float32)
+
+        @pl.when(lax.axis_index("lat") == 0)
+        def _():
+            once_ref[4 : 4 + HALO] = outside
+
+        @pl.when(lax.axis_index("lat") == lax.axis_size("lat") - 1)
+        def _():
+            once_ref[4 + HALO + rows : 4 + total] = outside
+
+        lax.fori_loop(0, GROUPS, second_pass, 0)
+    outside = jnp.zeros((HALO, snaps, LANES), jnp.float32)
+    twice_ref[:HALO] = outside
+    twice_ref[HALO + rows :] = outside
+
+
+def close_ends(strip_ref, span):
+    for at in range(4):
+        strip_ref[at] = pltpu.roll(strip_ref[span + at], STRIP, 1)
+        strip_ref[span + 4 + at] = pltpu.roll(strip_ref[4 + at], LANES - STRIP, 1)
+
+
+def rim_kernel(
     span,
     lon_ref,
     lat_ref,
     weight_ref,
-    once_ref,
+    twice_ref,
     strip_ref,
     first_ref,
     second_ref,
-    main_ref,
     edge_ref,
-    inward_ref,
+    again_ref,
     split_ref,
     gram_ref,
-    full_ref,
     outer_ref,
-    zonal_ref,
-    add_ref,
+    side_ref,
+    added_ref,
+    rim_ref,
     strip_rates_ref,
 ):
-    both = split_ref.shape[1]
-    rows = split_ref.shape[0] - HALO
+    total, both, _ = split_ref.shape
+    rows = total - 2 * HALO
     snaps = both // 2
     half = span // 2
-    total = span * GROUPS
     lon_even = lax.axis_index("lon") % 2 == 0
     lane = lax.broadcasted_iota(jnp.int32, (TILE, LANES), 1)
     left = lane % STRIP < HALO
@@ -244,15 +281,24 @@
         packed = [jnp.zeros((8, LANES), jnp.float32)] * 3
         for group in range(GROUPS):
             here = group_of == group
-            packed = [
-                jnp.where(here, value, old)
-                for value, old in zip(rates(group * span + at), packed)
-            ]
+            row = group * span + at
+            values = rates(row)
+            if row < HALO or row >= HALO + rows:
+                values[2] = 0.0
+            packed = [jnp.where(here, value, old) for value, old in zip(values, packed)]
         for kind in range(3):
             strip_rates_ref[kind, at] = packed[kind]
 
     def strip_rate(kind, at):
         return jnp.concatenate([strip_rates_ref[kind, at]] * (TILE // 8), axis=0)
+
+    def strip_stencil(source_ref, at, zonal):
+        pairs = [
+            source_ref[4 + at + offset] + source_ref[4 + at - offset] for offset in range(1, 5)
+        ]
+        return stencil_row(
+            source_ref[4 + at], pairs, zonal, strip_rate(0, at), strip_rate(1, at)
+        )
 
     for tile in range(0, snaps, TILE):
         snap = slice(tile, tile + TILE)
@@ -264,9 +310,7 @@
             outer_ref[4 + half + at] = jnp.where(
                 left, pltpu.roll(west, LANES - HALO, 1), pltpu.roll(east, HALO, 1)
             )
-        for at in range(4):
-            outer_ref[at] = pltpu.roll(outer_ref[span + at], STRIP, 1)
-            outer_ref[span + 4 + at] = pltpu.roll(outer_ref[4 + at], LANES - STRIP, 1)
+        close_ends(outer_ref, span)
         hi, lo = hi_lo(outer_ref[4 : 4 + span].reshape(span * TILE, LANES))
         own_hi, own_lo = hi_lo(strip_ref[:, snap].reshape(span * TILE, LANES))
         product = jnp.dot(
@@ -276,81 +320,47 @@
         ).reshape(span, TILE, 4 * LANES)
         for at in range(span):
             zonal = product[at, :, :LANES] + product[at, :, LANES : 2 * LANES]
-            pairs = [
-                outer_ref[4 + at + offset] + outer_ref[4 + at - offset] for offset in range(1, 5)
-            ]
-            zonal_rate = strip_rate(0, at)
-            zonal_ref[at] = stencil_row(
-                outer_ref[4 + at], pairs, zonal, zonal_rate, strip_rate(1, at)
-            )
-            add_ref[0, at] = zonal_rate * (
+            side_ref[at] = strip_stencil(outer_ref, at, zonal)
+            added_ref[4 + at] = strip_rate(0, at) * (
                 product[at, :, 2 * LANES : 3 * LANES] + product[at, :, 3 * LANES :]
             )
-        inner = zonal_ref[...].reshape(span * TILE, LANES)
-        product = zonal_terms(hi_lo(inner), inward_ref[...]).reshape(span, TILE, LANES)
+        close_ends(added_ref, span)
+        hi, lo = hi_lo(side_ref[...].reshape(span * TILE, LANES))
+        own_hi, own_lo = hi_lo(added_ref[4 : 4 + span].reshape(span * TILE, LANES))
+        part = zonal_terms([hi, lo, own_hi, own_lo], again_ref[...]).reshape(span, TILE, LANES)
         for at in range(span):
-            add_ref[1, at] = (strip_rate(2, at) * strip_rate(0, at)) * product[at]
-
-        def added(kind, at, group):
-            moved = pltpu.roll(add_ref[kind, at], LANES - HALO - STRIP * group, 1)
-            return jnp.where(rim, moved, 0.0)
-
-        def complete(group, carry):
-            begin = group * span
-            for at in range(span):
-                here = 4 + begin + at
-                full_ref[here] = once_ref[here, snap] + added(0, at, group)
-            return carry
-
-        lax.fori_loop(0, GROUPS, complete, 0)
-        outside = jnp.zeros((HALO, TILE, LANES), jnp.float32)
-
-        @pl.when(lax.axis_index("lat") == 0)
-        def _():
-            full_ref[4 : 4 + HALO] = outside
-
-        @pl.when(lax.axis_index("lat") == lax.axis_size("lat") - 1)
-        def _():
-            full_ref[4 + HALO + rows : 4 + total] = outside
-
-        for at in range(4):
-            full_ref[at] = once_ref[at, snap]
-            full_ref[total + 4 + at] = once_ref[total + 4 + at, snap]
-
-        def second_pass(group, carry):
-            begin = group * span
-            center = full_ref[pl.ds(4 + begin, span)].reshape(span * TILE, LANES)
-            part = zonal_terms(hi_lo(center), main_ref[...]).reshape(span, TILE, LANES)
-
-            def load(at):
-                return full_ref[at]
-
-            def store(at, value, values):
-                hi, lo = hi_lo(values[2] * value + added(1, at, group))
-                row = jnp.maximum(begin + at - HALO, 0)
-                split_ref[row, snap] = hi
-                split_ref[row, snaps + tile : snaps + tile + TILE] = lo
-
-            stencil_rows(load, begin, span, part, rates, store)
-            return carry
-
-        lax.fori_loop(0, GROUPS, second_pass, 0)
-
-    def square(at, total):
-        two = jnp.concatenate([split_ref[2 * at], split_ref[2 * at + 1]], axis=1)
-        return total + lax.dot_general(
-            two, two, (((1,), (1,)), ((), ())), preferred_element_type=jnp.float32
-        )
-
-    grams = lax.fori_loop(0, rows // 2, square, jnp.zeros((both, both), jnp.float32), unroll=8)
+            rim_ref[at, snap] = strip_rate(2, at) * strip_stencil(added_ref, at, part[at])
+
+    def finish(group, grams):
+        begin = group * span
+        shift = LANES - HALO - STRIP * group
+        for pair in range(0, span, 2):
+            rows_done = []
+            for at in (pair, pair + 1):
+                terms = []
+                for tile in range(0, snaps, TILE):
+                    snap = slice(tile, tile + TILE)
+                    moved = pltpu.roll(rim_ref[at, snap], shift, 1)
+                    value = twice_ref[begin + at, snap] + jnp.where(rim, moved, 0.0)
+                    terms.append(hi_lo(value))
+                row = jnp.concatenate(
+                    [term[0] for term in terms] + [term[1] for term in terms], axis=0
+                )
+                split_ref[begin + at] = row
+                rows_done.append(row)
+            two = jnp.concatenate(rows_done, axis=1)
+            grams = grams + lax.dot_general(
+                two, two, (((1,), (1,)), ((), ())), preferred_element_type=jnp.float32
+            )
+        return grams
+
+    grams = lax.fori_loop(0, GROUPS, finish, jnp.zeros((both, both), jnp.float32))
     gram = (
         grams[:snaps, :snaps]
         + grams[snaps:, snaps:]
         + (grams[:snaps, snaps:] + grams[snaps:, :snaps])
     )
-    gram_ref[...] = jnp.concatenate(
-        [gram[at : at + 8] for at in range(0, snaps, 8)], axis=1
-    )
+    gram_ref[...] = jnp.concatenate([gram[at : at + 8] for at in range(0, snaps, 8)], axis=1)
 
 
 def basis_kernel(root_count, gram_ref, split_ref, basis_ref, factor_ref, left_ref):
@@ -379,7 +389,7 @@
         left_ref[snaps:] = jnp.concatenate([lo, jnp.zeros_like(lo)], axis=1)
 
     left = left_ref[...]
-    start = pl.program_id(0) * basis_ref.shape[1]
+    start = pl.program_id(0) * basis_ref.shape[1] + HALO
 
     def body(at, carry):
         begin = pl.multiple_of(at * 16, 16)
@@ -461,37 +471,38 @@
 
     weight = area_weight(0, total_rows, total_rows)
 
-    main, edge, inward = zonal_matrices()
+    main, edge, again = zonal_matrices()
     bf16 = jnp.bfloat16
-    once = pl.pallas_call(
-        functools.partial(first_kernel, span),
-        in_specs=[whole(pltpu.SMEM)] * 2 + [whole()] * 2,
+    twice = pl.pallas_call(
+        functools.partial(tile_kernel, span),
+        in_specs=[whole(pltpu.SMEM)] * 3 + [whole()] * 2,
         out_specs=whole(),
-        out_shape=ext,
+        out_shape=jax.ShapeDtypeStruct((total, snaps, cols), f32),
+        scratch_shapes=[pltpu.VMEM((total + 8, TILE, cols), f32)],
         compiler_params=limits,
         cost_estimate=pl.CostEstimate(
             flops=100 * snaps * rows * cols, bytes_accessed=8 * snaps * rows * cols, transcendentals=0
         ),
-        name="first_pass",
-    )(lon_rate, lat_rate, turned, main)
+        name="both_passes",
+    )(lon_rate, lat_rate, weight, turned, main)
     split, gram = pl.pallas_call(
-        functools.partial(second_kernel, span),
-        in_specs=[whole(pltpu.SMEM)] * 3 + [whole()] * 7,
+        functools.partial(rim_kernel, span),
+        in_specs=[whole(pltpu.SMEM)] * 3 + [whole()] * 6,
         out_specs=[whole(), whole()],
         out_shape=[
-            jax.ShapeDtypeStruct((rows + HALO, 2 * snaps, cols), bf16),
+            jax.ShapeDtypeStruct((total, 2 * snaps, cols), bf16),
             jax.ShapeDtypeStruct((8, snaps // 8 * snaps), f32),
         ],
         scratch_shapes=[
-            pltpu.VMEM((total + 8, TILE, cols), f32),
             pltpu.VMEM((span + 8, TILE, cols), f32),
             pltpu.VMEM((span, TILE, cols), f32),
-            pltpu.VMEM((2, span, TILE, cols), f32),
+            pltpu.VMEM((span + 8, TILE, cols), f32),
+            pltpu.VMEM((span, snaps, cols), f32),
             pltpu.VMEM((3, span, 8, cols), f32),
         ],
         compiler_params=limits,
-        name="second_pass_and_gram",
-    )(lon_rate, lat_rate, weight, once, packed, first, second, main, edge, inward)
+        name="rim_and_gram",
+    )(lon_rate, lat_rate, weight, twice, packed, first, second, edge, again)
 
     grams = gather_all(gram)
     block = 64

time: 57.7 us -> 51.5 us (0.89)
  Pallas kernels: 31.3 us -> 28.3 us
  blocking collectives: 14.4 us -> 12.6 us
  waiting for transfers between devices: 1.26 us -> 0.01 us
    pallas_call x2, Pallas kernels: 18.8 us -> 15.8 us  [the longest x1 10.1 us: shards(): pl.pallas_call(functools.partial(tile_kernel, span), in_specs=[whole(pltp...]
    all_to_all x1, blocking collectives: 14.4 us -> 12.6 us  [gather_all(): lax.all_to_all(jnp.broadcast_to(values, (count,) + values.shape), axes, 0...]
    ppermute x2, waiting for transfers between devices: 1.26 us -> 0.01 us  [pair_permutes(): lax.ppermute(values[1], axis, outer)]
  transfers between devices with their start and end apart: 4 -> 4, of which waited for: 1 -> 0; matrix products, arithmetic and copies ran while one was open for 0% -> 0% of each run, Pallas kernels for 14% -> 26%
where the time goes in v5:
time: 51.5 us; the launch traced here: 51.3 us
  Pallas kernels  28.3 us (55%)
  blocking collectives  12.6 us (24%)
  starting transfers between devices  7.43 us (14%)
  local copies, waits for them, and re-layouts  2.22 us (4%)
  between operations  0.78 us (2%)
    all_to_all x1, blocking collectives, gather_all(): lax.all_to_all(jnp.broadcast_to(values, (count,) + values.shape), axes, 0...  12.6 us
    pallas_call x1, Pallas kernels, shards(): pl.pallas_call(functools.partial(tile_kernel, span), in_specs=[whole(pltp...  10.1 us
    pallas_call x1, Pallas kernels, shards(): pl.pallas_call(functools.partial(basis_kernel, math.sqrt(total_cells)), g...  7.33 us
    pallas_call x1, Pallas kernels, shards(): pl.pallas_call(functools.partial(rim_kernel, span), in_specs=[whole(pltpu...  5.68 us
    ppermute x2, starting transfers between devices, pair_permutes(): lax.ppermute(values[1], axis, outer)  4.36 us
    pallas_call x1, Pallas kernels, shards(): pl.pallas_call(functools.partial(strip_kernel, span), in_specs=[whole()],...  3.17 us
    ppermute x2, starting transfers between devices, pair_permutes(): lax.ppermute(values[0], axis, inner)  3.07 us
    unnamed x12, local copies, waits for them, and re-layouts  2.21 us
  transfers between devices with their start and end apart: 4, of which 0 were waited for; matrix products, arithmetic and copies ran while one was open for 0% of the time, Pallas kernels for 26%

profile of v5, /device:TPU:0, one launch (start us, length us, event | category | flops | bytes accessed | tf_op | source)
XLA Modules:
  0.0 51.3 jit_solution(8521970151780926801)
XLA Ops:
  0.6 1.7 %lat_messages.1 = (f32[32,8,128]{2,1,0:T(8,128)}, f32[32,8,128]{2,1,0:T(8,128)}) custom-call(f32[32,256,128]{2,1,0:T(8,128)} %field_ref.3), custom_call_target="tpu_custom_call" | custom-call | tf_op jit(solution)/shard_map/lat_messages/pallas_call | solution.py:443
  2.3 3.0 %collective-permute-start = (f32[32,8,128]{2,1,0:T(8,128)}, f32[32,8,128]{2,1,0:T(8,128)S(1)}, u32[]{:S(2)}, u32[]{:S(2)}) collective-permute-start(f32[32,8,128]{2,1,0:T(8,128)} %get-tuple-element.14), channel_id=1, source_target_pairs={{0,8},{8,0},{16,24},{24,16},{1,9},{9,1},{17,25},{25,17},{2,10},{10... | collective-permute-start | bytes 393224 | tf_op jit(solution)/shard_map/ppermute | solution.py:417
  5.3 0.7 %collective-permute-start.1 = (f32[32,8,128]{2,1,0:T(8,128)}, f32[32,8,128]{2,1,0:T(8,128)S(1)}, u32[]{:S(2)}, u32[]{:S(2)}) collective-permute-start(f32[32,8,128]{2,1,0:T(8,128)} %get-tuple-element.15), channel_id=1, source_target_pairs={{8,16},{16,8},{9,17},{17,9},{10,18},{18,10},{11,19},{19,11},{12,20... | collective-permute-start | bytes 393224 | tf_op jit(solution)/shard_map/ppermute | solution.py:417
  6.0 0.0 copy-start
  6.0 2.2 %copy-done = f32[32,256,128]{2,1,0:T(8,128)S(1)} copy-done((f32[32,256,128]{2,1,0:T(8,128)S(1)}, f32[32,256,128]{2,1,0:T(8,128)}, u32[]{:S(2)}) %copy-start) | copy-done | bytes 4194328
  8.2 3.2 %turn_and_pack.1 = (f32[280,32,128]{2,1,0:T(8,128)S(1)}, f32[34,32,128]{2,1,0:T(8,128)S(1)}) custom-call(f32[32,256,128]{2,1,0:T(8,128)S(1)} %copy-done), custom_call_target="tpu_custom_call" | custom-call | tf_op jit(solution)/shard_map/turn_and_pack/pallas_call | solution.py:453
  11.4 0.0 collective-permute-done.low_ref
  11.4 0.0 collective-permute-done.1.high_ref
  11.4 0.3 lon_messages.1
  11.7 0.1 collective-permute-start.2
  11.8 3.7 %collective-permute-start.3 = (f32[17,32,128]{2,1,0:T(8,128)S(1)}, f32[17,32,128]{2,1,0:T(8,128)S(1)}, u32[]{:S(2)}, u32[]{:S(2)}) collective-permute-start(f32[17,32,128]{2,1,0:T(8,128)S(1)} %get-tuple-element.19), channel_id=1, source_target_pairs={{1,2},{2,1},{3,4},{4,3},{5,6},{6,5},{7,0},{0,7},{9,10},{10,9},{11,... | collective-permute-start | bytes 835592 | tf_op jit(solution)/shard_map/ppermute | solution.py:417
  15.5 0.0 copy-done.3
  15.5 0.0 copy-done.4
  15.6 0.0 copy-done.5
  15.6 0.0 copy-start.1
  15.6 0.0 copy-start.2
  15.6 10.1 %both_passes.1.twice_ref = f32[272,32,128]{2,1,0:T(8,128)S(1)} custom-call(f32[1024]{0:T(1024)S(1)} %copy-done.4, f32[1024]{0:T(1024)S(1)} %copy-done.5, f32[1024]{0:T(1024)S(1)} %cosine_sqrt_fusion.weight_ref, f32[280,32,128]{2,1,0:T(8,128)S(1)} %get-tuple-element.16.ext_ref, bf16[256,256]{1,0:T(8,128)(2,1)S(1)} %copy-done.3), custom_call_target="tpu_custom_call" | custom-call | flops 104857600 | bytes 8388608 | tf_op jit(solution)/shard_map/both_passes/pallas_call | solution.py:476
  25.7 0.0 collective-permute-done.2.first_ref
  25.7 0.0 collective-permute-done.3.second_ref
  25.7 0.0 copy-done.1
  25.7 0.0 copy-done.2
  25.7 5.7 %rim_and_gram.1 = (bf16[272,64,128]{2,1,0:T(8,128)(2,1)S(1)}, f32[8,128]{1,0:T(8,128)S(1)}) custom-call(f32[1024]{0:T(1024)S(1)} %copy-done.4, f32[1024]{0:T(1024)S(1)} %copy-done.5, f32[1024]{0:T(1024)S(1)} %cosine_sqrt_fusion.weight_ref, f32[272,32,128]{2,1,0:T(8,128)S(1)} %both_passes.1.twice_ref, f32[34,32,128]{2,1,0:T(8,128)S(1)} %get-tuple-element.17.strip_ref, ...), custom_call_target="tpu_custom_call" | custom-call | tf_op jit(solution)/shard_map/rim_and_gram/pallas_call | solution.py:488
  31.4 12.6 %all_to_all.5.gram_ref = f32[32,8,128]{2,1,0:T(8,128)S(1)} all-to-all(f32[32,8,128]{2,1,0:T(8,128)S(1)} %broadcast_in_dim.3), channel_id=1, replica_groups=mesh['lat'=4,'lon'=8] {'lat','lon'}, dimensions={0} | all-to-all | bytes 262144 | tf_op jit(solution)/shard_map/all_to_all | solution.py:423
  44.0 7.3 %factor_and_basis.1 = (bf16[32,256,128]{2,1,0:T(8,128)(2,1)}, f32[32,32]{1,0:T(8,128)}) custom-call(f32[32,8,128]{2,1,0:T(8,128)S(1)} %all_to_all.5.gram_ref, bf16[272,64,128]{2,1,0:T(8,128)(2,1)S(1)} %get-tuple-element.21.split_ref), custom_call_target="tpu_custom_call" | custom-call | tf_op jit(solution)/shard_map/factor_and_basis/pallas_call | solution.py:509
  (5 shorter events, 0.1 us)
Async XLA Ops:
  2.3 9.0 %collective-permute-start = (f32[32,8,128]{2,1,0:T(8,128)}, f32[32,8,128]{2,1,0:T(8,128)S(1)}, u32[]{:S(2)}, u32[]{:S(2)}) collective-permute-start(f32[32,8,128]{2,1,0:T(8,128)} %get-tuple-element.14), channel_id=1, source_target_pairs={{0,8},{8,0},{16,24},{24,16},{1,9},{9,1},{17,25},{25,17},{2,10},{10... | collective-permute-start | bytes 393224 | tf_op jit(solution)/shard_map/ppermute | solution.py:417
  5.3 6.1 %collective-permute-start.1 = (f32[32,8,128]{2,1,0:T(8,128)}, f32[32,8,128]{2,1,0:T(8,128)S(1)}, u32[]{:S(2)}, u32[]{:S(2)}) collective-permute-start(f32[32,8,128]{2,1,0:T(8,128)} %get-tuple-element.15), channel_id=1, source_target_pairs={{8,16},{16,8},{9,17},{17,9},{10,18},{18,10},{11,19},{19,11},{12,20... | collective-permute-start | bytes 393224 | tf_op jit(solution)/shard_map/ppermute | solution.py:417
  6.0 2.2 %copy-start = (f32[32,256,128]{2,1,0:T(8,128)S(1)}, f32[32,256,128]{2,1,0:T(8,128)}, u32[]{:S(2)}) copy-start(f32[32,256,128]{2,1,0:T(8,128)} %field_ref.3) | copy-start | bytes 12582916
  8.2 7.3 %copy-start.3 = (bf16[256,256]{1,0:T(8,128)(2,1)S(1)}, bf16[256,256]{1,0:T(8,128)(2,1)}, u32[]{:S(2)}) copy-start(bf16[256,256]{1,0:T(8,128)(2,1)} %constant.14.clone.main_ref) | copy-start | bytes 393220
  8.2 7.4 %copy-start.4 = (f32[1024]{0:T(1024)S(1)}, f32[1024]{0:T(1024)}, u32[]{:S(2)}) copy-start(f32[1024]{0:T(1024)} %lon_ref.3) | copy-start | bytes 12292
  8.2 7.4 %copy-start.5 = (f32[1024]{0:T(1024)S(1)}, f32[1024]{0:T(1024)}, u32[]{:S(2)}) copy-start(f32[1024]{0:T(1024)} %lat_ref.3) | copy-start | bytes 12292
  11.7 14.0 %collective-permute-start.2 = (f32[17,32,128]{2,1,0:T(8,128)S(1)}, f32[17,32,128]{2,1,0:T(8,128)S(1)}, u32[]{:S(2)}, u32[]{:S(2)}) collective-permute-start(f32[17,32,128]{2,1,0:T(8,128)S(1)} %get-tuple-element.18), channel_id=1, source_target_pairs={{0,1},{1,0},{2,3},{3,2},{4,5},{5,4},{6,7},{7,6},{8,9},{9,8},{10,11... | collective-permute-start | bytes 835592 | tf_op jit(solution)/shard_map/ppermute | solution.py:417
  11.8 13.9 %collective-permute-start.3 = (f32[17,32,128]{2,1,0:T(8,128)S(1)}, f32[17,32,128]{2,1,0:T(8,128)S(1)}, u32[]{:S(2)}, u32[]{:S(2)}) collective-permute-start(f32[17,32,128]{2,1,0:T(8,128)S(1)} %get-tuple-element.19), channel_id=1, source_target_pairs={{1,2},{2,1},{3,4},{4,3},{5,6},{6,5},{7,0},{0,7},{9,10},{10,9},{11,... | collective-permute-start | bytes 835592 | tf_op jit(solution)/shard_map/ppermute | solution.py:417
  15.6 10.1 %copy-start.1 = (bf16[512,512]{1,0:T(8,128)(2,1)S(1)}, bf16[512,512]{1,0:T(8,128)(2,1)}, u32[]{:S(2)}) copy-start(bf16[512,512]{1,0:T(8,128)(2,1)} %constant.15.clone.edge_ref) | copy-start | bytes 1572868
  15.6 10.1 %copy-start.2 = (bf16[512,256]{1,0:T(8,128)(2,1)S(1)}, bf16[512,256]{1,0:T(8,128)(2,1)}, u32[]{:S(2)}) copy-start(bf16[512,256]{1,0:T(8,128)(2,1)} %constant.16.clone.again_ref) | copy-start | bytes 786436

commit v6 on v5

--- a/solution.py
+++ b/solution.py
@@ -16,6 +16,7 @@
 LANES = 128
 GROUPS = LANES // STRIP
 TILE = 16
+PIVOTS = 8
 VMEM_BYTES = 24 * 1024 * 1024
 
 
@@ -68,21 +69,12 @@
     return np.concatenate([main, main], axis=0), np.concatenate([edge, inward_only], axis=1), again
 
 
-def edge_kernel(field_ref, first_ref, second_ref, sems):
+def edge_kernel(field_ref, first_ref, second_ref):
     rows = field_ref.shape[1]
-    begin = (1 - lax.axis_index("lat") % 2) * (rows - HALO)
-    copies = []
-    for at, (start, target) in enumerate(
-        [(begin, first_ref), (rows - HALO - begin, second_ref)]
-    ):
-        start = pl.multiple_of(start, HALO)
-        copies.append(
-            pltpu.make_async_copy(field_ref.at[:, pl.ds(start, HALO), :], target, sems.at[at])
-        )
-    for copy in copies:
-        copy.start()
-    for copy in copies:
-        copy.wait()
+    lat_even = lax.axis_index("lat") % 2 == 0
+    north, south = field_ref[:, :HALO], field_ref[:, rows - HALO :]
+    first_ref[...] = jnp.where(lat_even, south, north)
+    second_ref[...] = jnp.where(lat_even, north, south)
 
 
 def strip_kernel(span, field_ref, ext_ref, strip_ref):
@@ -96,7 +88,7 @@
             )
         return carry
 
-    lax.fori_loop(0, rows // 8, turn, 0, unroll=2)
+    lax.fori_loop(0, rows // 8, turn, 0, unroll=4)
     ends = jnp.zeros((4 + HALO, snaps, LANES), jnp.float32)
     ext_ref[: 4 + HALO] = ends
     ext_ref[4 + HALO + rows :] = ends
@@ -111,7 +103,7 @@
         strip_ref[at] = packed
         return carry
 
-    lax.fori_loop(0, span, pack, 0, unroll=2)
+    lax.fori_loop(0, span, pack, 0, unroll=span // 2)
 
 
 def message_kernel(
@@ -191,13 +183,18 @@
     total = span * GROUPS
     rows = total - 2 * HALO
     rates = rate_reader(rows, (lon_ref, lat_ref, weight_ref))
-    for tile in range(0, snaps, TILE):
-        snap = slice(tile, tile + TILE)
-
-        def first_pass(group, carry):
-            begin = group * span
-            center = ext_ref[pl.ds(4 + begin, span), snap].reshape(span * TILE, LANES)
-            part = zonal_terms(hi_lo(center), main_ref[...]).reshape(span, TILE, LANES)
+    chunk = total // 2
+    ends = jnp.zeros((4, TILE, LANES), jnp.float32)
+    once_ref[:4] = ends
+    once_ref[total + 4 :] = ends
+
+    def one_tile(tile, carry):
+        snap = pl.ds(pl.multiple_of(tile * TILE, TILE), TILE)
+
+        def first_pass(part, carry):
+            begin = part * chunk
+            center = ext_ref[pl.ds(4 + begin, chunk), snap].reshape(chunk * TILE, LANES)
+            part = zonal_terms(hi_lo(center), main_ref[...]).reshape(chunk, TILE, LANES)
 
             def load(at):
                 return ext_ref[at, snap]
@@ -205,13 +202,13 @@
             def store(at, value, _):
                 once_ref[4 + begin + at] = value
 
-            stencil_rows(load, begin, span, part, rates, store)
+            stencil_rows(load, begin, chunk, part, rates, store)
             return carry
 
-        def second_pass(group, carry):
-            begin = group * span
-            center = once_ref[pl.ds(4 + begin, span)].reshape(span * TILE, LANES)
-            part = zonal_terms(hi_lo(center), main_ref[...]).reshape(span, TILE, LANES)
+        def second_pass(part, carry):
+            begin = part * chunk
+            center = once_ref[pl.ds(4 + begin, chunk)].reshape(chunk * TILE, LANES)
+            part = zonal_terms(hi_lo(center), main_ref[...]).reshape(chunk, TILE, LANES)
 
             def load(at):
                 return once_ref[at]
@@ -219,13 +216,10 @@
             def store(at, value, values):
                 twice_ref[begin + at, snap] = values[2] * value
 
-            stencil_rows(load, begin, span, part, rates, store)
+            stencil_rows(load, begin, chunk, part, rates, store)
             return carry
 
-        lax.fori_loop(0, GROUPS, first_pass, 0)
-        ends = jnp.zeros((4, TILE, LANES), jnp.float32)
-        once_ref[:4] = ends
-        once_ref[total + 4 :] = ends
+        lax.fori_loop(0, 2, first_pass, 0)
         outside = jnp.zeros((HALO, TILE, LANES), jnp.float32)
 
         @pl.when(lax.axis_index("lat") == 0)
@@ -236,7 +230,10 @@
         def _():
             once_ref[4 + HALO + rows : 4 + total] = outside
 
-        lax.fori_loop(0, GROUPS, second_pass, 0)
+        lax.fori_loop(0, 2, second_pass, 0)
+        return carry
+
+    lax.fori_loop(0, snaps // TILE, one_tile, 0)
     outside = jnp.zeros((HALO, snaps, LANES), jnp.float32)
     twice_ref[:HALO] = outside
     twice_ref[HALO + rows :] = outside
@@ -376,10 +373,21 @@
         )
         work = jnp.concatenate([gram, jnp.zeros((snaps, snaps), jnp.float32)], axis=1)
         work = jnp.where(col == row + snaps, 1.0, work)
-        for step in range(snaps):
-            pivot_row = work[step : step + 1, :]
-            ratio = work[:, step : step + 1] / work[step : step + 1, step : step + 1]
-            work = work - jnp.where(row > step, ratio, 0.0) * pivot_row
+        for step in range(0, snaps, PIVOTS):
+            below = [
+                jnp.broadcast_to(work[:, pivot : pivot + 1], work.shape)
+                for pivot in range(step, step + PIVOTS)
+            ]
+            across = [work[pivot : pivot + 1, :] for pivot in range(step, step + PIVOTS)]
+            for at in range(PIVOTS):
+                pivot = step + at
+                ratio = 1.0 / below[at][pivot : pivot + 1, :]
+                rest = jnp.where(row > pivot, below[at], 0.0)
+                work = work - (rest * ratio) * across[at]
+                for later in range(at + 1, PIVOTS):
+                    factor = below[later][pivot : pivot + 1, :] * ratio
+                    below[later] = below[later] - rest * factor
+                    across[later] = across[later] - factor * across[at]
         diagonal = jnp.sum(jnp.where(row == col, work, 0.0), axis=1, keepdims=True)
         work = work * lax.rsqrt(diagonal)
         upper = jnp.where(col >= row, work, 0.0)
@@ -442,11 +450,10 @@
     edge_rows = jax.ShapeDtypeStruct((snaps, HALO, cols), f32)
     first, second = pl.pallas_call(
         edge_kernel,
-        in_specs=[whole(pl.ANY)],
+        in_specs=[whole()],
         out_specs=[whole()] * 2,
         out_shape=[edge_rows, edge_rows],
-        scratch_shapes=[pltpu.SemaphoreType.DMA((2,))],
-        compiler_params=pltpu.CompilerParams(vmem_limit_bytes=60 * 1024 * 1024),
+        compiler_params=limits,
         name="lat_messages",
     )(field)
     low, high = pair_permutes([first, second], "lat", False)

time: 51.5 us -> 47.4 us (0.920)
  Pallas kernels: 28.3 us -> 21.8 us
  blocking collectives: 12.6 us -> 14 us
  waiting for transfers between devices: 0.01 us -> 0.59 us
    pallas_call x1, Pallas kernels: 10.1 us -> 8.18 us  [shards(): pl.pallas_call(functools.partial(tile_kernel, span), in_specs=[whole(pltp...]
    pallas_call x1, Pallas kernels: 7.33 us -> 5.49 us  [shards(): pl.pallas_call(functools.partial(basis_kernel, math.sqrt(total_cells)), g...]
    pallas_call x1, Pallas kernels: 1.69 us -> 0.03 us  [shards(): pl.pallas_call(edge_kernel, in_specs=[whole()], out_specs=[whole()] * 2,...]
    all_to_all x1, blocking collectives: 12.6 us -> 14 us  [gather_all(): lax.all_to_all(jnp.broadcast_to(values, (count,) + values.shape), axes, 0...]
    pallas_call x1, Pallas kernels: 3.17 us -> 2.1 us  [shards(): pl.pallas_call(functools.partial(strip_kernel, span), in_specs=[whole()],...]
    ppermute x2, waiting for transfers between devices: 0.01 us -> 0.59 us  [pair_permutes(): lax.ppermute(values[0], axis, inner)]
  transfers between devices with their start and end apart: 4 -> 4, of which waited for: 0 -> 1; matrix products, arithmetic and copies ran while one was open for 0% -> 0% of each run, Pallas kernels for 26% -> 22%
where the time goes in v6:
time: 47.4 us; the launch traced here: 47.3 us
  Pallas kernels  21.8 us (46%)
  blocking collectives  14 us (30%)
  starting transfers between devices  7.82 us (16%)
  local copies, waits for them, and re-layouts  2.22 us (5%)
  between operations  0.76 us (2%)
  waiting for transfers between devices  0.59 us (1%)
    all_to_all x1, blocking collectives, gather_all(): lax.all_to_all(jnp.broadcast_to(values, (count,) + values.shape), axes, 0...  14 us
    pallas_call x1, Pallas kernels, shards(): pl.pallas_call(functools.partial(tile_kernel, span), in_specs=[whole(pltp...  8.18 us
    pallas_call x1, Pallas kernels, shards(): pl.pallas_call(functools.partial(rim_kernel, span), in_specs=[whole(pltpu...  5.69 us
    pallas_call x1, Pallas kernels, shards(): pl.pallas_call(functools.partial(basis_kernel, math.sqrt(total_cells)), g...  5.49 us
    ppermute x2, starting transfers between devices, pair_permutes(): lax.ppermute(values[1], axis, outer)  4.74 us
    ppermute x2, starting transfers between devices, pair_permutes(): lax.ppermute(values[0], axis, inner)  3.07 us
    unnamed x12, local copies, waits for them, and re-layouts  2.21 us
    pallas_call x1, Pallas kernels, shards(): pl.pallas_call(functools.partial(strip_kernel, span), in_specs=[whole()],...  2.1 us
  transfers between devices with their start and end apart: 4, of which 1 were waited for; matrix products, arithmetic and copies ran while one was open for 0% of the time, Pallas kernels for 22%

profile of v6, /device:TPU:0, one launch (start us, length us, event | category | flops | bytes accessed | tf_op | source)
XLA Modules:
  0.0 47.3 jit_solution(9097984300371571031)
XLA Ops:
  0.6 0.0 copy-start
  0.6 2.2 %copy-done = f32[32,256,128]{2,1,0:T(8,128)S(1)} copy-done((f32[32,256,128]{2,1,0:T(8,128)S(1)}, f32[32,256,128]{2,1,0:T(8,128)}, u32[]{:S(2)}) %copy-start) | copy-done | bytes 4194328
  2.9 3.0 %collective-permute-start = (f32[32,8,128]{2,1,0:T(8,128)S(1)}, f32[32,8,128]{2,1,0:T(8,128)S(1)}, u32[]{:S(2)}, u32[]{:S(2)}) collective-permute-start(f32[32,8,128]{2,1,0:T(8,128)S(1)} %get-tuple-element.14), channel_id=1, source_target_pairs={{0,8},{8,0},{16,24},{24,16},{1,9},{9,1},{17,25},{25,17},{2,10},{10... | collective-permute-start | bytes 393224 | tf_op jit(solution)/shard_map/ppermute | solution.py:425
  5.9 0.0 copy-start.3
  5.9 0.8 %collective-permute-start.1 = (f32[32,8,128]{2,1,0:T(8,128)S(1)}, f32[32,8,128]{2,1,0:T(8,128)S(1)}, u32[]{:S(2)}, u32[]{:S(2)}) collective-permute-start(f32[32,8,128]{2,1,0:T(8,128)S(1)} %get-tuple-element.15), channel_id=1, source_target_pairs={{8,16},{16,8},{9,17},{17,9},{10,18},{18,10},{11,19},{19,11},{12,20... | collective-permute-start | bytes 393224 | tf_op jit(solution)/shard_map/ppermute | solution.py:425
  6.7 2.1 %turn_and_pack.1 = (f32[280,32,128]{2,1,0:T(8,128)S(1)}, f32[34,32,128]{2,1,0:T(8,128)S(1)}) custom-call(f32[32,256,128]{2,1,0:T(8,128)S(1)} %copy-done), custom_call_target="tpu_custom_call" | custom-call | tf_op jit(solution)/shard_map/turn_and_pack/pallas_call | solution.py:460
  8.8 0.6 %collective-permute-done.low_ref = f32[32,8,128]{2,1,0:T(8,128)S(1)} collective-permute-done((f32[32,8,128]{2,1,0:T(8,128)S(1)}, f32[32,8,128]{2,1,0:T(8,128)S(1)}, u32[]{:S(2)}, u32[]{:S(2)}) %collective-permute-start) | collective-permute-done | bytes 131104 | tf_op jit(solution)/shard_map/ppermute | solution.py:425
  9.4 0.0 collective-permute-done.1.high_ref
  9.4 0.3 lon_messages.1
  9.7 0.1 collective-permute-start.2
  9.7 4.0 %collective-permute-start.3 = (f32[17,32,128]{2,1,0:T(8,128)S(1)}, f32[17,32,128]{2,1,0:T(8,128)S(1)}, u32[]{:S(2)}, u32[]{:S(2)}) collective-permute-start(f32[17,32,128]{2,1,0:T(8,128)S(1)} %get-tuple-element.19), channel_id=1, source_target_pairs={{1,2},{2,1},{3,4},{4,3},{5,6},{6,5},{7,0},{0,7},{9,10},{10,9},{11,... | collective-permute-start | bytes 835592 | tf_op jit(solution)/shard_map/ppermute | solution.py:425
  13.7 0.0 copy-done.3
  13.8 0.0 copy-done.4
  13.8 0.0 copy-done.5
  13.8 0.0 copy-start.1
  13.8 0.0 copy-start.2
  13.8 8.2 %both_passes.1.twice_ref = f32[272,32,128]{2,1,0:T(8,128)S(1)} custom-call(f32[1024]{0:T(1024)S(1)} %copy-done.4, f32[1024]{0:T(1024)S(1)} %copy-done.5, f32[1024]{0:T(1024)S(1)} %cosine_sqrt_fusion.weight_ref, f32[280,32,128]{2,1,0:T(8,128)S(1)} %get-tuple-element.16.ext_ref, bf16[256,256]{1,0:T(8,128)(2,1)S(1)} %copy-done.3), custom_call_target="tpu_custom_call" | custom-call | flops 104857600 | bytes 8388608 | tf_op jit(solution)/shard_map/both_passes/pallas_call | solution.py:483
  22.0 0.0 collective-permute-done.2.first_ref
  22.0 0.0 collective-permute-done.3.second_ref
  22.0 0.0 copy-done.1
  22.0 0.0 copy-done.2
  22.0 5.7 %rim_and_gram.1 = (bf16[272,64,128]{2,1,0:T(8,128)(2,1)S(1)}, f32[8,128]{1,0:T(8,128)S(1)}) custom-call(f32[1024]{0:T(1024)S(1)} %copy-done.4, f32[1024]{0:T(1024)S(1)} %copy-done.5, f32[1024]{0:T(1024)S(1)} %cosine_sqrt_fusion.weight_ref, f32[272,32,128]{2,1,0:T(8,128)S(1)} %both_passes.1.twice_ref, f32[34,32,128]{2,1,0:T(8,128)S(1)} %get-tuple-element.17.strip_ref, ...), custom_call_target="tpu_custom_call" | custom-call | tf_op jit(solution)/shard_map/rim_and_gram/pallas_call | solution.py:495
  27.7 14.0 %all_to_all.5.gram_ref = f32[32,8,128]{2,1,0:T(8,128)S(1)} all-to-all(f32[32,8,128]{2,1,0:T(8,128)S(1)} %broadcast_in_dim.3), channel_id=1, replica_groups=mesh['lat'=4,'lon'=8] {'lat','lon'}, dimensions={0} | all-to-all | bytes 262144 | tf_op jit(solution)/shard_map/all_to_all | solution.py:431
  41.8 5.5 %factor_and_basis.1 = (bf16[32,256,128]{2,1,0:T(8,128)(2,1)}, f32[32,32]{1,0:T(8,128)}) custom-call(f32[32,8,128]{2,1,0:T(8,128)S(1)} %all_to_all.5.gram_ref, bf16[272,64,128]{2,1,0:T(8,128)(2,1)S(1)} %get-tuple-element.21.split_ref), custom_call_target="tpu_custom_call" | custom-call | tf_op jit(solution)/shard_map/factor_and_basis/pallas_call | solution.py:516
  (5 shorter events, 0.1 us)
Async XLA Ops:
  0.6 2.2 %copy-start = (f32[32,256,128]{2,1,0:T(8,128)S(1)}, f32[32,256,128]{2,1,0:T(8,128)}, u32[]{:S(2)}) copy-start(f32[32,256,128]{2,1,0:T(8,128)} %field_ref.3) | copy-start | bytes 12582916
  2.9 6.5 %collective-permute-start = (f32[32,8,128]{2,1,0:T(8,128)S(1)}, f32[32,8,128]{2,1,0:T(8,128)S(1)}, u32[]{:S(2)}, u32[]{:S(2)}) collective-permute-start(f32[32,8,128]{2,1,0:T(8,128)S(1)} %get-tuple-element.14), channel_id=1, source_target_pairs={{0,8},{8,0},{16,24},{24,16},{1,9},{9,1},{17,25},{25,17},{2,10},{10... | collective-permute-start | bytes 393224 | tf_op jit(solution)/shard_map/ppermute | solution.py:425
  5.9 7.9 %copy-start.3 = (bf16[256,256]{1,0:T(8,128)(2,1)S(1)}, bf16[256,256]{1,0:T(8,128)(2,1)}, u32[]{:S(2)}) copy-start(bf16[256,256]{1,0:T(8,128)(2,1)} %constant.14.clone.main_ref) | copy-start | bytes 393220
  5.9 7.9 %copy-start.4 = (f32[1024]{0:T(1024)S(1)}, f32[1024]{0:T(1024)}, u32[]{:S(2)}) copy-start(f32[1024]{0:T(1024)} %lon_ref.3) | copy-start | bytes 12292
  5.9 7.9 %copy-start.5 = (f32[1024]{0:T(1024)S(1)}, f32[1024]{0:T(1024)}, u32[]{:S(2)}) copy-start(f32[1024]{0:T(1024)} %lat_ref.3) | copy-start | bytes 12292
  5.9 3.5 %collective-permute-start.1 = (f32[32,8,128]{2,1,0:T(8,128)S(1)}, f32[32,8,128]{2,1,0:T(8,128)S(1)}, u32[]{:S(2)}, u32[]{:S(2)}) collective-permute-start(f32[32,8,128]{2,1,0:T(8,128)S(1)} %get-tuple-element.15), channel_id=1, source_target_pairs={{8,16},{16,8},{9,17},{17,9},{10,18},{18,10},{11,19},{19,11},{12,20... | collective-permute-start | bytes 393224 | tf_op jit(solution)/shard_map/ppermute | solution.py:425
  9.7 12.3 %collective-permute-start.2 = (f32[17,32,128]{2,1,0:T(8,128)S(1)}, f32[17,32,128]{2,1,0:T(8,128)S(1)}, u32[]{:S(2)}, u32[]{:S(2)}) collective-permute-start(f32[17,32,128]{2,1,0:T(8,128)S(1)} %get-tuple-element.18), channel_id=1, source_target_pairs={{0,1},{1,0},{2,3},{3,2},{4,5},{5,4},{6,7},{7,6},{8,9},{9,8},{10,11... | collective-permute-start | bytes 835592 | tf_op jit(solution)/shard_map/ppermute | solution.py:425
  9.7 12.3 %collective-permute-start.3 = (f32[17,32,128]{2,1,0:T(8,128)S(1)}, f32[17,32,128]{2,1,0:T(8,128)S(1)}, u32[]{:S(2)}, u32[]{:S(2)}) collective-permute-start(f32[17,32,128]{2,1,0:T(8,128)S(1)} %get-tuple-element.19), channel_id=1, source_target_pairs={{1,2},{2,1},{3,4},{4,3},{5,6},{6,5},{7,0},{0,7},{9,10},{10,9},{11,... | collective-permute-start | bytes 835592 | tf_op jit(solution)/shard_map/ppermute | solution.py:425
  13.8 8.2 %copy-start.1 = (bf16[512,512]{1,0:T(8,128)(2,1)S(1)}, bf16[512,512]{1,0:T(8,128)(2,1)}, u32[]{:S(2)}) copy-start(bf16[512,512]{1,0:T(8,128)(2,1)} %constant.15.clone.edge_ref) | copy-start | bytes 1572868
  13.8 8.2 %copy-start.2 = (bf16[512,256]{1,0:T(8,128)(2,1)S(1)}, bf16[512,256]{1,0:T(8,128)(2,1)}, u32[]{:S(2)}) copy-start(bf16[512,256]{1,0:T(8,128)(2,1)} %constant.16.clone.again_ref) | copy-start | bytes 786436

commit v7 on v6

--- a/solution.py
+++ b/solution.py
@@ -20,10 +20,11 @@
 VMEM_BYTES = 24 * 1024 * 1024
 
 
-def area_weight(first_row, row_count, total_rows):
-    row_index = (jnp.arange(row_count) + first_row).astype(jnp.float32)
-    latitude = (-90.0 + (row_index + 0.5) * (180.0 / total_rows)) * (math.pi / 180.0)
-    return jnp.sqrt(jnp.cos(latitude))
+def area_weight(total_rows):
+    row_index = np.arange(total_rows).astype(np.float32)
+    step = np.float32(180.0 / total_rows)
+    latitude = np.float32(-90.0) + (row_index + np.float32(0.5)) * step
+    return np.sqrt(np.cos(latitude * np.float32(math.pi / 180.0))).astype(np.float32)
 
 
 def hi_lo(values):
@@ -77,7 +78,9 @@
     second_ref[...] = jnp.where(lat_even, north, south)
 
 
-def strip_kernel(span, field_ref, ext_ref, strip_ref):
+def strip_kernel(
+    span, lon_ref, lat_ref, weight_ref, field_ref, ext_ref, strip_ref, strip_rates_ref
+):
     snaps, rows, _ = field_ref.shape
 
     def turn(at, carry):
@@ -104,6 +107,19 @@
         return carry
 
     lax.fori_loop(0, span, pack, 0, unroll=span // 2)
+    lane_group = lax.broadcasted_iota(jnp.int32, (8, LANES), 1) // STRIP
+    rates = rate_reader(rows, (lon_ref, lat_ref, weight_ref))
+    for at in range(span):
+        values_at = [jnp.zeros((8, LANES), jnp.float32)] * 3
+        for group in range(GROUPS):
+            here = lane_group == group
+            row = group * span + at
+            values = rates(row)
+            if row < HALO or row >= HALO + rows:
+                values[2] = 0.0
+            values_at = [jnp.where(here, value, old) for value, old in zip(values, values_at)]
+        for kind in range(3):
+            strip_rates_ref[kind, at] = values_at[kind]
 
 
 def message_kernel(
@@ -137,11 +153,13 @@
         second_ref[at] = jnp.where(lon_even, westward, eastward)
 
 
-def stencil_row(center, pairs, zonal, zonal_rate, merid_rate):
+def stencil_row(center, pairs, zonal, zonal_rate, merid_rate, weight=None):
     merid = stencil_weights[1] * pairs[0]
     for offset in range(2, 5):
         merid = merid + stencil_weights[offset] * pairs[offset - 1]
     scale = 1.0 + stencil_weights[0] * merid_rate
+    if weight is not None:
+        scale, merid_rate, zonal_rate = scale * weight, merid_rate * weight, zonal_rate * weight
     return scale * center + merid_rate * merid + zonal_rate * zonal
 
 
@@ -174,53 +192,35 @@
     for at in range(span):
         here = at + 4
         pairs = [row(here + offset) + row(here - offset) for offset in range(1, 5)]
-        values = rates(begin + at)
-        store(at, stencil_row(row(here), pairs, part[at], values[0], values[1]), values)
+        store(at, stencil_row(row(here), pairs, part[at], *rates(begin + at)))
 
 
 def tile_kernel(span, lon_ref, lat_ref, weight_ref, ext_ref, main_ref, twice_ref, once_ref):
     snaps = ext_ref.shape[1]
     total = span * GROUPS
     rows = total - 2 * HALO
-    rates = rate_reader(rows, (lon_ref, lat_ref, weight_ref))
-    chunk = total // 2
+    plain = rate_reader(rows, (lon_ref, lat_ref))
+    weighted = rate_reader(rows, (lon_ref, lat_ref, weight_ref))
     ends = jnp.zeros((4, TILE, LANES), jnp.float32)
     once_ref[:4] = ends
     once_ref[total + 4 :] = ends
+    outside = jnp.zeros((HALO, TILE, LANES), jnp.float32)
 
     def one_tile(tile, carry):
         snap = pl.ds(pl.multiple_of(tile * TILE, TILE), TILE)
 
-        def first_pass(part, carry):
-            begin = part * chunk
-            center = ext_ref[pl.ds(4 + begin, chunk), snap].reshape(chunk * TILE, LANES)
-            part = zonal_terms(hi_lo(center), main_ref[...]).reshape(chunk, TILE, LANES)
-
-            def load(at):
-                return ext_ref[at, snap]
-
-            def store(at, value, _):
-                once_ref[4 + begin + at] = value
-
-            stencil_rows(load, begin, chunk, part, rates, store)
-            return carry
-
-        def second_pass(part, carry):
-            begin = part * chunk
-            center = once_ref[pl.ds(4 + begin, chunk)].reshape(chunk * TILE, LANES)
-            part = zonal_terms(hi_lo(center), main_ref[...]).reshape(chunk, TILE, LANES)
-
-            def load(at):
-                return once_ref[at]
-
-            def store(at, value, values):
-                twice_ref[begin + at, snap] = values[2] * value
-
-            stencil_rows(load, begin, chunk, part, rates, store)
-            return carry
-
-        lax.fori_loop(0, 2, first_pass, 0)
-        outside = jnp.zeros((HALO, TILE, LANES), jnp.float32)
+        def one_pass(load, rates, store):
+            center = load(slice(4, 4 + total)).reshape(total * TILE, LANES)
+            part = zonal_terms(hi_lo(center), main_ref[...]).reshape(total, TILE, LANES)
+            stencil_rows(load, 0, total, part, rates, store)
+
+        def store_once(at, value):
+            once_ref[4 + at] = value
+
+        def store_twice(at, value):
+            twice_ref[at, snap] = value
+
+        one_pass(lambda at: ext_ref[at, snap], plain, store_once)
 
         @pl.when(lax.axis_index("lat") == 0)
         def _():
@@ -230,7 +230,7 @@
         def _():
             once_ref[4 + HALO + rows : 4 + total] = outside
 
-        lax.fori_loop(0, 2, second_pass, 0)
+        one_pass(lambda at: once_ref[at], weighted, store_twice)
         return carry
 
     lax.fori_loop(0, snaps // TILE, one_tile, 0)
@@ -247,11 +247,9 @@
 
 def rim_kernel(
     span,
-    lon_ref,
-    lat_ref,
-    weight_ref,
     twice_ref,
     strip_ref,
+    strip_rates_ref,
     first_ref,
     second_ref,
     edge_ref,
@@ -262,30 +260,14 @@
     side_ref,
     added_ref,
     rim_ref,
-    strip_rates_ref,
 ):
-    total, both, _ = split_ref.shape
-    rows = total - 2 * HALO
+    both = split_ref.shape[1]
     snaps = both // 2
     half = span // 2
     lon_even = lax.axis_index("lon") % 2 == 0
     lane = lax.broadcasted_iota(jnp.int32, (TILE, LANES), 1)
     left = lane % STRIP < HALO
     rim = (lane < HALO) | (lane >= LANES - HALO)
-    group_of = lax.broadcasted_iota(jnp.int32, (8, LANES), 1) // STRIP
-    rates = rate_reader(rows, (lon_ref, lat_ref, weight_ref))
-    for at in range(span):
-        packed = [jnp.zeros((8, LANES), jnp.float32)] * 3
-        for group in range(GROUPS):
-            here = group_of == group
-            row = group * span + at
-            values = rates(row)
-            if row < HALO or row >= HALO + rows:
-                values[2] = 0.0
-            packed = [jnp.where(here, value, old) for value, old in zip(values, packed)]
-        for kind in range(3):
-            strip_rates_ref[kind, at] = packed[kind]
-
     def strip_rate(kind, at):
         return jnp.concatenate([strip_rates_ref[kind, at]] * (TILE // 8), axis=0)
 
@@ -412,7 +394,7 @@
         basis_ref[:, pl.ds(begin, 16), :] = turned.astype(jnp.bfloat16)
         return carry
 
-    lax.fori_loop(0, basis_ref.shape[1] // 16, body, 0)
+    lax.fori_loop(0, basis_ref.shape[1] // 16, body, 0, unroll=8)
 
 
 def pair_permutes(values, axis, periodic):
@@ -457,14 +439,15 @@
         name="lat_messages",
     )(field)
     low, high = pair_permutes([first, second], "lat", False)
-    turned, packed = pl.pallas_call(
+    weight = area_weight(total_rows)
+    turned, packed, strip_rates = pl.pallas_call(
         functools.partial(strip_kernel, span),
-        in_specs=[whole()],
-        out_specs=[whole()] * 2,
-        out_shape=[ext, strip],
+        in_specs=[whole(pltpu.SMEM)] * 3 + [whole()],
+        out_specs=[whole()] * 3,
+        out_shape=[ext, strip, jax.ShapeDtypeStruct((3, span, 8, cols), f32)],
         compiler_params=limits,
         name="turn_and_pack",
-    )(field)
+    )(lon_rate, lat_rate, weight, field)
     turned, packed, first, second = pl.pallas_call(
         functools.partial(message_kernel, span),
         in_specs=[whole()] * 4,
@@ -475,8 +458,6 @@
         name="lon_messages",
     )(turned, packed, low, high)
     first, second = pair_permutes([first, second], "lon", True)
-
-    weight = area_weight(0, total_rows, total_rows)
 
     main, edge, again = zonal_matrices()
     bf16 = jnp.bfloat16
@@ -494,7 +475,7 @@
     )(lon_rate, lat_rate, weight, turned, main)
     split, gram = pl.pallas_call(
         functools.partial(rim_kernel, span),
-        in_specs=[whole(pltpu.SMEM)] * 3 + [whole()] * 6,
+        in_specs=[whole()] * 7,
         out_specs=[whole(), whole()],
         out_shape=[
             jax.ShapeDtypeStruct((total, 2 * snaps, cols), bf16),
@@ -505,14 +486,13 @@
             pltpu.VMEM((span, TILE, cols), f32),
             pltpu.VMEM((span + 8, TILE, cols), f32),
             pltpu.VMEM((span, snaps, cols), f32),
-            pltpu.VMEM((3, span, 8, cols), f32),
         ],
         compiler_params=limits,
         name="rim_and_gram",
-    )(lon_rate, lat_rate, weight, twice, packed, first, second, edge, again)
+    )(twice, packed, strip_rates, first, second, edge, again)
 
     grams = gather_all(gram)
-    block = 64
+    block = 128
     basis, factor = pl.pallas_call(
         functools.partial(basis_kernel, math.sqrt(total_cells)),
         grid=(rows // block,),

time: 47.4 us -> 45.4 us (0.958)
  Pallas kernels: 21.8 us -> 19 us
  local copies, waits for them, and re-layouts: 2.22 us -> 4.26 us
  waiting for transfers between devices: 0.59 us -> 0.01 us
    unnamed x12 -> x16, local copies, waits for them, and re-layouts: 2.21 us -> 4.25 us
    pallas_call x1, Pallas kernels: 5.49 us -> 3.45 us  [shards(): pl.pallas_call(functools.partial(basis_kernel, math.sqrt(total_cells)), g...]
    pallas_call x1, Pallas kernels: 8.18 us -> 7.31 us  [shards(): pl.pallas_call(functools.partial(tile_kernel, span), in_specs=[whole(pltp...]
    ppermute x2, waiting for transfers between devices: 0.59 us -> 0.01 us  [pair_permutes(): lax.ppermute(values[0], axis, inner)]
  transfers between devices with their start and end apart: 4 -> 4, of which waited for: 1 -> 0; matrix products, arithmetic and copies ran while one was open for 0% -> 0% of each run, Pallas kernels for 22% -> 23%
where the time goes in v7:
time: 45.4 us; the launch traced here: 45.2 us
  Pallas kernels  19 us (42%)
  blocking collectives  13.6 us (30%)
  starting transfers between devices  7.57 us (17%)
  local copies, waits for them, and re-layouts  4.26 us (9%)
  between operations  0.76 us (2%)
    all_to_all x1, blocking collectives, gather_all(): lax.all_to_all(jnp.broadcast_to(values, (count,) + values.shape), axes, 0...  13.6 us
    pallas_call x1, Pallas kernels, shards(): pl.pallas_call(functools.partial(tile_kernel, span), in_specs=[whole(pltp...  7.31 us
    pallas_call x1, Pallas kernels, shards(): pl.pallas_call(functools.partial(rim_kernel, span), in_specs=[whole()] *...  4.64 us
    ppermute x2, starting transfers between devices, pair_permutes(): lax.ppermute(values[1], axis, outer)  4.49 us
    unnamed x16, local copies, waits for them, and re-layouts  4.25 us
    pallas_call x1, Pallas kernels, shards(): pl.pallas_call(functools.partial(basis_kernel, math.sqrt(total_cells)), g...  3.45 us
    pallas_call x1, Pallas kernels, shards(): pl.pallas_call(functools.partial(strip_kernel, span), in_specs=[whole(plt...  3.28 us
    ppermute x2, starting transfers between devices, pair_permutes(): lax.ppermute(values[0], axis, inner)  3.07 us
  transfers between devices with their start and end apart: 4, of which 0 were waited for; matrix products, arithmetic and copies ran while one was open for 0% of the time, Pallas kernels for 23%

profile of v7, /device:TPU:0, one launch (start us, length us, event | category | flops | bytes accessed | tf_op | source)
XLA Modules:
  0.0 45.2 jit_solution(6227796121237796586)
XLA Ops:
  0.6 0.0 copy-start
  0.6 2.2 %copy-done = f32[32,256,128]{2,1,0:T(8,128)S(1)} copy-done((f32[32,256,128]{2,1,0:T(8,128)S(1)}, f32[32,256,128]{2,1,0:T(8,128)}, u32[]{:S(2)}) %copy-start) | copy-done | bytes 4194328
  2.9 3.0 %collective-permute-start = (f32[32,8,128]{2,1,0:T(8,128)S(1)}, f32[32,8,128]{2,1,0:T(8,128)S(1)}, u32[]{:S(2)}, u32[]{:S(2)}) collective-permute-start(f32[32,8,128]{2,1,0:T(8,128)S(1)} %get-tuple-element.15), channel_id=1, source_target_pairs={{0,8},{8,0},{16,24},{24,16},{1,9},{9,1},{17,25},{25,17},{2,10},{10... | collective-permute-start | bytes 393224 | tf_op jit(solution)/shard_map/ppermute | solution.py:407
  5.9 0.8 %collective-permute-start.1 = (f32[32,8,128]{2,1,0:T(8,128)S(1)}, f32[32,8,128]{2,1,0:T(8,128)S(1)}, u32[]{:S(2)}, u32[]{:S(2)}) collective-permute-start(f32[32,8,128]{2,1,0:T(8,128)S(1)} %get-tuple-element.16), channel_id=1, source_target_pairs={{8,16},{16,8},{9,17},{17,9},{10,18},{18,10},{11,19},{19,11},{12,20... | collective-permute-start | bytes 393224 | tf_op jit(solution)/shard_map/ppermute | solution.py:407
  6.7 0.0 copy-done.1
  6.7 0.0 copy-start.5
  6.7 0.7 %copy-done.5 = f32[1024]{0:T(1024)S(1)} copy-done((f32[1024]{0:T(1024)S(1)}, f32[1024]{0:T(1024)}, u32[]{:S(2)}) %copy-start.5) | copy-done | bytes 4120
  7.4 0.7 %copy-done.6 = f32[1024]{0:T(1024)S(1)} copy-done((f32[1024]{0:T(1024)S(1)}, f32[1024]{0:T(1024)}, u32[]{:S(2)}) %copy-start.6) | copy-done | bytes 4120
  8.0 0.7 %copy-done.7 = f32[1024]{0:T(1024)S(1)} copy-done((f32[1024]{0:T(1024)S(1)}, f32[1024]{0:T(1024)}, u32[]{:S(2)}) %copy-start.7) | copy-done | bytes 4120
  8.7 3.3 %turn_and_pack.1 = (f32[280,32,128]{2,1,0:T(8,128)S(1)}, f32[34,32,128]{2,1,0:T(8,128)S(1)}, f32[3,34,8,128]{3,2,1,0:T(8,128)S(1)}) custom-call(f32[1024]{0:T(1024)S(1)} %copy-done.5, f32[1024]{0:T(1024)S(1)} %copy-done.6, f32[1024]{0:T(1024)S(1)} %copy-done.7, f32[32,256,128]{2,1,0:T(8,128)S(1)} %copy-done.1), custom_call_target="tpu_custom_call" | custom-call | tf_op jit(solution)/shard_map/turn_and_pack/pallas_call | solution.py:443
  12.0 0.0 collective-permute-done.low_ref
  12.0 0.0 collective-permute-done.1.high_ref
  12.0 0.3 lon_messages.1
  12.3 0.1 collective-permute-start.2
  12.4 3.7 %collective-permute-start.3 = (f32[17,32,128]{2,1,0:T(8,128)S(1)}, f32[17,32,128]{2,1,0:T(8,128)S(1)}, u32[]{:S(2)}, u32[]{:S(2)}) collective-permute-start(f32[17,32,128]{2,1,0:T(8,128)S(1)} %get-tuple-element.21), channel_id=1, source_target_pairs={{1,2},{2,1},{3,4},{4,3},{5,6},{6,5},{7,0},{0,7},{9,10},{10,9},{11,... | collective-permute-start | bytes 835592 | tf_op jit(solution)/shard_map/ppermute | solution.py:407
  16.1 0.0 copy-done.4
  16.1 7.3 %both_passes.1.twice_ref = f32[272,32,128]{2,1,0:T(8,128)S(1)} custom-call(f32[1024]{0:T(1024)S(1)} %copy-done.5, f32[1024]{0:T(1024)S(1)} %copy-done.6, f32[1024]{0:T(1024)S(1)} %copy-done.7, f32[280,32,128]{2,1,0:T(8,128)S(1)} %get-tuple-element.17.ext_ref, bf16[256,256]{1,0:T(8,128)(2,1)S(1)} %copy-done.4), custom_call_target="tpu_custom_call" | custom-call | flops 104857600 | bytes 8388608 | tf_op jit(solution)/shard_map/both_passes/pallas_call | solution.py:464
  23.5 0.0 collective-permute-done.2.first_ref
  23.5 0.0 collective-permute-done.3.second_ref
  23.5 0.0 copy-done.2
  23.5 0.0 copy-done.3
  23.5 4.6 %rim_and_gram.1 = (bf16[272,64,128]{2,1,0:T(8,128)(2,1)S(1)}, f32[8,128]{1,0:T(8,128)S(1)}) custom-call(f32[272,32,128]{2,1,0:T(8,128)S(1)} %both_passes.1.twice_ref, f32[34,32,128]{2,1,0:T(8,128)S(1)} %get-tuple-element.18.strip_ref, f32[3,34,8,128]{3,2,1,0:T(8,128)S(1)} %get-tuple-element.19.strip_rates_ref, ...), custom_call_target="tpu_custom_call" | custom-call | tf_op jit(solution)/shard_map/rim_and_gram/pallas_call | solution.py:476
  28.2 13.6 %all_to_all.5.gram_ref = f32[32,8,128]{2,1,0:T(8,128)S(1)} all-to-all(f32[32,8,128]{2,1,0:T(8,128)S(1)} %broadcast_in_dim.3), channel_id=1, replica_groups=mesh['lat'=4,'lon'=8] {'lat','lon'}, dimensions={0} | all-to-all | bytes 262144 | tf_op jit(solution)/shard_map/all_to_all | solution.py:413
  41.7 3.5 %factor_and_basis.1 = (bf16[32,256,128]{2,1,0:T(8,128)(2,1)}, f32[32,32]{1,0:T(8,128)}) custom-call(f32[32,8,128]{2,1,0:T(8,128)S(1)} %all_to_all.5.gram_ref, bf16[272,64,128]{2,1,0:T(8,128)(2,1)S(1)} %get-tuple-element.23.split_ref), custom_call_target="tpu_custom_call" | custom-call | tf_op jit(solution)/shard_map/factor_and_basis/pallas_call | solution.py:496
  (8 shorter events, 0.1 us)
Async XLA Ops:
  0.6 2.2 %copy-start = (f32[32,256,128]{2,1,0:T(8,128)S(1)}, f32[32,256,128]{2,1,0:T(8,128)}, u32[]{:S(2)}) copy-start(f32[32,256,128]{2,1,0:T(8,128)} %field_ref.3) | copy-start | bytes 12582916
  2.8 3.8 %copy-start.1 = (f32[32,256,128]{2,1,0:T(8,128)S(1)}, f32[32,256,128]{2,1,0:T(8,128)}, u32[]{:S(2)}) copy-start(f32[32,256,128]{2,1,0:T(8,128)} %field_ref.3) | copy-start | bytes 12582916
  2.9 9.2 %collective-permute-start = (f32[32,8,128]{2,1,0:T(8,128)S(1)}, f32[32,8,128]{2,1,0:T(8,128)S(1)}, u32[]{:S(2)}, u32[]{:S(2)}) collective-permute-start(f32[32,8,128]{2,1,0:T(8,128)S(1)} %get-tuple-element.15), channel_id=1, source_target_pairs={{0,8},{8,0},{16,24},{24,16},{1,9},{9,1},{17,25},{25,17},{2,10},{10... | collective-permute-start | bytes 393224 | tf_op jit(solution)/shard_map/ppermute | solution.py:407
  5.9 10.3 %copy-start.4 = (bf16[256,256]{1,0:T(8,128)(2,1)S(1)}, bf16[256,256]{1,0:T(8,128)(2,1)}, u32[]{:S(2)}) copy-start(bf16[256,256]{1,0:T(8,128)(2,1)} %constant.9.clone.main_ref) | copy-start | bytes 393220
  5.9 6.2 %collective-permute-start.1 = (f32[32,8,128]{2,1,0:T(8,128)S(1)}, f32[32,8,128]{2,1,0:T(8,128)S(1)}, u32[]{:S(2)}, u32[]{:S(2)}) collective-permute-start(f32[32,8,128]{2,1,0:T(8,128)S(1)} %get-tuple-element.16), channel_id=1, source_target_pairs={{8,16},{16,8},{9,17},{17,9},{10,18},{18,10},{11,19},{19,11},{12,20... | collective-permute-start | bytes 393224 | tf_op jit(solution)/shard_map/ppermute | solution.py:407
  6.7 0.7 %copy-start.5 = (f32[1024]{0:T(1024)S(1)}, f32[1024]{0:T(1024)}, u32[]{:S(2)}) copy-start(f32[1024]{0:T(1024)} %lon_ref.3) | copy-start | bytes 12292
  7.4 0.7 %copy-start.6 = (f32[1024]{0:T(1024)S(1)}, f32[1024]{0:T(1024)}, u32[]{:S(2)}) copy-start(f32[1024]{0:T(1024)} %lat_ref.3) | copy-start | bytes 12292
  8.0 0.7 %copy-start.7 = (f32[1024]{0:T(1024)S(1)}, f32[1024]{0:T(1024)}, u32[]{:S(2)}) copy-start(f32[1024]{0:T(1024)} %constant.8.clone.weight_ref) | copy-start | bytes 12292
  12.3 11.1 %collective-permute-start.2 = (f32[17,32,128]{2,1,0:T(8,128)S(1)}, f32[17,32,128]{2,1,0:T(8,128)S(1)}, u32[]{:S(2)}, u32[]{:S(2)}) collective-permute-start(f32[17,32,128]{2,1,0:T(8,128)S(1)} %get-tuple-element.20), channel_id=1, source_target_pairs={{0,1},{1,0},{2,3},{3,2},{4,5},{5,4},{6,7},{7,6},{8,9},{9,8},{10,11... | collective-permute-start | bytes 835592 | tf_op jit(solution)/shard_map/ppermute | solution.py:407
  12.4 11.0 %collective-permute-start.3 = (f32[17,32,128]{2,1,0:T(8,128)S(1)}, f32[17,32,128]{2,1,0:T(8,128)S(1)}, u32[]{:S(2)}, u32[]{:S(2)}) collective-permute-start(f32[17,32,128]{2,1,0:T(8,128)S(1)} %get-tuple-element.21), channel_id=1, source_target_pairs={{1,2},{2,1},{3,4},{4,3},{5,6},{6,5},{7,0},{0,7},{9,10},{10,9},{11,... | collective-permute-start | bytes 835592 | tf_op jit(solution)/shard_map/ppermute | solution.py:407
  16.1 7.3 %copy-start.2 = (bf16[512,512]{1,0:T(8,128)(2,1)S(1)}, bf16[512,512]{1,0:T(8,128)(2,1)}, u32[]{:S(2)}) copy-start(bf16[512,512]{1,0:T(8,128)(2,1)} %constant.10.clone.edge_ref) | copy-start | bytes 1572868
  16.1 7.4 %copy-start.3 = (bf16[512,256]{1,0:T(8,128)(2,1)S(1)}, bf16[512,256]{1,0:T(8,128)(2,1)}, u32[]{:S(2)}) copy-start(bf16[512,256]{1,0:T(8,128)(2,1)} %constant.11.clone.again_ref) | copy-start | bytes 786436

commit v8 on v7

--- a/solution.py
+++ b/solution.py
@@ -16,7 +16,7 @@
 LANES = 128
 GROUPS = LANES // STRIP
 TILE = 16
-PIVOTS = 8
+PIVOTS = 16
 VMEM_BYTES = 24 * 1024 * 1024
 
 
@@ -78,9 +78,7 @@
     second_ref[...] = jnp.where(lat_even, north, south)
 
 
-def strip_kernel(
-    span, lon_ref, lat_ref, weight_ref, field_ref, ext_ref, strip_ref, strip_rates_ref
-):
+def strip_kernel(span, field_ref, ext_ref, strip_ref):
     snaps, rows, _ = field_ref.shape
 
     def turn(at, carry):
@@ -107,19 +105,6 @@
         return carry
 
     lax.fori_loop(0, span, pack, 0, unroll=span // 2)
-    lane_group = lax.broadcasted_iota(jnp.int32, (8, LANES), 1) // STRIP
-    rates = rate_reader(rows, (lon_ref, lat_ref, weight_ref))
-    for at in range(span):
-        values_at = [jnp.zeros((8, LANES), jnp.float32)] * 3
-        for group in range(GROUPS):
-            here = lane_group == group
-            row = group * span + at
-            values = rates(row)
-            if row < HALO or row >= HALO + rows:
-                values[2] = 0.0
-            values_at = [jnp.where(here, value, old) for value, old in zip(values, values_at)]
-        for kind in range(3):
-            strip_rates_ref[kind, at] = values_at[kind]
 
 
 def message_kernel(
@@ -195,7 +180,9 @@
         store(at, stencil_row(row(here), pairs, part[at], *rates(begin + at)))
 
 
-def tile_kernel(span, lon_ref, lat_ref, weight_ref, ext_ref, main_ref, twice_ref, once_ref):
+def tile_kernel(
+    span, lon_ref, lat_ref, weight_ref, ext_ref, main_ref, twice_ref, strip_rates_ref, once_ref
+):
     snaps = ext_ref.shape[1]
     total = span * GROUPS
     rows = total - 2 * HALO
@@ -237,6 +224,18 @@
     outside = jnp.zeros((HALO, snaps, LANES), jnp.float32)
     twice_ref[:HALO] = outside
     twice_ref[HALO + rows :] = outside
+    lane_group = lax.broadcasted_iota(jnp.int32, (8, LANES), 1) // STRIP
+    for at in range(span):
+        values_at = [jnp.zeros((8, LANES), jnp.float32)] * 3
+        for group in range(GROUPS):
+            here = lane_group == group
+            row = group * span + at
+            values = weighted(row)
+            if row < HALO or row >= HALO + rows:
+                values[2] = 0.0
+            values_at = [jnp.where(here, value, old) for value, old in zip(values, values_at)]
+        for kind in range(3):
+            strip_rates_ref[kind, at] = values_at[kind]
 
 
 def close_ends(strip_ref, span):
@@ -440,14 +439,14 @@
     )(field)
     low, high = pair_permutes([first, second], "lat", False)
     weight = area_weight(total_rows)
-    turned, packed, strip_rates = pl.pallas_call(
+    turned, packed = pl.pallas_call(
         functools.partial(strip_kernel, span),
-        in_specs=[whole(pltpu.SMEM)] * 3 + [whole()],
-        out_specs=[whole()] * 3,
-        out_shape=[ext, strip, jax.ShapeDtypeStruct((3, span, 8, cols), f32)],
+        in_specs=[whole()],
+        out_specs=[whole()] * 2,
+        out_shape=[ext, strip],
         compiler_params=limits,
         name="turn_and_pack",
-    )(lon_rate, lat_rate, weight, field)
+    )(field)
     turned, packed, first, second = pl.pallas_call(
         functools.partial(message_kernel, span),
         in_specs=[whole()] * 4,
@@ -461,11 +460,14 @@
 
     main, edge, again = zonal_matrices()
     bf16 = jnp.bfloat16
-    twice = pl.pallas_call(
+    twice, strip_rates = pl.pallas_call(
         functools.partial(tile_kernel, span),
         in_specs=[whole(pltpu.SMEM)] * 3 + [whole()] * 2,
-        out_specs=whole(),
-        out_shape=jax.ShapeDtypeStruct((total, snaps, cols), f32),
+        out_specs=[whole()] * 2,
+        out_shape=[
+            jax.ShapeDtypeStruct((total, snaps, cols), f32),
+            jax.ShapeDtypeStruct((3, span, 8, cols), f32),
+        ],
         scratch_shapes=[pltpu.VMEM((total + 8, TILE, cols), f32)],
         compiler_params=limits,
         cost_estimate=pl.CostEstimate(

time: 45.4 us -> 44.2 us (0.974)
  local copies, waits for them, and re-layouts: 4.26 us -> 2.22 us
  blocking collectives: 13.6 us -> 14.5 us
  Pallas kernels: 19 us -> 18.2 us
  waiting for transfers between devices: 0.01 us -> 0.58 us
    unnamed x16 -> x14, local copies, waits for them, and re-layouts: 4.25 us -> 2.2 us
    pallas_call x1, Pallas kernels: 3.28 us -> 2.1 us  [shards(): pl.pallas_call(functools.partial(strip_kernel, span), in_specs=[whole()],...]
    all_to_all x1, blocking collectives: 13.6 us -> 14.5 us  [gather_all(): lax.all_to_all(jnp.broadcast_to(values, (count,) + values.shape), axes, 0...]
    ppermute x2, waiting for transfers between devices: 0.01 us -> 0.57 us  [pair_permutes(): lax.ppermute(values[0], axis, inner)]
    pallas_call x1, Pallas kernels: 7.31 us -> 7.79 us  [shards(): pl.pallas_call(functools.partial(tile_kernel, span), in_specs=[whole(pltp...]
  transfers between devices with their start and end apart: 4 -> 4, of which waited for: 0 -> 1; matrix products, arithmetic and copies ran while one was open for 0% -> 0% of each run, Pallas kernels for 23% -> 22%
where the time goes in v8:
time: 44.2 us; the launch traced here: 44.1 us
  Pallas kernels  18.2 us (41%)
  blocking collectives  14.5 us (33%)
  starting transfers between devices  7.83 us (18%)
  local copies, waits for them, and re-layouts  2.22 us (5%)
  between operations  0.73 us (2%)
  waiting for transfers between devices  0.58 us (1%)
    all_to_all x1, blocking collectives, gather_all(): lax.all_to_all(jnp.broadcast_to(values, (count,) + values.shape), axes, 0...  14.5 us
    pallas_call x1, Pallas kernels, shards(): pl.pallas_call(functools.partial(tile_kernel, span), in_specs=[whole(pltp...  7.79 us
    ppermute x2, starting transfers between devices, pair_permutes(): lax.ppermute(values[1], axis, outer)  4.75 us
    pallas_call x1, Pallas kernels, shards(): pl.pallas_call(functools.partial(rim_kernel, span), in_specs=[whole()] *...  4.6 us
    pallas_call x1, Pallas kernels, shards(): pl.pallas_call(functools.partial(basis_kernel, math.sqrt(total_cells)), g...  3.36 us
    ppermute x2, starting transfers between devices, pair_permutes(): lax.ppermute(values[0], axis, inner)  3.07 us
    unnamed x14, local copies, waits for them, and re-layouts  2.2 us
    pallas_call x1, Pallas kernels, shards(): pl.pallas_call(functools.partial(strip_kernel, span), in_specs=[whole()],...  2.1 us
  transfers between devices with their start and end apart: 4, of which 1 were waited for; matrix products, arithmetic and copies ran while one was open for 0% of the time, Pallas kernels for 22%

profile of v8, /device:TPU:0, one launch (start us, length us, event | category | flops | bytes accessed | tf_op | source)
XLA Modules:
  0.0 44.1 jit_solution(10912066561144378657)
XLA Ops:
  0.6 0.0 copy-start
  0.6 2.2 %copy-done = f32[32,256,128]{2,1,0:T(8,128)S(1)} copy-done((f32[32,256,128]{2,1,0:T(8,128)S(1)}, f32[32,256,128]{2,1,0:T(8,128)}, u32[]{:S(2)}) %copy-start) | copy-done | bytes 4194328
  2.9 3.0 %collective-permute-start = (f32[32,8,128]{2,1,0:T(8,128)S(1)}, f32[32,8,128]{2,1,0:T(8,128)S(1)}, u32[]{:S(2)}, u32[]{:S(2)}) collective-permute-start(f32[32,8,128]{2,1,0:T(8,128)S(1)} %get-tuple-element.16), channel_id=1, source_target_pairs={{0,8},{8,0},{16,24},{24,16},{1,9},{9,1},{17,25},{25,17},{2,10},{10... | collective-permute-start | bytes 393224 | tf_op jit(solution)/shard_map/ppermute | solution.py:406
  5.9 0.0 copy-start.3
  5.9 0.0 copy-start.4
  5.9 0.8 %collective-permute-start.1 = (f32[32,8,128]{2,1,0:T(8,128)S(1)}, f32[32,8,128]{2,1,0:T(8,128)S(1)}, u32[]{:S(2)}, u32[]{:S(2)}) collective-permute-start(f32[32,8,128]{2,1,0:T(8,128)S(1)} %get-tuple-element.17), channel_id=1, source_target_pairs={{8,16},{16,8},{9,17},{17,9},{10,18},{18,10},{11,19},{19,11},{12,20... | collective-permute-start | bytes 393224 | tf_op jit(solution)/shard_map/ppermute | solution.py:406
  6.7 2.1 %turn_and_pack.1 = (f32[280,32,128]{2,1,0:T(8,128)S(1)}, f32[34,32,128]{2,1,0:T(8,128)S(1)}) custom-call(f32[32,256,128]{2,1,0:T(8,128)S(1)} %copy-done), custom_call_target="tpu_custom_call" | custom-call | tf_op jit(solution)/shard_map/turn_and_pack/pallas_call | solution.py:442
  8.8 0.6 %collective-permute-done.low_ref = f32[32,8,128]{2,1,0:T(8,128)S(1)} collective-permute-done((f32[32,8,128]{2,1,0:T(8,128)S(1)}, f32[32,8,128]{2,1,0:T(8,128)S(1)}, u32[]{:S(2)}, u32[]{:S(2)}) %collective-permute-start) | collective-permute-done | bytes 131104 | tf_op jit(solution)/shard_map/ppermute | solution.py:406
  9.4 0.0 collective-permute-done.1.high_ref
  9.4 0.3 lon_messages.1
  9.7 0.1 collective-permute-start.2
  9.7 4.0 %collective-permute-start.3 = (f32[17,32,128]{2,1,0:T(8,128)S(1)}, f32[17,32,128]{2,1,0:T(8,128)S(1)}, u32[]{:S(2)}, u32[]{:S(2)}) collective-permute-start(f32[17,32,128]{2,1,0:T(8,128)S(1)} %get-tuple-element.23), channel_id=1, source_target_pairs={{1,2},{2,1},{3,4},{4,3},{5,6},{6,5},{7,0},{0,7},{9,10},{10,9},{11,... | collective-permute-start | bytes 835592 | tf_op jit(solution)/shard_map/ppermute | solution.py:406
  13.7 0.0 copy-done.3
  13.7 0.0 copy-done.4
  13.7 0.0 copy-done.5
  13.7 0.0 copy-done.6
  13.7 7.8 %both_passes.1 = (f32[272,32,128]{2,1,0:T(8,128)S(1)}, f32[3,34,8,128]{3,2,1,0:T(8,128)S(1)}) custom-call(f32[1024]{0:T(1024)S(1)} %copy-done.4, f32[1024]{0:T(1024)S(1)} %copy-done.5, f32[1024]{0:T(1024)S(1)} %copy-done.6, f32[280,32,128]{2,1,0:T(8,128)S(1)} %get-tuple-element.18.ext_ref, bf16[256,256]{1,0:T(8,128)(2,1)S(1)} %copy-done.3), custom_call_target="tpu_custom_call" | custom-call | flops 104857600 | bytes 8388608 | tf_op jit(solution)/shard_map/both_passes/pallas_call | solution.py:463
  21.5 0.0 collective-permute-done.2.first_ref
  21.5 0.0 collective-permute-done.3.second_ref
  21.5 0.0 copy-done.1
  21.5 0.0 copy-done.2
  21.6 4.6 %rim_and_gram.1 = (bf16[272,64,128]{2,1,0:T(8,128)(2,1)S(1)}, f32[8,128]{1,0:T(8,128)S(1)}) custom-call(f32[272,32,128]{2,1,0:T(8,128)S(1)} %get-tuple-element.19.twice_ref, f32[34,32,128]{2,1,0:T(8,128)S(1)} %get-tuple-element.20.strip_ref, f32[3,34,8,128]{3,2,1,0:T(8,128)S(1)} %get-tuple-element.21.strip_rates_ref, ...), custom_call_target="tpu_custom_call" | custom-call | tf_op jit(solution)/shard_map/rim_and_gram/pallas_call | solution.py:478
  26.2 14.5 %all_to_all.5.gram_ref = f32[32,8,128]{2,1,0:T(8,128)S(1)} all-to-all(f32[32,8,128]{2,1,0:T(8,128)S(1)} %broadcast_in_dim.3), channel_id=1, replica_groups=mesh['lat'=4,'lon'=8] {'lat','lon'}, dimensions={0} | all-to-all | bytes 262144 | tf_op jit(solution)/shard_map/all_to_all | solution.py:412
  40.7 3.4 %factor_and_basis.1 = (bf16[32,256,128]{2,1,0:T(8,128)(2,1)}, f32[32,32]{1,0:T(8,128)}) custom-call(f32[32,8,128]{2,1,0:T(8,128)S(1)} %all_to_all.5.gram_ref, bf16[272,64,128]{2,1,0:T(8,128)(2,1)S(1)} %get-tuple-element.25.split_ref), custom_call_target="tpu_custom_call" | custom-call | tf_op jit(solution)/shard_map/factor_and_basis/pallas_call | solution.py:498
  (6 shorter events, 0.1 us)
Async XLA Ops:
  0.6 2.2 %copy-start = (f32[32,256,128]{2,1,0:T(8,128)S(1)}, f32[32,256,128]{2,1,0:T(8,128)}, u32[]{:S(2)}) copy-start(f32[32,256,128]{2,1,0:T(8,128)} %field_ref.3) | copy-start | bytes 12582916
  2.9 6.5 %collective-permute-start = (f32[32,8,128]{2,1,0:T(8,128)S(1)}, f32[32,8,128]{2,1,0:T(8,128)S(1)}, u32[]{:S(2)}, u32[]{:S(2)}) collective-permute-start(f32[32,8,128]{2,1,0:T(8,128)S(1)} %get-tuple-element.16), channel_id=1, source_target_pairs={{0,8},{8,0},{16,24},{24,16},{1,9},{9,1},{17,25},{25,17},{2,10},{10... | collective-permute-start | bytes 393224 | tf_op jit(solution)/shard_map/ppermute | solution.py:406
  5.9 7.8 %copy-start.3 = (bf16[256,256]{1,0:T(8,128)(2,1)S(1)}, bf16[256,256]{1,0:T(8,128)(2,1)}, u32[]{:S(2)}) copy-start(bf16[256,256]{1,0:T(8,128)(2,1)} %constant.9.clone.main_ref) | copy-start | bytes 393220
  5.9 7.8 %copy-start.4 = (f32[1024]{0:T(1024)S(1)}, f32[1024]{0:T(1024)}, u32[]{:S(2)}) copy-start(f32[1024]{0:T(1024)} %lon_ref.1) | copy-start | bytes 12292
  5.9 7.8 %copy-start.5 = (f32[1024]{0:T(1024)S(1)}, f32[1024]{0:T(1024)}, u32[]{:S(2)}) copy-start(f32[1024]{0:T(1024)} %lat_ref.1) | copy-start | bytes 12292
  5.9 7.8 %copy-start.6 = (f32[1024]{0:T(1024)S(1)}, f32[1024]{0:T(1024)}, u32[]{:S(2)}) copy-start(f32[1024]{0:T(1024)} %constant.8.clone.weight_ref) | copy-start | bytes 12292
  5.9 3.5 %collective-permute-start.1 = (f32[32,8,128]{2,1,0:T(8,128)S(1)}, f32[32,8,128]{2,1,0:T(8,128)S(1)}, u32[]{:S(2)}, u32[]{:S(2)}) collective-permute-start(f32[32,8,128]{2,1,0:T(8,128)S(1)} %get-tuple-element.17), channel_id=1, source_target_pairs={{8,16},{16,8},{9,17},{17,9},{10,18},{18,10},{11,19},{19,11},{12,20... | collective-permute-start | bytes 393224 | tf_op jit(solution)/shard_map/ppermute | solution.py:406
  9.4 12.2 %copy-start.1 = (bf16[512,512]{1,0:T(8,128)(2,1)S(1)}, bf16[512,512]{1,0:T(8,128)(2,1)}, u32[]{:S(2)}) copy-start(bf16[512,512]{1,0:T(8,128)(2,1)} %constant.10.clone.edge_ref) | copy-start | bytes 1572868
  9.4 12.2 %copy-start.2 = (bf16[512,256]{1,0:T(8,128)(2,1)S(1)}, bf16[512,256]{1,0:T(8,128)(2,1)}, u32[]{:S(2)}) copy-start(bf16[512,256]{1,0:T(8,128)(2,1)} %constant.11.clone.again_ref) | copy-start | bytes 786436
  9.7 11.8 %collective-permute-start.2 = (f32[17,32,128]{2,1,0:T(8,128)S(1)}, f32[17,32,128]{2,1,0:T(8,128)S(1)}, u32[]{:S(2)}, u32[]{:S(2)}) collective-permute-start(f32[17,32,128]{2,1,0:T(8,128)S(1)} %get-tuple-element.22), channel_id=1, source_target_pairs={{0,1},{1,0},{2,3},{3,2},{4,5},{5,4},{6,7},{7,6},{8,9},{9,8},{10,11... | collective-permute-start | bytes 835592 | tf_op jit(solution)/shard_map/ppermute | solution.py:406
  9.7 11.8 %collective-permute-start.3 = (f32[17,32,128]{2,1,0:T(8,128)S(1)}, f32[17,32,128]{2,1,0:T(8,128)S(1)}, u32[]{:S(2)}, u32[]{:S(2)}) collective-permute-start(f32[17,32,128]{2,1,0:T(8,128)S(1)} %get-tuple-element.23), channel_id=1, source_target_pairs={{1,2},{2,1},{3,4},{4,3},{5,6},{6,5},{7,0},{0,7},{9,10},{10,9},{11,... | collective-permute-start | bytes 835592 | tf_op jit(solution)/shard_map/ppermute | solution.py:406

commit v9 on v8

--- a/solution.py
+++ b/solution.py
@@ -70,14 +70,6 @@
     return np.concatenate([main, main], axis=0), np.concatenate([edge, inward_only], axis=1), again
 
 
-def edge_kernel(field_ref, first_ref, second_ref):
-    rows = field_ref.shape[1]
-    lat_even = lax.axis_index("lat") % 2 == 0
-    north, south = field_ref[:, :HALO], field_ref[:, rows - HALO :]
-    first_ref[...] = jnp.where(lat_even, south, north)
-    second_ref[...] = jnp.where(lat_even, north, south)
-
-
 def strip_kernel(span, field_ref, ext_ref, strip_ref):
     snaps, rows, _ = field_ref.shape
 
@@ -114,14 +106,18 @@
     half = span // 2
     end = ext_ref.shape[0] - 4 - HALO
     lane = lax.broadcasted_iota(jnp.int32, (snaps, LANES), 1)
-    lat_even = lax.axis_index("lat") % 2 == 0
+    lat = lax.axis_index("lat")
+    last_lat = lax.axis_size("lat") - 1
+    lat_even = lat % 2 == 0
     lon_even = lax.axis_index("lon") % 2 == 0
     full_ref[...] = strip_ref[...]
     for tile in range(0, snaps, 8):
         first = jnp.swapaxes(low_ref[tile : tile + 8], 0, 1)
         second = jnp.swapaxes(high_ref[tile : tile + 8], 0, 1)
-        ext_ref[4 : 4 + HALO, tile : tile + 8] = jnp.where(lat_even, second, first)
-        ext_ref[end : end + HALO, tile : tile + 8] = jnp.where(lat_even, first, second)
+        north = jnp.where(lat_even, second, first)
+        south = jnp.where(lat_even, first, second)
+        ext_ref[4 : 4 + HALO, tile : tile + 8] = jnp.where(lat == 0, 0.0, north)
+        ext_ref[end : end + HALO, tile : tile + 8] = jnp.where(lat == last_lat, 0.0, south)
     for at in range(HALO):
         north, south = ext_ref[4 + at], ext_ref[end + at]
         full_ref[at] = jnp.where(lane < STRIP, pltpu.roll(north, HALO, 1), full_ref[at])
@@ -396,13 +392,10 @@
     lax.fori_loop(0, basis_ref.shape[1] // 16, body, 0, unroll=8)
 
 
-def pair_permutes(values, axis, periodic):
+def pair_permutes(values, axis):
     count = lax.axis_size(axis)
     inner = [(i, i ^ 1) for i in range(count)]
-    outer = []
-    for i in range(1, count, 2):
-        if periodic or i + 1 < count:
-            outer += [(i, (i + 1) % count), ((i + 1) % count, i)]
+    outer = [(i, (i + 1 if i % 2 else i - 1) % count) for i in range(count)]
     return lax.ppermute(values[0], axis, inner), lax.ppermute(values[1], axis, outer)
 
 
@@ -428,17 +421,15 @@
     ext = jax.ShapeDtypeStruct((total + 8, snaps, cols), f32)
     strip = jax.ShapeDtypeStruct((span, snaps, cols), f32)
     half = jax.ShapeDtypeStruct((span // 2, snaps, cols), f32)
-    edge_rows = jax.ShapeDtypeStruct((snaps, HALO, cols), f32)
-    first, second = pl.pallas_call(
-        edge_kernel,
-        in_specs=[whole()],
-        out_specs=[whole()] * 2,
-        out_shape=[edge_rows, edge_rows],
-        compiler_params=limits,
-        name="lat_messages",
-    )(field)
-    low, high = pair_permutes([first, second], "lat", False)
     weight = area_weight(total_rows)
+    begin = jnp.where(lax.axis_index("lat") % 2 == 0, rows - HALO, 0)
+    low, high = pair_permutes(
+        [
+            lax.dynamic_slice_in_dim(field, start, HALO, axis=1)
+            for start in (begin, rows - HALO - begin)
+        ],
+        "lat",
+    )
     turned, packed = pl.pallas_call(
         functools.partial(strip_kernel, span),
         in_specs=[whole()],
@@ -456,7 +447,7 @@
         compiler_params=limits,
         name="lon_messages",
     )(turned, packed, low, high)
-    first, second = pair_permutes([first, second], "lon", True)
+    first, second = pair_permutes([first, second], "lon")
 
     main, edge, again = zonal_matrices()
     bf16 = jnp.bfloat16

time: 44.2 us -> 42.6 us (0.964)
  blocking collectives: 14.5 us -> 10.4 us
  waiting for transfers between devices: 0.58 us -> 1.71 us
  local copies, waits for them, and re-layouts: 2.22 us -> 3.22 us
    all_to_all x1, blocking collectives: 14.5 us -> 10.4 us  [gather_all(): lax.all_to_all(jnp.broadcast_to(values, (count,) + values.shape), axes, 0...]
    ppermute x2, starting transfers between devices: 4.75 us -> 7.66 us  [pair_permutes(): lax.ppermute(values[1], axis, outer)]
    ppermute x2, starting transfers between devices: 3.07 us -> 0.61 us  [pair_permutes(): lax.ppermute(values[0], axis, inner)]
    ppermute x2, waiting for transfers between devices: 0.57 us -> 1.7 us  [pair_permutes(): lax.ppermute(values[0], axis, inner)]
    dynamic_slice x0 -> x1, local copies, waits for them, and re-layouts: none -> 0.99 us  [shards(): lax.dynamic_slice_in_dim(field, start, HALO, axis=1)]
  transfers between devices with their start and end apart: 4 -> 4, of which waited for: 1 -> 1; matrix products, arithmetic and copies ran while one was open for 0% -> 0% of each run, Pallas kernels for 22% -> 23%
where the time goes in v9:
time: 42.6 us; the launch traced here: 42.4 us
  Pallas kernels  18.1 us (42%)
  blocking collectives  10.4 us (24%)
  starting transfers between devices  8.27 us (19%)
  local copies, waits for them, and re-layouts  3.22 us (8%)
  waiting for transfers between devices  1.71 us (4%)
  between operations  0.74 us (2%)
    all_to_all x1, blocking collectives, gather_all(): lax.all_to_all(jnp.broadcast_to(values, (count,) + values.shape), axes, 0...  10.4 us
    pallas_call x1, Pallas kernels, shards(): pl.pallas_call(functools.partial(tile_kernel, span), in_specs=[whole(pltp...  7.77 us
    ppermute x2, starting transfers between devices, pair_permutes(): lax.ppermute(values[1], axis, outer)  7.66 us
    pallas_call x1, Pallas kernels, shards(): pl.pallas_call(functools.partial(rim_kernel, span), in_specs=[whole()] *...  4.57 us
    pallas_call x1, Pallas kernels, shards(): pl.pallas_call(functools.partial(basis_kernel, math.sqrt(total_cells)), g...  3.36 us
    unnamed x14, local copies, waits for them, and re-layouts  2.21 us
    pallas_call x1, Pallas kernels, shards(): pl.pallas_call(functools.partial(strip_kernel, span), in_specs=[whole()],...  2.1 us
    ppermute x2, waiting for transfers between devices, pair_permutes(): lax.ppermute(values[0], axis, inner)  1.7 us
  transfers between devices with their start and end apart: 4, of which 1 were waited for; matrix products, arithmetic and copies ran while one was open for 0% of the time, Pallas kernels for 23%

profile of v9, /device:TPU:0, one launch (start us, length us, event | category | flops | bytes accessed | tf_op | source)
XLA Modules:
  0.0 42.4 jit_solution(4522301277405021651)
XLA Ops:
  0.6 1.0 %constant_dynamic-slice_fusion = (f32[32,8,128]{2,1,0:T(8,128)S(1)}, f32[32,8,128]{2,1,0:T(8,128)S(1)}) fusion(f32[32,256,128]{2,1,0:T(8,128)} %field_ref.1, s32[]{:T(128)S(6)} %select_n.17, s32[]{:T(128)S(6)} %select_n.16), kind=kLoop, calls=%fused_computation | loop fusion | bytes 524296 | tf_op jit(solution)/shard_map/dynamic_slice | solution.py:428
  1.6 4.0 %collective-permute-start.1 = (f32[32,8,128]{2,1,0:T(8,128)S(1)}, f32[32,8,128]{2,1,0:T(8,128)S(1)}, u32[]{:S(2)}, u32[]{:S(2)}) collective-permute-start(f32[32,8,128]{2,1,0:T(8,128)S(1)} %get-tuple-element.22), channel_id=1, source_target_pairs={{0,24},{8,16},{16,8},{24,0},{1,25},{9,17},{17,9},{25,1},{2,26},{10... | collective-permute-start | bytes 393224 | tf_op jit(solution)/shard_map/ppermute | solution.py:399
  5.6 0.5 %collective-permute-start = (f32[32,8,128]{2,1,0:T(8,128)S(1)}, f32[32,8,128]{2,1,0:T(8,128)S(1)}, u32[]{:S(2)}, u32[]{:S(2)}) collective-permute-start(f32[32,8,128]{2,1,0:T(8,128)S(1)} %get-tuple-element.23), channel_id=1, source_target_pairs={{0,8},{8,0},{16,24},{24,16},{1,9},{9,1},{17,25},{25,17},{2,10},{10... | collective-permute-start | bytes 393224 | tf_op jit(solution)/shard_map/ppermute | solution.py:399
  6.1 0.0 copy-start
  6.1 2.2 %copy-done = f32[32,256,128]{2,1,0:T(8,128)S(1)} copy-done((f32[32,256,128]{2,1,0:T(8,128)S(1)}, f32[32,256,128]{2,1,0:T(8,128)}, u32[]{:S(2)}) %copy-start) | copy-done | bytes 4194328
  8.3 0.0 copy-start.3
  8.3 2.1 %turn_and_pack.1 = (f32[280,32,128]{2,1,0:T(8,128)S(1)}, f32[34,32,128]{2,1,0:T(8,128)S(1)}) custom-call(f32[32,256,128]{2,1,0:T(8,128)S(1)} %copy-done), custom_call_target="tpu_custom_call" | custom-call | tf_op jit(solution)/shard_map/turn_and_pack/pallas_call | solution.py:433
  10.4 0.0 collective-permute-done.1.high_ref
  10.5 1.7 %collective-permute-done.low_ref = f32[32,8,128]{2,1,0:T(8,128)S(1)} collective-permute-done((f32[32,8,128]{2,1,0:T(8,128)S(1)}, f32[32,8,128]{2,1,0:T(8,128)S(1)}, u32[]{:S(2)}, u32[]{:S(2)}) %collective-permute-start) | collective-permute-done | bytes 131104 | tf_op jit(solution)/shard_map/ppermute | solution.py:399
  12.2 0.3 lon_messages.1
  12.5 0.1 collective-permute-start.2
  12.5 3.7 %collective-permute-start.3 = (f32[17,32,128]{2,1,0:T(8,128)S(1)}, f32[17,32,128]{2,1,0:T(8,128)S(1)}, u32[]{:S(2)}, u32[]{:S(2)}) collective-permute-start(f32[17,32,128]{2,1,0:T(8,128)S(1)} %get-tuple-element.19), channel_id=1, source_target_pairs={{0,7},{1,2},{2,1},{3,4},{4,3},{5,6},{6,5},{7,0},{8,15},{9,10},{10,... | collective-permute-start | bytes 835592 | tf_op jit(solution)/shard_map/ppermute | solution.py:399
  16.2 0.0 copy-done.3
  16.2 0.0 copy-done.4
  16.3 0.0 copy-done.5
  16.3 0.0 copy-done.6
  16.3 7.8 %both_passes.1 = (f32[272,32,128]{2,1,0:T(8,128)S(1)}, f32[3,34,8,128]{3,2,1,0:T(8,128)S(1)}) custom-call(f32[1024]{0:T(1024)S(1)} %copy-done.4, f32[1024]{0:T(1024)S(1)} %copy-done.5, f32[1024]{0:T(1024)S(1)} %copy-done.6, f32[280,32,128]{2,1,0:T(8,128)S(1)} %get-tuple-element.14.ext_ref, bf16[256,256]{1,0:T(8,128)(2,1)S(1)} %copy-done.3), custom_call_target="tpu_custom_call" | custom-call | flops 104857600 | bytes 8388608 | tf_op jit(solution)/shard_map/both_passes/pallas_call | solution.py:454
  24.0 0.0 collective-permute-done.2.first_ref
  24.1 0.0 collective-permute-done.3.second_ref
  24.1 0.0 copy-done.1
  24.1 0.0 copy-done.2
  24.1 4.6 %rim_and_gram.1 = (bf16[272,64,128]{2,1,0:T(8,128)(2,1)S(1)}, f32[8,128]{1,0:T(8,128)S(1)}) custom-call(f32[272,32,128]{2,1,0:T(8,128)S(1)} %get-tuple-element.15.twice_ref, f32[34,32,128]{2,1,0:T(8,128)S(1)} %get-tuple-element.16.strip_ref, f32[3,34,8,128]{3,2,1,0:T(8,128)S(1)} %get-tuple-element.17.strip_rates_ref, ...), custom_call_target="tpu_custom_call" | custom-call | tf_op jit(solution)/shard_map/rim_and_gram/pallas_call | solution.py:469
  28.7 10.4 %all_to_all.5.gram_ref = f32[32,8,128]{2,1,0:T(8,128)S(1)} all-to-all(f32[32,8,128]{2,1,0:T(8,128)S(1)} %broadcast_in_dim.3), channel_id=1, replica_groups=mesh['lat'=4,'lon'=8] {'lat','lon'}, dimensions={0} | all-to-all | bytes 262144 | tf_op jit(solution)/shard_map/all_to_all | solution.py:405
  39.0 3.4 %factor_and_basis.1 = (bf16[32,256,128]{2,1,0:T(8,128)(2,1)}, f32[32,32]{1,0:T(8,128)}) custom-call(f32[32,8,128]{2,1,0:T(8,128)S(1)} %all_to_all.5.gram_ref, bf16[272,64,128]{2,1,0:T(8,128)(2,1)S(1)} %get-tuple-element.21.split_ref), custom_call_target="tpu_custom_call" | custom-call | tf_op jit(solution)/shard_map/factor_and_basis/pallas_call | solution.py:489
  (6 shorter events, 0.0 us)
Async XLA Ops:
  1.6 8.8 %collective-permute-start.1 = (f32[32,8,128]{2,1,0:T(8,128)S(1)}, f32[32,8,128]{2,1,0:T(8,128)S(1)}, u32[]{:S(2)}, u32[]{:S(2)}) collective-permute-start(f32[32,8,128]{2,1,0:T(8,128)S(1)} %get-tuple-element.22), channel_id=1, source_target_pairs={{0,24},{8,16},{16,8},{24,0},{1,25},{9,17},{17,9},{25,1},{2,26},{10... | collective-permute-start | bytes 393224 | tf_op jit(solution)/shard_map/ppermute | solution.py:399
  5.6 6.6 %collective-permute-start = (f32[32,8,128]{2,1,0:T(8,128)S(1)}, f32[32,8,128]{2,1,0:T(8,128)S(1)}, u32[]{:S(2)}, u32[]{:S(2)}) collective-permute-start(f32[32,8,128]{2,1,0:T(8,128)S(1)} %get-tuple-element.23), channel_id=1, source_target_pairs={{0,8},{8,0},{16,24},{24,16},{1,9},{9,1},{17,25},{25,17},{2,10},{10... | collective-permute-start | bytes 393224 | tf_op jit(solution)/shard_map/ppermute | solution.py:399
  6.1 2.2 %copy-start = (f32[32,256,128]{2,1,0:T(8,128)S(1)}, f32[32,256,128]{2,1,0:T(8,128)}, u32[]{:S(2)}) copy-start(f32[32,256,128]{2,1,0:T(8,128)} %field_ref.1) | copy-start | bytes 12582916
  8.3 7.9 %copy-start.3 = (bf16[256,256]{1,0:T(8,128)(2,1)S(1)}, bf16[256,256]{1,0:T(8,128)(2,1)}, u32[]{:S(2)}) copy-start(bf16[256,256]{1,0:T(8,128)(2,1)} %constant.34.clone.main_ref) | copy-start | bytes 393220
  8.3 7.9 %copy-start.4 = (f32[1024]{0:T(1024)S(1)}, f32[1024]{0:T(1024)}, u32[]{:S(2)}) copy-start(f32[1024]{0:T(1024)} %lon_ref.1) | copy-start | bytes 12292
  8.3 7.9 %copy-start.5 = (f32[1024]{0:T(1024)S(1)}, f32[1024]{0:T(1024)}, u32[]{:S(2)}) copy-start(f32[1024]{0:T(1024)} %lat_ref.1) | copy-start | bytes 12292
  8.3 7.9 %copy-start.6 = (f32[1024]{0:T(1024)S(1)}, f32[1024]{0:T(1024)}, u32[]{:S(2)}) copy-start(f32[1024]{0:T(1024)} %constant.33.clone.weight_ref) | copy-start | bytes 12292
  12.2 11.9 %copy-start.1 = (bf16[512,512]{1,0:T(8,128)(2,1)S(1)}, bf16[512,512]{1,0:T(8,128)(2,1)}, u32[]{:S(2)}) copy-start(bf16[512,512]{1,0:T(8,128)(2,1)} %constant.35.clone.edge_ref) | copy-start | bytes 1572868
  12.2 11.9 %copy-start.2 = (bf16[512,256]{1,0:T(8,128)(2,1)S(1)}, bf16[512,256]{1,0:T(8,128)(2,1)}, u32[]{:S(2)}) copy-start(bf16[512,256]{1,0:T(8,128)(2,1)} %constant.36.clone.again_ref) | copy-start | bytes 786436
  12.5 11.6 %collective-permute-start.2 = (f32[17,32,128]{2,1,0:T(8,128)S(1)}, f32[17,32,128]{2,1,0:T(8,128)S(1)}, u32[]{:S(2)}, u32[]{:S(2)}) collective-permute-start(f32[17,32,128]{2,1,0:T(8,128)S(1)} %get-tuple-element.18), channel_id=1, source_target_pairs={{0,1},{1,0},{2,3},{3,2},{4,5},{5,4},{6,7},{7,6},{8,9},{9,8},{10,11... | collective-permute-start | bytes 835592 | tf_op jit(solution)/shard_map/ppermute | solution.py:399
  12.5 11.5 %collective-permute-start.3 = (f32[17,32,128]{2,1,0:T(8,128)S(1)}, f32[17,32,128]{2,1,0:T(8,128)S(1)}, u32[]{:S(2)}, u32[]{:S(2)}) collective-permute-start(f32[17,32,128]{2,1,0:T(8,128)S(1)} %get-tuple-element.19), channel_id=1, source_target_pairs={{0,7},{1,2},{2,1},{3,4},{4,3},{5,6},{6,5},{7,0},{8,15},{9,10},{10,... | collective-permute-start | bytes 835592 | tf_op jit(solution)/shard_map/ppermute | solution.py:399

commit v10 on v9

--- a/solution.py
+++ b/solution.py
@@ -328,7 +328,7 @@
             )
         return grams
 
-    grams = lax.fori_loop(0, GROUPS, finish, jnp.zeros((both, both), jnp.float32))
+    grams = lax.fori_loop(0, GROUPS, finish, jnp.zeros((both, both), jnp.float32), unroll=4)
     gram = (
         grams[:snaps, :snaps]
         + grams[snaps:, snaps:]

time: 42.6 us -> 41.3 us (0.969)
  Pallas kernels: 18.1 us -> 16.8 us
    pallas_call x1, Pallas kernels: 4.57 us -> 3.24 us  [shards(): pl.pallas_call(functools.partial(rim_kernel, span), in_specs=[whole()] *...]
  transfers between devices with their start and end apart: 4 -> 4, of which waited for: 1 -> 1; matrix products, arithmetic and copies ran while one was open for 0% -> 0% of each run, Pallas kernels for 23% -> 24%
where the time goes in v10:
time: 41.3 us; the launch traced here: 41.1 us
  Pallas kernels  16.8 us (41%)
  blocking collectives  10.4 us (25%)
  starting transfers between devices  8.27 us (20%)
  local copies, waits for them, and re-layouts  3.22 us (8%)
  waiting for transfers between devices  1.71 us (4%)
  between operations  0.74 us (2%)
    all_to_all x1, blocking collectives, gather_all(): lax.all_to_all(jnp.broadcast_to(values, (count,) + values.shape), axes, 0...  10.4 us
    pallas_call x1, Pallas kernels, shards(): pl.pallas_call(functools.partial(tile_kernel, span), in_specs=[whole(pltp...  7.77 us
    ppermute x2, starting transfers between devices, pair_permutes(): lax.ppermute(values[1], axis, outer)  7.66 us
    pallas_call x1, Pallas kernels, shards(): pl.pallas_call(functools.partial(basis_kernel, math.sqrt(total_cells)), g...  3.36 us
    pallas_call x1, Pallas kernels, shards(): pl.pallas_call(functools.partial(rim_kernel, span), in_specs=[whole()] *...  3.24 us
    unnamed x14, local copies, waits for them, and re-layouts  2.21 us
    pallas_call x1, Pallas kernels, shards(): pl.pallas_call(functools.partial(strip_kernel, span), in_specs=[whole()],...  2.1 us
    ppermute x2, waiting for transfers between devices, pair_permutes(): lax.ppermute(values[0], axis, inner)  1.7 us
  transfers between devices with their start and end apart: 4, of which 1 were waited for; matrix products, arithmetic and copies ran while one was open for 0% of the time, Pallas kernels for 24%

profile of v10, /device:TPU:0, one launch (start us, length us, event | category | flops | bytes accessed | tf_op | source)
XLA Modules:
  0.0 41.1 jit_solution(2512553469624902067)
XLA Ops:
  0.6 1.0 %constant_dynamic-slice_fusion = (f32[32,8,128]{2,1,0:T(8,128)S(1)}, f32[32,8,128]{2,1,0:T(8,128)S(1)}) fusion(f32[32,256,128]{2,1,0:T(8,128)} %field_ref.1, s32[]{:T(128)S(6)} %select_n.17, s32[]{:T(128)S(6)} %select_n.16), kind=kLoop, calls=%fused_computation | loop fusion | bytes 524296 | tf_op jit(solution)/shard_map/dynamic_slice | solution.py:428
  1.6 4.0 %collective-permute-start.1 = (f32[32,8,128]{2,1,0:T(8,128)S(1)}, f32[32,8,128]{2,1,0:T(8,128)S(1)}, u32[]{:S(2)}, u32[]{:S(2)}) collective-permute-start(f32[32,8,128]{2,1,0:T(8,128)S(1)} %get-tuple-element.22), channel_id=1, source_target_pairs={{0,24},{8,16},{16,8},{24,0},{1,25},{9,17},{17,9},{25,1},{2,26},{10... | collective-permute-start | bytes 393224 | tf_op jit(solution)/shard_map/ppermute | solution.py:399
  5.6 0.5 %collective-permute-start = (f32[32,8,128]{2,1,0:T(8,128)S(1)}, f32[32,8,128]{2,1,0:T(8,128)S(1)}, u32[]{:S(2)}, u32[]{:S(2)}) collective-permute-start(f32[32,8,128]{2,1,0:T(8,128)S(1)} %get-tuple-element.23), channel_id=1, source_target_pairs={{0,8},{8,0},{16,24},{24,16},{1,9},{9,1},{17,25},{25,17},{2,10},{10... | collective-permute-start | bytes 393224 | tf_op jit(solution)/shard_map/ppermute | solution.py:399
  6.1 0.0 copy-start
  6.1 2.2 %copy-done = f32[32,256,128]{2,1,0:T(8,128)S(1)} copy-done((f32[32,256,128]{2,1,0:T(8,128)S(1)}, f32[32,256,128]{2,1,0:T(8,128)}, u32[]{:S(2)}) %copy-start) | copy-done | bytes 4194328
  8.3 0.0 copy-start.3
  8.3 2.1 %turn_and_pack.1 = (f32[280,32,128]{2,1,0:T(8,128)S(1)}, f32[34,32,128]{2,1,0:T(8,128)S(1)}) custom-call(f32[32,256,128]{2,1,0:T(8,128)S(1)} %copy-done), custom_call_target="tpu_custom_call" | custom-call | tf_op jit(solution)/shard_map/turn_and_pack/pallas_call | solution.py:433
  10.4 0.0 collective-permute-done.1.high_ref
  10.5 1.7 %collective-permute-done.low_ref = f32[32,8,128]{2,1,0:T(8,128)S(1)} collective-permute-done((f32[32,8,128]{2,1,0:T(8,128)S(1)}, f32[32,8,128]{2,1,0:T(8,128)S(1)}, u32[]{:S(2)}, u32[]{:S(2)}) %collective-permute-start) | collective-permute-done | bytes 131104 | tf_op jit(solution)/shard_map/ppermute | solution.py:399
  12.2 0.3 lon_messages.1
  12.5 0.1 collective-permute-start.2
  12.5 3.7 %collective-permute-start.3 = (f32[17,32,128]{2,1,0:T(8,128)S(1)}, f32[17,32,128]{2,1,0:T(8,128)S(1)}, u32[]{:S(2)}, u32[]{:S(2)}) collective-permute-start(f32[17,32,128]{2,1,0:T(8,128)S(1)} %get-tuple-element.19), channel_id=1, source_target_pairs={{0,7},{1,2},{2,1},{3,4},{4,3},{5,6},{6,5},{7,0},{8,15},{9,10},{10,... | collective-permute-start | bytes 835592 | tf_op jit(solution)/shard_map/ppermute | solution.py:399
  16.2 0.0 copy-done.3
  16.2 0.0 copy-done.4
  16.3 0.0 copy-done.5
  16.3 0.0 copy-done.6
  16.3 7.8 %both_passes.1 = (f32[272,32,128]{2,1,0:T(8,128)S(1)}, f32[3,34,8,128]{3,2,1,0:T(8,128)S(1)}) custom-call(f32[1024]{0:T(1024)S(1)} %copy-done.4, f32[1024]{0:T(1024)S(1)} %copy-done.5, f32[1024]{0:T(1024)S(1)} %copy-done.6, f32[280,32,128]{2,1,0:T(8,128)S(1)} %get-tuple-element.14.ext_ref, bf16[256,256]{1,0:T(8,128)(2,1)S(1)} %copy-done.3), custom_call_target="tpu_custom_call" | custom-call | flops 104857600 | bytes 8388608 | tf_op jit(solution)/shard_map/both_passes/pallas_call | solution.py:454
  24.0 0.0 collective-permute-done.2.first_ref
  24.1 0.0 collective-permute-done.3.second_ref
  24.1 0.0 copy-done.1
  24.1 0.0 copy-done.2
  24.1 3.2 %rim_and_gram.1 = (bf16[272,64,128]{2,1,0:T(8,128)(2,1)S(1)}, f32[8,128]{1,0:T(8,128)S(1)}) custom-call(f32[272,32,128]{2,1,0:T(8,128)S(1)} %get-tuple-element.15.twice_ref, f32[34,32,128]{2,1,0:T(8,128)S(1)} %get-tuple-element.16.strip_ref, f32[3,34,8,128]{3,2,1,0:T(8,128)S(1)} %get-tuple-element.17.strip_rates_ref, ...), custom_call_target="tpu_custom_call" | custom-call | tf_op jit(solution)/shard_map/rim_and_gram/pallas_call | solution.py:469
  27.3 10.4 %all_to_all.5.gram_ref = f32[32,8,128]{2,1,0:T(8,128)S(1)} all-to-all(f32[32,8,128]{2,1,0:T(8,128)S(1)} %broadcast_in_dim.3), channel_id=1, replica_groups=mesh['lat'=4,'lon'=8] {'lat','lon'}, dimensions={0} | all-to-all | bytes 262144 | tf_op jit(solution)/shard_map/all_to_all | solution.py:405
  37.7 3.4 %factor_and_basis.1 = (bf16[32,256,128]{2,1,0:T(8,128)(2,1)}, f32[32,32]{1,0:T(8,128)}) custom-call(f32[32,8,128]{2,1,0:T(8,128)S(1)} %all_to_all.5.gram_ref, bf16[272,64,128]{2,1,0:T(8,128)(2,1)S(1)} %get-tuple-element.21.split_ref), custom_call_target="tpu_custom_call" | custom-call | tf_op jit(solution)/shard_map/factor_and_basis/pallas_call | solution.py:489
  (6 shorter events, 0.0 us)
Async XLA Ops:
  1.6 8.8 %collective-permute-start.1 = (f32[32,8,128]{2,1,0:T(8,128)S(1)}, f32[32,8,128]{2,1,0:T(8,128)S(1)}, u32[]{:S(2)}, u32[]{:S(2)}) collective-permute-start(f32[32,8,128]{2,1,0:T(8,128)S(1)} %get-tuple-element.22), channel_id=1, source_target_pairs={{0,24},{8,16},{16,8},{24,0},{1,25},{9,17},{17,9},{25,1},{2,26},{10... | collective-permute-start | bytes 393224 | tf_op jit(solution)/shard_map/ppermute | solution.py:399
  5.6 6.6 %collective-permute-start = (f32[32,8,128]{2,1,0:T(8,128)S(1)}, f32[32,8,128]{2,1,0:T(8,128)S(1)}, u32[]{:S(2)}, u32[]{:S(2)}) collective-permute-start(f32[32,8,128]{2,1,0:T(8,128)S(1)} %get-tuple-element.23), channel_id=1, source_target_pairs={{0,8},{8,0},{16,24},{24,16},{1,9},{9,1},{17,25},{25,17},{2,10},{10... | collective-permute-start | bytes 393224 | tf_op jit(solution)/shard_map/ppermute | solution.py:399
  6.1 2.2 %copy-start = (f32[32,256,128]{2,1,0:T(8,128)S(1)}, f32[32,256,128]{2,1,0:T(8,128)}, u32[]{:S(2)}) copy-start(f32[32,256,128]{2,1,0:T(8,128)} %field_ref.1) | copy-start | bytes 12582916
  8.3 7.9 %copy-start.3 = (bf16[256,256]{1,0:T(8,128)(2,1)S(1)}, bf16[256,256]{1,0:T(8,128)(2,1)}, u32[]{:S(2)}) copy-start(bf16[256,256]{1,0:T(8,128)(2,1)} %constant.34.clone.main_ref) | copy-start | bytes 393220
  8.3 7.9 %copy-start.4 = (f32[1024]{0:T(1024)S(1)}, f32[1024]{0:T(1024)}, u32[]{:S(2)}) copy-start(f32[1024]{0:T(1024)} %lon_ref.1) | copy-start | bytes 12292
  8.3 7.9 %copy-start.5 = (f32[1024]{0:T(1024)S(1)}, f32[1024]{0:T(1024)}, u32[]{:S(2)}) copy-start(f32[1024]{0:T(1024)} %lat_ref.1) | copy-start | bytes 12292
  8.3 7.9 %copy-start.6 = (f32[1024]{0:T(1024)S(1)}, f32[1024]{0:T(1024)}, u32[]{:S(2)}) copy-start(f32[1024]{0:T(1024)} %constant.33.clone.weight_ref) | copy-start | bytes 12292
  12.2 11.9 %copy-start.1 = (bf16[512,512]{1,0:T(8,128)(2,1)S(1)}, bf16[512,512]{1,0:T(8,128)(2,1)}, u32[]{:S(2)}) copy-start(bf16[512,512]{1,0:T(8,128)(2,1)} %constant.35.clone.edge_ref) | copy-start | bytes 1572868
  12.2 11.9 %copy-start.2 = (bf16[512,256]{1,0:T(8,128)(2,1)S(1)}, bf16[512,256]{1,0:T(8,128)(2,1)}, u32[]{:S(2)}) copy-start(bf16[512,256]{1,0:T(8,128)(2,1)} %constant.36.clone.again_ref) | copy-start | bytes 786436
  12.5 11.6 %collective-permute-start.2 = (f32[17,32,128]{2,1,0:T(8,128)S(1)}, f32[17,32,128]{2,1,0:T(8,128)S(1)}, u32[]{:S(2)}, u32[]{:S(2)}) collective-permute-start(f32[17,32,128]{2,1,0:T(8,128)S(1)} %get-tuple-element.18), channel_id=1, source_target_pairs={{0,1},{1,0},{2,3},{3,2},{4,5},{5,4},{6,7},{7,6},{8,9},{9,8},{10,11... | collective-permute-start | bytes 835592 | tf_op jit(solution)/shard_map/ppermute | solution.py:399
  12.5 11.5 %collective-permute-start.3 = (f32[17,32,128]{2,1,0:T(8,128)S(1)}, f32[17,32,128]{2,1,0:T(8,128)S(1)}, u32[]{:S(2)}, u32[]{:S(2)}) collective-permute-start(f32[17,32,128]{2,1,0:T(8,128)S(1)} %get-tuple-element.19), channel_id=1, source_target_pairs={{0,7},{1,2},{2,1},{3,4},{4,3},{5,6},{6,5},{7,0},{8,15},{9,10},{10,... | collective-permute-start | bytes 835592 | tf_op jit(solution)/shard_map/ppermute | solution.py:399

commit v11 on v10

--- a/solution.py
+++ b/solution.py
@@ -81,7 +81,7 @@
             )
         return carry
 
-    lax.fori_loop(0, rows // 8, turn, 0, unroll=4)
+    lax.fori_loop(0, rows // 8, turn, 0, unroll=16)
     ends = jnp.zeros((4 + HALO, snaps, LANES), jnp.float32)
     ext_ref[: 4 + HALO] = ends
     ext_ref[4 + HALO + rows :] = ends
@@ -96,7 +96,7 @@
         strip_ref[at] = packed
         return carry
 
-    lax.fori_loop(0, span, pack, 0, unroll=span // 2)
+    lax.fori_loop(0, span, pack, 0, unroll=span)
 
 
 def message_kernel(
@@ -216,7 +216,7 @@
         one_pass(lambda at: once_ref[at], weighted, store_twice)
         return carry
 
-    lax.fori_loop(0, snaps // TILE, one_tile, 0)
+    lax.fori_loop(0, snaps // TILE, one_tile, 0, unroll=True)
     outside = jnp.zeros((HALO, snaps, LANES), jnp.float32)
     twice_ref[:HALO] = outside
     twice_ref[HALO + rows :] = outside

time: 41.3 us -> 41.3 us (level)
  transfers between devices with their start and end apart: 4 -> 4, of which waited for: 1 -> 1; matrix products, arithmetic and copies ran while one was open for 0% -> 0% of each run, Pallas kernels for 24% -> 23%
where the time goes in v11:
time: 41.3 us; the launch traced here: 41.1 us
  Pallas kernels  16.5 us (40%)
  blocking collectives  10.5 us (25%)
  starting transfers between devices  8.27 us (20%)
  local copies, waits for them, and re-layouts  3.22 us (8%)
  waiting for transfers between devices  1.88 us (5%)
  between operations  0.74 us (2%)
    all_to_all x1, blocking collectives, gather_all(): lax.all_to_all(jnp.broadcast_to(values, (count,) + values.shape), axes, 0...  10.5 us
    ppermute x2, starting transfers between devices, pair_permutes(): lax.ppermute(values[1], axis, outer)  7.66 us
    pallas_call x1, Pallas kernels, shards(): pl.pallas_call(functools.partial(tile_kernel, span), in_specs=[whole(pltp...  7.63 us
    pallas_call x1, Pallas kernels, shards(): pl.pallas_call(functools.partial(basis_kernel, math.sqrt(total_cells)), g...  3.36 us
    pallas_call x1, Pallas kernels, shards(): pl.pallas_call(functools.partial(rim_kernel, span), in_specs=[whole()] *...  3.26 us
    unnamed x14, local copies, waits for them, and re-layouts  2.21 us
    pallas_call x1, Pallas kernels, shards(): pl.pallas_call(functools.partial(strip_kernel, span), in_specs=[whole()],...  1.94 us
    ppermute x2, waiting for transfers between devices, pair_permutes(): lax.ppermute(values[0], axis, inner)  1.87 us
  transfers between devices with their start and end apart: 4, of which 1 were waited for; matrix products, arithmetic and copies ran while one was open for 0% of the time, Pallas kernels for 23%

profile of v11, /device:TPU:0, one launch (start us, length us, event | category | flops | bytes accessed | tf_op | source)
XLA Modules:
  0.0 41.1 jit_solution(12750931340850222420)
XLA Ops:
  0.6 1.0 %constant_dynamic-slice_fusion = (f32[32,8,128]{2,1,0:T(8,128)S(1)}, f32[32,8,128]{2,1,0:T(8,128)S(1)}) fusion(f32[32,256,128]{2,1,0:T(8,128)} %field_ref.1, s32[]{:T(128)S(6)} %select_n.17, s32[]{:T(128)S(6)} %select_n.16), kind=kLoop, calls=%fused_computation | loop fusion | bytes 524296 | tf_op jit(solution)/shard_map/dynamic_slice | solution.py:428
  1.6 4.0 %collective-permute-start.1 = (f32[32,8,128]{2,1,0:T(8,128)S(1)}, f32[32,8,128]{2,1,0:T(8,128)S(1)}, u32[]{:S(2)}, u32[]{:S(2)}) collective-permute-start(f32[32,8,128]{2,1,0:T(8,128)S(1)} %get-tuple-element.22), channel_id=1, source_target_pairs={{0,24},{8,16},{16,8},{24,0},{1,25},{9,17},{17,9},{25,1},{2,26},{10... | collective-permute-start | bytes 393224 | tf_op jit(solution)/shard_map/ppermute | solution.py:399
  5.6 0.5 %collective-permute-start = (f32[32,8,128]{2,1,0:T(8,128)S(1)}, f32[32,8,128]{2,1,0:T(8,128)S(1)}, u32[]{:S(2)}, u32[]{:S(2)}) collective-permute-start(f32[32,8,128]{2,1,0:T(8,128)S(1)} %get-tuple-element.23), channel_id=1, source_target_pairs={{0,8},{8,0},{16,24},{24,16},{1,9},{9,1},{17,25},{25,17},{2,10},{10... | collective-permute-start | bytes 393224 | tf_op jit(solution)/shard_map/ppermute | solution.py:399
  6.1 0.0 copy-start
  6.1 2.2 %copy-done = f32[32,256,128]{2,1,0:T(8,128)S(1)} copy-done((f32[32,256,128]{2,1,0:T(8,128)S(1)}, f32[32,256,128]{2,1,0:T(8,128)}, u32[]{:S(2)}) %copy-start) | copy-done | bytes 4194328
  8.3 0.0 copy-start.3
  8.3 1.9 %turn_and_pack.1 = (f32[280,32,128]{2,1,0:T(8,128)S(1)}, f32[34,32,128]{2,1,0:T(8,128)S(1)}) custom-call(f32[32,256,128]{2,1,0:T(8,128)S(1)} %copy-done), custom_call_target="tpu_custom_call" | custom-call | tf_op jit(solution)/shard_map/turn_and_pack/pallas_call | solution.py:433
  10.3 0.0 collective-permute-done.1.high_ref
  10.3 1.9 %collective-permute-done.low_ref = f32[32,8,128]{2,1,0:T(8,128)S(1)} collective-permute-done((f32[32,8,128]{2,1,0:T(8,128)S(1)}, f32[32,8,128]{2,1,0:T(8,128)S(1)}, u32[]{:S(2)}, u32[]{:S(2)}) %collective-permute-start) | collective-permute-done | bytes 131104 | tf_op jit(solution)/shard_map/ppermute | solution.py:399
  12.2 0.3 lon_messages.1
  12.5 0.1 collective-permute-start.2
  12.5 3.7 %collective-permute-start.3 = (f32[17,32,128]{2,1,0:T(8,128)S(1)}, f32[17,32,128]{2,1,0:T(8,128)S(1)}, u32[]{:S(2)}, u32[]{:S(2)}) collective-permute-start(f32[17,32,128]{2,1,0:T(8,128)S(1)} %get-tuple-element.19), channel_id=1, source_target_pairs={{0,7},{1,2},{2,1},{3,4},{4,3},{5,6},{6,5},{7,0},{8,15},{9,10},{10,... | collective-permute-start | bytes 835592 | tf_op jit(solution)/shard_map/ppermute | solution.py:399
  16.2 0.0 copy-done.3
  16.2 0.0 copy-done.4
  16.3 0.0 copy-done.5
  16.3 0.0 copy-done.6
  16.3 7.6 %both_passes.1 = (f32[272,32,128]{2,1,0:T(8,128)S(1)}, f32[3,34,8,128]{3,2,1,0:T(8,128)S(1)}) custom-call(f32[1024]{0:T(1024)S(1)} %copy-done.4, f32[1024]{0:T(1024)S(1)} %copy-done.5, f32[1024]{0:T(1024)S(1)} %copy-done.6, f32[280,32,128]{2,1,0:T(8,128)S(1)} %get-tuple-element.14.ext_ref, bf16[256,256]{1,0:T(8,128)(2,1)S(1)} %copy-done.3), custom_call_target="tpu_custom_call" | custom-call | flops 104857600 | bytes 8388608 | tf_op jit(solution)/shard_map/both_passes/pallas_call | solution.py:454
  23.9 0.0 collective-permute-done.2.first_ref
  23.9 0.0 collective-permute-done.3.second_ref
  23.9 0.0 copy-done.1
  23.9 0.0 copy-done.2
  23.9 3.3 %rim_and_gram.1 = (bf16[272,64,128]{2,1,0:T(8,128)(2,1)S(1)}, f32[8,128]{1,0:T(8,128)S(1)}) custom-call(f32[272,32,128]{2,1,0:T(8,128)S(1)} %get-tuple-element.15.twice_ref, f32[34,32,128]{2,1,0:T(8,128)S(1)} %get-tuple-element.16.strip_ref, f32[3,34,8,128]{3,2,1,0:T(8,128)S(1)} %get-tuple-element.17.strip_rates_ref, ...), custom_call_target="tpu_custom_call" | custom-call | tf_op jit(solution)/shard_map/rim_and_gram/pallas_call | solution.py:469
  27.2 10.5 %all_to_all.5.gram_ref = f32[32,8,128]{2,1,0:T(8,128)S(1)} all-to-all(f32[32,8,128]{2,1,0:T(8,128)S(1)} %broadcast_in_dim.3), channel_id=1, replica_groups=mesh['lat'=4,'lon'=8] {'lat','lon'}, dimensions={0} | all-to-all | bytes 262144 | tf_op jit(solution)/shard_map/all_to_all | solution.py:405
  37.7 3.4 %factor_and_basis.1 = (bf16[32,256,128]{2,1,0:T(8,128)(2,1)}, f32[32,32]{1,0:T(8,128)}) custom-call(f32[32,8,128]{2,1,0:T(8,128)S(1)} %all_to_all.5.gram_ref, bf16[272,64,128]{2,1,0:T(8,128)(2,1)S(1)} %get-tuple-element.21.split_ref), custom_call_target="tpu_custom_call" | custom-call | tf_op jit(solution)/shard_map/factor_and_basis/pallas_call | solution.py:489
  (6 shorter events, 0.0 us)
Async XLA Ops:
  1.6 8.6 %collective-permute-start.1 = (f32[32,8,128]{2,1,0:T(8,128)S(1)}, f32[32,8,128]{2,1,0:T(8,128)S(1)}, u32[]{:S(2)}, u32[]{:S(2)}) collective-permute-start(f32[32,8,128]{2,1,0:T(8,128)S(1)} %get-tuple-element.22), channel_id=1, source_target_pairs={{0,24},{8,16},{16,8},{24,0},{1,25},{9,17},{17,9},{25,1},{2,26},{10... | collective-permute-start | bytes 393224 | tf_op jit(solution)/shard_map/ppermute | solution.py:399
  5.6 6.6 %collective-permute-start = (f32[32,8,128]{2,1,0:T(8,128)S(1)}, f32[32,8,128]{2,1,0:T(8,128)S(1)}, u32[]{:S(2)}, u32[]{:S(2)}) collective-permute-start(f32[32,8,128]{2,1,0:T(8,128)S(1)} %get-tuple-element.23), channel_id=1, source_target_pairs={{0,8},{8,0},{16,24},{24,16},{1,9},{9,1},{17,25},{25,17},{2,10},{10... | collective-permute-start | bytes 393224 | tf_op jit(solution)/shard_map/ppermute | solution.py:399
  6.1 2.2 %copy-start = (f32[32,256,128]{2,1,0:T(8,128)S(1)}, f32[32,256,128]{2,1,0:T(8,128)}, u32[]{:S(2)}) copy-start(f32[32,256,128]{2,1,0:T(8,128)} %field_ref.1) | copy-start | bytes 12582916
  8.3 7.9 %copy-start.3 = (bf16[256,256]{1,0:T(8,128)(2,1)S(1)}, bf16[256,256]{1,0:T(8,128)(2,1)}, u32[]{:S(2)}) copy-start(bf16[256,256]{1,0:T(8,128)(2,1)} %constant.34.clone.main_ref) | copy-start | bytes 393220
  8.3 7.9 %copy-start.4 = (f32[1024]{0:T(1024)S(1)}, f32[1024]{0:T(1024)}, u32[]{:S(2)}) copy-start(f32[1024]{0:T(1024)} %lon_ref.1) | copy-start | bytes 12292
  8.3 7.9 %copy-start.5 = (f32[1024]{0:T(1024)S(1)}, f32[1024]{0:T(1024)}, u32[]{:S(2)}) copy-start(f32[1024]{0:T(1024)} %lat_ref.1) | copy-start | bytes 12292
  8.3 7.9 %copy-start.6 = (f32[1024]{0:T(1024)S(1)}, f32[1024]{0:T(1024)}, u32[]{:S(2)}) copy-start(f32[1024]{0:T(1024)} %constant.33.clone.weight_ref) | copy-start | bytes 12292
  12.2 11.8 %copy-start.1 = (bf16[512,512]{1,0:T(8,128)(2,1)S(1)}, bf16[512,512]{1,0:T(8,128)(2,1)}, u32[]{:S(2)}) copy-start(bf16[512,512]{1,0:T(8,128)(2,1)} %constant.35.clone.edge_ref) | copy-start | bytes 1572868
  12.2 11.8 %copy-start.2 = (bf16[512,256]{1,0:T(8,128)(2,1)S(1)}, bf16[512,256]{1,0:T(8,128)(2,1)}, u32[]{:S(2)}) copy-start(bf16[512,256]{1,0:T(8,128)(2,1)} %constant.36.clone.again_ref) | copy-start | bytes 786436
  12.5 11.4 %collective-permute-start.2 = (f32[17,32,128]{2,1,0:T(8,128)S(1)}, f32[17,32,128]{2,1,0:T(8,128)S(1)}, u32[]{:S(2)}, u32[]{:S(2)}) collective-permute-start(f32[17,32,128]{2,1,0:T(8,128)S(1)} %get-tuple-element.18), channel_id=1, source_target_pairs={{0,1},{1,0},{2,3},{3,2},{4,5},{5,4},{6,7},{7,6},{8,9},{9,8},{10,11... | collective-permute-start | bytes 835592 | tf_op jit(solution)/shard_map/ppermute | solution.py:399
  12.5 11.4 %collective-permute-start.3 = (f32[17,32,128]{2,1,0:T(8,128)S(1)}, f32[17,32,128]{2,1,0:T(8,128)S(1)}, u32[]{:S(2)}, u32[]{:S(2)}) collective-permute-start(f32[17,32,128]{2,1,0:T(8,128)S(1)} %get-tuple-element.19), channel_id=1, source_target_pairs={{0,7},{1,2},{2,1},{3,4},{4,3},{5,6},{6,5},{7,0},{8,15},{9,10},{10,... | collective-permute-start | bytes 835592 | tf_op jit(solution)/shard_map/ppermute | solution.py:399
